TPU v7x, 32 devices: a whole 2x2x4 slice. The times are simulated.
32 devices in a mesh: rep: 4 (over y, x), shard: 8 (over z, core).
Axes of the slice: x: 2, y: 2, z: 4, core: 2. Of those that a mesh axis runs over, the one named last changes fastest.
Arguments:
- tokens: bfloat16 [4096, 768], P(('rep', 'shard')), may hold values from -6 to 6
- out_grad: bfloat16 [4096, 768], P(('rep', 'shard')), may hold values from -6 to 6
- lengths: int32 [32, 4], P(('rep', 'shard')), may hold values from 0 to 128, as said below
- gains: bfloat16 [2, 768], P(None, 'shard'), may hold values from 0.5 to 1.5
- shifts: bfloat16 [6, 768], P(None, 'shard'), may hold values from -3 to 3
- w_qkv: bfloat16 [768, 2304], P('shard'), may hold values from -0.21875 to 0.21875
- w_proj: bfloat16 [768, 768], P('shard'), may hold values from -0.875 to 0.875
- w_fc: bfloat16 [768, 3072], P('shard'), may hold values from -0.21875 to 0.21875
- bias_fc: bfloat16 [3072], P('shard'), may hold values from -3 to 3
- w_fc2: bfloat16 [3072, 768], P('shard'), may hold values from -0.109375 to 0.109375
Outputs:
- mixed_out: bfloat16 [4096, 768], P(('rep', 'shard'))
- grad_tokens: float32 [4096, 768], P(('rep', 'shard'))
- grad_gains: float32 [2, 768], P(None, 'shard')
- grad_shifts: float32 [6, 768], P(None, 'shard')
- grad_w_qkv: float32 [768, 2304], P('shard')
- grad_w_proj: float32 [768, 768], P('shard')
- grad_w_fc: float32 [768, 3072], P('shard')
- grad_bias_fc: float32 [3072], P('shard')
- grad_w_fc2: float32 [3072, 768], P('shard')
Inputs may be any that keep to these rules, and one draw needn't show every extreme that they name: `lengths`: row d lists, in slot order from slot 0, the sequences on device d = 8 * rep + shard; zeros stand only after the last sequence; the first entry is 1 or more; a row sums to at most 128; some row holds a single sequence of 128.
All inputs are finite; a program needn't handle non-finite values.
Results may differ from a plain program's by a relative error of at most 0.014.
Values may be sent and summed in bfloat16 or wider, within the bound.
No kernel may reach another device: no remote copies, remote signals or barrier semaphores. Data moves between devices by JAX's collectives and lax.ppermute only.
A program may use at most 128 MiB of HBM per device.

v0:
```python
from functools import partial

import jax
import jax.numpy as jnp
from jax import lax
from jax.experimental import pallas as pl
from jax.experimental.pallas import tpu as pltpu
from jax.sharding import PartitionSpec as P

HEAD_DIM = 64
EPS = 1e-05
LOW = jnp.bfloat16
F32 = jnp.float32


def normalize(values, gain_row, shift_row):
    row_mean = jnp.mean(values, axis=-1, keepdims=True)
    centered = values - row_mean
    variance = jnp.mean(centered * centered, axis=-1, keepdims=True)
    return centered * lax.rsqrt(variance + EPS) * gain_row + shift_row


def contract(left_rows, right_rows):
    return lax.dot_general(
        left_rows, right_rows, (((0,), (0,)), ((), ())), preferred_element_type=F32
    )


def back_mult(grad_rows, weight):
    return lax.dot_general(
        grad_rows, weight, (((1,), (1,)), ((), ())), preferred_element_type=F32
    )


def mult(left, right):
    return jnp.dot(left, right, preferred_element_type=F32)


class Links:
    def __init__(self):
        self.shards = lax.axis_size("shard")
        self.line = self.shards // 2
        place = lax.axis_index("shard")
        self.z = place // 2
        self.c = place % 2
        self.j = lax.axis_index("rep")
        self.scalars = jnp.stack([self.z, self.c, self.j]).astype(jnp.int32)
        assert lax.axis_size("rep") == 4

    def core(self, v):
        return lax.ppermute(v, "shard", [(i, i ^ 1) for i in range(self.shards)])

    def along(self, v, hop):
        n = self.shards
        return lax.ppermute(v, "shard", [(i, (i + 2 * hop) % n) for i in range(n)])

    def rep(self, v, k):
        return lax.ppermute(v, "rep", [(i, i ^ k) for i in range(4)])

    def rep_gather(self, v):
        return [v] + [self.rep(v, k) for k in range(1, 4)]


def pick(stack, index, axis=0):
    return lax.dynamic_index_in_dim(stack, index, axis, keepdims=False)


def run(kernel, out_shapes, scalars, args, scratch=()):
    return pl.pallas_call(
        kernel,
        out_shape=[jax.ShapeDtypeStruct(shape, dtype) for shape, dtype in out_shapes],
        in_specs=[pl.BlockSpec(memory_space=pltpu.SMEM)]
        + [pl.BlockSpec(memory_space=pltpu.VMEM)] * len(args),
        out_specs=[pl.BlockSpec(memory_space=pltpu.VMEM)] * len(out_shapes),
        scratch_shapes=list(scratch),
        compiler_params=pltpu.CompilerParams(vmem_limit_bytes=56 * 1024 * 1024),
        cost_estimate=pl.CostEstimate(flops=1, bytes_accessed=1, transcendentals=0),
    )(scalars, *args)


def tie(value, *others):
    return lax.optimization_barrier((value, others))[0]


def line_gather(links, block):
    return [block] + [links.along(block, hop) for hop in range(1, links.line)]


def with_partners(links, mine):
    return mine + [links.core(v) for v in mine]


def assemble(scalar_ref, refs, out, start, rows):
    line = len(refs) // 2
    z, c = scalar_ref[0], scalar_ref[1]
    for hop in range(line):
        at = lax.rem(z + line - hop, line)
        for side in range(2):
            to = (2 * at + c) if side == 0 else (2 * at + 1 - c)
            block = refs[side * line + hop][pl.ds(start, rows), :]
            if rows % 16 == 0:
                out[pl.ds(pl.multiple_of(to * rows, 16), rows), :] = block
                continue
            for s in range(2 * line):

                @pl.when(to == s)
                def _(block=block, s=s):
                    out[s * rows : (s + 1) * rows, :] = block


def one_of_pair(scratch, z, side, rows):
    if rows % 16 == 0:
        return scratch[pl.ds(pl.multiple_of((2 * z + side) * rows, 16), rows), :].astype(LOW)
    first, second = (scratch[(2 * z + k) * rows : (2 * z + k + 1) * rows, :] for k in range(2))
    return jnp.where(side == 0, first, second).astype(LOW)


def line_sum(links, mine, theirs):
    line = links.line
    theirs = theirs.astype(F32)
    sent = []
    for hop in range(1, line):
        at = (links.z + hop) % line
        sent.append((pick(mine, at).astype(F32) + pick(theirs, at)).astype(LOW))
    own = pick(mine, links.z).astype(F32) + pick(theirs, links.z)
    return sent, own


def line_send(links, sent, own):
    for hop, value in enumerate(sent, start=1):
        own = own + links.along(value, hop).astype(F32)
    return own


def pad_rows(v, rows):
    return v if v.shape[0] == rows else jnp.pad(v, ((0, rows - v.shape[0]), (0, 0)))


def unit(values):
    row_mean = jnp.mean(values, axis=-1, keepdims=True)
    centered = values - row_mean
    variance = jnp.mean(centered * centered, axis=-1, keepdims=True)
    scale = lax.rsqrt(variance + EPS)
    return centered * scale, scale


def norm_back(cotangent, gain, unit_rows, scale):
    weighted = cotangent * gain
    return scale * (
        weighted
        - jnp.mean(weighted, axis=-1, keepdims=True)
        - unit_rows * jnp.mean(weighted * unit_rows, axis=-1, keepdims=True)
    )


def gelu_pair(x):
    root = 0.7978845608028654
    square = x * x
    bend = jnp.tanh(root * x * (1.0 + 0.044715 * square))
    half = 0.5 * (1.0 + bend)
    slope = half + 0.5 * x * (1.0 - bend * bend) * root * (1.0 + 3 * 0.044715 * square)
    return x * half, slope


def choose(index, options):
    value = options[0]
    for k in range(1, len(options)):
        value = jnp.where(index == k, options[k], value)
    return value


def live_rows(got, slots, count):
    total = jnp.zeros((1, 1), F32)
    for s in range(count):
        total = total + got[2 * slots : 2 * slots + 1, s : s + 1].astype(F32)
    place = lax.broadcasted_iota(jnp.int32, (slots, 1), 0).astype(F32)
    return (place < total).astype(F32)


def pack_attn(links, place, args, slots, rows, part, full):
    tokens, out_grad, lengths, gains, shifts, bias, w_qkv, w_proj = args
    model = tokens.shape[1]
    count = lengths.shape[1]

    def kernel(scalar_ref, tok, cot, len_ref, gain, shift, bias_ref, qkv_ref, p_ref, out, sent):
        j, s_here = scalar_ref[2], scalar_ref[3]
        for t in range(3):
            out[pl.ds(0, rows), t * part : (t + 1) * part] = choose(
                j,
                [
                    qkv_ref[:, t * model + p * part : t * model + (p + 1) * part]
                    for p in range(4)
                ],
            )
        out[pl.ds(0, rows), 3 * part :] = choose(
            j, [p_ref[:, p * part : (p + 1) * part] for p in range(4)]
        )
        mine = choose(j, [bias_ref[:, p * rows : (p + 1) * rows] for p in range(4)])
        small = jnp.concatenate(
            [v.astype(F32) for v in (gain[...], shift[...], mine)] + [jnp.zeros((7, rows), F32)]
        )
        small = jnp.concatenate([small] * links.shards, axis=1)
        lane = lax.broadcasted_iota(jnp.int32, small.shape, 1)
        here = (lane >= s_here * rows) & (lane < (s_here + 1) * rows)
        out[pl.ds(full, 16), :] = jnp.where(here, small, 0.0).astype(LOW)
        sent[pl.ds(0, slots), :] = tok[...]
        sent[pl.ds(slots, slots), :] = cot[...]
        sent[pl.ds(2 * slots, 16), :] = jnp.zeros((16, model), LOW)
        sent[2 * slots : 2 * slots + 1, :count] = len_ref[...].astype(F32).astype(LOW)

    scalars = jnp.concatenate([links.scalars, place[None].astype(jnp.int32)])
    shapes = [((full + 16, model), LOW), ((2 * slots + 16, model), LOW)]
    return run(kernel, shapes, scalars, args)


def pack_ff(links, w_fc, w_fc2, rows, full):
    model = w_fc2.shape[1]

    def kernel(scalar_ref, fc_ref, fc2_ref, out):
        j = scalar_ref[2]
        for s in range(links.shards):
            out[pl.ds(0, rows), s * rows : (s + 1) * rows] = choose(
                j,
                [fc_ref[:, (4 * s + p) * rows : (4 * s + p + 1) * rows] for p in range(4)],
            )
        out[pl.ds(full, rows), :] = choose(
            j, [fc2_ref[p * rows : (p + 1) * rows, :] for p in range(4)]
        )

    return run(kernel, [((full + rows, model), LOW)], links.scalars, [w_fc, w_fc2])[0]


def proj_lanes(links, blocks, rows, part):
    model = blocks[0].shape[1]
    line = links.line

    def kernel(scalar_ref, *refs):
        ins, out, scratch = refs[:-2], refs[-2], refs[-1]
        assemble(scalar_ref, [ref.at[:, pl.ds(512, 256)] for ref in ins], scratch, 0, rows)
        for g in range(4):
            out[:, g * part : (g + 1) * part] = scratch[pl.ds(g * part, part), 64:]

    return run(
        kernel, [((part, model), LOW)], links.scalars, blocks, [pltpu.VMEM((model, 256), LOW)]
    )[0]


def attn_forward(links, got, blocks, slots, heads, count, rows):
    model = blocks[0].shape[1]
    part = heads * HEAD_DIM
    full = -(-rows // 16) * 16

    def kernel(scalar_ref, *refs):
        ins, parts = refs[:4], refs[4 : 4 + len(blocks)]
        w_ref, unit_out, qkv_out, probs_out, sent_out, small_out = refs[4 + len(blocks) :]
        j = scalar_ref[2]
        assemble(scalar_ref, parts, w_ref, 0, rows)
        small_sum = jnp.zeros(small_out.shape, F32)
        for ref in parts:
            small_sum = small_sum + ref[pl.ds(full, 16), :].astype(F32)
        small_out[...] = small_sum
        cut = lambda row: choose(
            j, [small_sum[row : row + 1, p * part : (p + 1) * part] for p in range(4)]
        )
        q_bias, v_bias = cut(4), cut(5)
        rows_at = lax.broadcasted_iota(jnp.int32, (slots, slots), 0).astype(F32)
        cols_at = lax.broadcasted_iota(jnp.int32, (slots, slots), 1).astype(F32)
        for k in range(4):
            normed = unit(ins[k][:slots].astype(F32))[0] * small_sum[0:1] + small_sum[2:3]
            normed = normed.astype(LOW)
            unit_out[k] = normed
            qkv = mult(normed, w_ref[:, : 3 * part])
            qkv_out[k, :, :part] = (qkv[:, :part] + q_bias).astype(LOW)
            qkv_out[k, :, part : 2 * part] = qkv[:, part : 2 * part].astype(LOW)
            qkv_out[k, :, 2 * part :] = (qkv[:, 2 * part :] + v_bias).astype(LOW)
            end = jnp.zeros((1, 1), F32)
            row_seq, col_seq = jnp.zeros((slots, slots), F32), jnp.zeros((slots, slots), F32)
            for s in range(count):
                end = end + ins[k][2 * slots : 2 * slots + 1, s : s + 1].astype(F32)
                row_seq = row_seq + (end <= rows_at).astype(F32)
                col_seq = col_seq + (end <= cols_at).astype(F32)
            allowed = (row_seq == col_seq) & (cols_at <= rows_at)
            for h in range(heads):
                at = h * HEAD_DIM
                query = qkv_out[k, :, at : at + HEAD_DIM]
                keys = qkv_out[k, :, part + at : part + at + HEAD_DIM]
                values = qkv_out[k, :, 2 * part + at : 2 * part + at + HEAD_DIM]
                scores = back_mult(query, keys) * (HEAD_DIM**-0.5)
                scores = jnp.where(allowed, scores, -1000000000.0)
                exponent = jnp.exp(scores - jnp.max(scores, axis=-1, keepdims=True))
                probs = exponent / jnp.sum(exponent, axis=-1, keepdims=True)
                probs_out[k, h] = probs
                attended = mult(probs.astype(LOW), values)
                sent_out[:, k * part + at : k * part + at + HEAD_DIM] = attended.astype(LOW)

    shapes = [
        ((model, model), LOW),
        ((4, slots, model), LOW),
        ((4, slots, 3 * part), LOW),
        ((4, heads, slots, slots), F32),
        ((slots, 4 * part), LOW),
        ((16, model), F32),
    ]
    return run(kernel, shapes, links.scalars, [*got, *blocks])


def ff_both(links, got, attended, proj, blocks, small, slots, count, rows):
    model = blocks[0].shape[1]
    part = model // 4
    full = -(-rows // 16) * 16
    held = 4 + 1 + 4 + len(blocks) + 1

    def kernel(scalar_ref, *refs):
        ins, att, p_parts, parts, small_ref = (
            refs[:4],
            refs[4],
            refs[5:9],
            refs[9 : held - 1],
            refs[held - 1],
        )
        att_out, middle_out, normed_out, active_out, hidden_out, cot_out = refs[held : held + 6]
        own_out, *sent_out = refs[held + 6 : held + 10]
        sums_out, p_ref, fc2_ref, fc_ref = refs[held + 10 :]
        j = scalar_ref[2]
        assemble(scalar_ref, parts, fc_ref, 0, rows)
        assemble(scalar_ref, parts, fc2_ref, full, rows)
        for p in range(4):
            for g in range(4):
                p_ref[pl.ds(g * part, part), p * part : (p + 1) * part] = choose(
                    j ^ p, [ref[:, g * part : (g + 1) * part] for ref in p_parts]
                )
        total = jnp.zeros((1, model), F32)
        for k in range(4):
            for p in range(4):
                att_out[k, :, p * part : (p + 1) * part] = choose(
                    j ^ p, [att[p, :, (k ^ m) * part : ((k ^ m) + 1) * part] for m in range(4)]
                )
            middle = ins[k][:slots].astype(F32) + mult(att_out[k], p_ref[...]) + small_ref[6:7]
            if k == 0:
                middle_out[...] = middle
            normed = (unit(middle)[0] * small_ref[1:2] + small_ref[3:4]).astype(LOW)
            normed_out[k] = normed
            hidden = mult(normed, fc_ref[...]) + small_ref[8:9]
            active, slope = gelu_pair(hidden)
            active_out[k] = active.astype(LOW)
            live = live_rows(ins[k], slots, count)
            cot = (ins[k][slots : 2 * slots].astype(F32) * live).astype(LOW)
            cot_out[k] = cot
            grad_hidden = (back_mult(cot, fc2_ref[...]) * slope).astype(LOW)
            hidden_out[k] = grad_hidden
            total = total + jnp.sum(grad_hidden.astype(F32), axis=0, keepdims=True)
            grad_normed = back_mult(grad_hidden, fc_ref[...])
            if k == 0:
                own_out[...] = grad_normed
            else:
                sent_out[k - 1][...] = grad_normed.astype(LOW)
        sums_out[...] = total

    shapes = [
        ((4, slots, model), LOW),
        ((slots, model), F32),
        ((4, slots, model), LOW),
        ((4, slots, model), LOW),
        ((4, slots, model), LOW),
        ((4, slots, model), LOW),
        ((slots, model), F32),
        *[((slots, model), LOW)] * 3,
        ((1, model), F32),
        ((model, model), LOW),
        ((model, model), LOW),
    ]
    args = [*got, attended, *proj, *blocks, small]
    return run(kernel, shapes, links.scalars, args, [pltpu.VMEM((model, model), LOW)])


def ff_grads(links, normed, active, hidden, cot, fc2, rows):
    reps, slots, model = normed.shape
    line = links.line
    full = -(-rows // 16) * 16

    def kernel(scalar_ref, *refs):
        normed_ref, active_ref, hidden_ref, cot_ref, fc2_ref = refs[:5]
        mine_out, other_out, branch_own, *branch_sent, scratch = refs[5:]
        c = scalar_ref[1]
        for start, left, right in ((0, normed_ref, hidden_ref), (full, active_ref, cot_ref)):
            total = contract(left[0], right[0])
            for k in range(1, reps):
                total = total + contract(left[k], right[k])
            scratch[...] = total
            for z in range(line):
                for side, out in ((c, mine_out), (1 - c, other_out)):
                    out[z, pl.ds(start, rows), :] = one_of_pair(scratch, z, side, rows)
        for k in range(reps):
            branch = mult(active_ref[k], fc2_ref[...])
            if k == 0:
                branch_own[...] = branch
            else:
                branch_sent[k - 1][...] = branch.astype(LOW)

    shapes = [
        ((line, full + rows, model), LOW),
        ((line, full + rows, model), LOW),
        ((slots, model), F32),
        *[((slots, model), LOW)] * 3,
    ]
    args = [normed, active, hidden, cot, fc2]
    return run(kernel, shapes, links.scalars, args, [pltpu.VMEM((model, model), F32)])


def middle_back(links, own, received, middle, got, small, slots, count):
    def kernel(scalar_ref, own_ref, r1, r2, r3, middle_ref, got_ref, small_ref, *outs):
        grad_out, branch_out, sums_out = outs
        cotangent = own_ref[...] + r1[...].astype(F32) + r2[...].astype(F32) + r3[...].astype(F32)
        unit_rows, scale = unit(middle_ref[...])
        live = live_rows(got_ref, slots, count)
        cot = got_ref[slots : 2 * slots].astype(F32) * live
        grad = cot + norm_back(cotangent, small_ref[1:2], unit_rows, scale)
        grad_out[...] = grad
        branch = grad.astype(LOW)
        branch_out[...] = branch
        sums_out[0:1] = jnp.sum(cotangent * unit_rows, axis=0, keepdims=True)
        sums_out[1:2] = jnp.sum(cotangent, axis=0, keepdims=True)
        sums_out[2:3] = jnp.sum(branch.astype(F32), axis=0, keepdims=True)
        sums_out[3:4] = jnp.sum(cot, axis=0, keepdims=True)

    model = own.shape[1]
    shapes = [((slots, model), F32), ((slots, model), LOW), ((4, model), F32)]
    return run(kernel, shapes, links.scalars, [own, *received, middle, got, small])


def attn_back(links, grads, got, proj, weights, normed, qkv, probs, attended, sums, bias, rows):
    reps, slots, model = normed.shape
    heads = probs.shape[1]
    part = heads * HEAD_DIM
    line = links.line
    full = -(-rows // 16) * 16
    scale = HEAD_DIM**-0.5

    def kernel(scalar_ref, *refs):
        grad_ref, ins = refs[0], refs[1:5]
        p_ref, w_ref, normed_ref, qkv_ref, probs_ref, att_ref, sums_ref, bias_ref = refs[5:13]
        mine_out, other_out, own_out, *sent_out, scratch, grad_qkv = refs[13:]
        c, j = scalar_ref[1], scalar_ref[2]
        proj_rows = p_ref[pl.ds(pl.multiple_of(j * part, part), part), :]
        gain_sum, shift_sum = jnp.zeros((1, model), F32), jnp.zeros((1, model), F32)
        qkv_sum = jnp.zeros((1, 3 * part), F32)
        for k in range(reps):
            grad_att = back_mult(grad_ref[j ^ k], proj_rows).astype(LOW)
            for h in range(heads):
                at = h * HEAD_DIM
                query = qkv_ref[k, :, at : at + HEAD_DIM]
                keys = qkv_ref[k, :, part + at : part + at + HEAD_DIM]
                values = qkv_ref[k, :, 2 * part + at : 2 * part + at + HEAD_DIM]
                prob = probs_ref[k, h]
                cot = grad_att[:, at : at + HEAD_DIM]
                grad_probs = back_mult(cot, values)
                inner = jnp.sum(prob * grad_probs, axis=-1, keepdims=True)
                grad_scores = (prob * (grad_probs - inner)).astype(LOW)
                grad_qkv[k, :, at : at + HEAD_DIM] = (mult(grad_scores, keys) * scale).astype(LOW)
                grad_qkv[k, :, part + at : part + at + HEAD_DIM] = (
                    contract(grad_scores, query) * scale
                ).astype(LOW)
                grad_qkv[k, :, 2 * part + at : 2 * part + at + HEAD_DIM] = contract(
                    prob.astype(LOW), cot
                ).astype(LOW)
            grad_rows = grad_qkv[k]
            qkv_sum = qkv_sum + jnp.sum(grad_rows.astype(F32), axis=0, keepdims=True)
            grad_normed = back_mult(grad_rows, w_ref[:, : 3 * part])
            if k == 0:
                own_out[...] = grad_normed
            else:
                sent_out[k - 1][...] = grad_normed.astype(LOW)
            unit_rows = unit(ins[k][:slots].astype(F32))[0]
            gain_sum = gain_sum + jnp.sum(grad_normed * unit_rows, axis=0, keepdims=True)
            shift_sum = shift_sum + jnp.sum(grad_normed, axis=0, keepdims=True)
        total_qkv = contract(normed_ref[0], grad_qkv[0])
        for k in range(1, reps):
            total_qkv = total_qkv + contract(normed_ref[k], grad_qkv[k])
        scratch[:, : 3 * part] = total_qkv
        for k in range(reps):
            cols = choose(j, [grad_ref[j ^ k, :, p * part : (p + 1) * part] for p in range(4)])
            product = contract(att_ref[k], cols)
            total_proj = product if k == 0 else total_proj + product
        scratch[:, 3 * part :] = total_proj
        spread = lambda v: jnp.concatenate(
            [jnp.where(j == p, v, jnp.zeros_like(v)) for p in range(4)], axis=1
        )
        vectors = jnp.concatenate(
            [
                gain_sum,
                sums_ref[0:1],
                shift_sum,
                sums_ref[1:2],
                spread(qkv_sum[:, :part]),
                spread(qkv_sum[:, 2 * part :]),
                sums_ref[2:4],
                bias_ref[...],
                jnp.zeros((7, model), F32),
            ]
        ).astype(LOW)
        for z in range(line):
            for side, out in ((c, mine_out), (1 - c, other_out)):
                out[z, pl.ds(0, rows), :] = one_of_pair(scratch, z, side, rows)
                out[z, pl.ds(full, 16), :] = vectors

    shapes = [
        ((line, full + 16, model), LOW),
        ((line, full + 16, model), LOW),
        ((slots, model), F32),
        *[((slots, model), LOW)] * 3,
    ]
    args = [grads, *got, proj, weights, normed, qkv, probs, attended, sums, bias]
    scratch = [pltpu.VMEM((model, model), F32), pltpu.VMEM((reps, slots, 3 * part), LOW)]
    return run(kernel, shapes, links.scalars, args, scratch)


def ff_results(links, parts, rows):
    model = parts[0].shape[1]
    shards = links.shards
    full = -(-rows // 16) * 16

    def kernel(scalar_ref, *refs):
        ins, fc_out, fc2_out = refs[:4], refs[4], refs[5]
        j = scalar_ref[2]
        for p in range(4):
            left = choose(j ^ p, [ref[pl.ds(0, rows), :].astype(F32) for ref in ins])
            for s in range(shards):
                at = (s * 4 + p) * rows
                fc_out[:, at : at + rows] = left[:, s * rows : (s + 1) * rows]
            fc2_out[pl.ds(p * rows, rows), :] = choose(
                j ^ p, [ref[pl.ds(full, rows), :].astype(F32) for ref in ins]
            )

    shapes = [((rows, 4 * model), F32), ((4 * rows, model), F32)]
    return run(kernel, shapes, links.scalars, parts)


def attn_results(links, place, parts, rows):
    model = parts[0].shape[1]
    shards = links.shards
    part = model // 4
    full = -(-rows // 16) * 16

    def kernel(scalar_ref, *refs):
        ins, qkv_out, proj_out, gains_out, shifts_out, bias_out = refs[:4], *refs[4:]
        j, s_here = scalar_ref[2], scalar_ref[3]
        for p in range(4):
            block = choose(j ^ p, [ref[pl.ds(0, rows), :].astype(F32) for ref in ins])
            for t in range(3):
                at = t * model + p * part
                qkv_out[:, at : at + part] = block[:, t * part : (t + 1) * part]
            proj_out[:, p * part : (p + 1) * part] = block[:, 3 * part :]
        cut = lambda v: choose(s_here, [v[:, s * rows : (s + 1) * rows] for s in range(shards)])
        low = [cut(ref[pl.ds(full, 16), :].astype(F32)) for ref in ins]
        sums = low[0] + low[1] + low[2] + low[3]
        gains_out[...] = sums[:2]
        shifts_out[...] = sums[2:8]
        for p in range(4):
            bias_out[:, p * rows : (p + 1) * rows] = choose(j ^ p, [v[8:9] for v in low])

    shapes = [
        ((rows, 3 * model), F32),
        ((rows, model), F32),
        ((2, rows), F32),
        ((6, rows), F32),
        ((1, 4 * rows), F32),
    ]
    scalars = jnp.concatenate([links.scalars, place[None].astype(jnp.int32)])
    return run(kernel, shapes, scalars, parts)


def local(tokens, out_grad, lengths, gains, shifts, w_qkv, w_proj, w_fc, bias_fc, w_fc2):
    links = Links()
    line, shards = links.line, links.shards
    z, c, j = links.z, links.c, links.j
    place = lax.axis_index("shard")
    slots, model = tokens.shape
    count = lengths.shape[1]
    rows = w_proj.shape[0]
    quarter = w_fc2.shape[0] // 4
    assert quarter == rows and w_fc.shape[1] == 4 * model
    heads = model // HEAD_DIM // 4
    part = heads * HEAD_DIM
    full_rows = -(-rows // 16) * 16

    args = [tokens, out_grad, lengths, gains, shifts, bias_fc.reshape(1, -1), w_qkv, w_proj]
    attn_block, sent = pack_attn(links, place, args, slots, rows, part, full_rows)
    w_fc, w_fc2 = tie((w_fc, w_fc2), attn_block)
    ff_block = pack_ff(links, w_fc, w_fc2, rows, full_rows)

    attn_mine = line_gather(links, attn_block)
    got = links.rep_gather(sent)
    attn_mine, got, ff_block = lax.optimization_barrier((attn_mine, got, ff_block))
    attn_blocks = with_partners(links, attn_mine)
    ff_mine = line_gather(links, ff_block)

    proj = proj_lanes(links, attn_blocks, rows, part)
    proj = links.rep_gather(proj)
    weights, normed_one, qkv, probs, sent, small_f = attn_forward(
        links, got, attn_blocks, slots, heads, count, rows
    )
    ff_blocks = with_partners(links, tie(ff_mine, sent))
    attended = lax.all_gather(sent, "rep", axis=0)
    (
        attended,
        middle,
        normed_two,
        active,
        grad_hidden,
        cot,
        own,
        sent_x,
        sent_y,
        sent_d,
        bias_sums,
        proj,
        fc2,
    ) = ff_both(links, got, attended, proj, ff_blocks, small_f, slots, count, rows)
    received = [links.rep(v, k) for k, v in ((1, sent_x), (2, sent_y), (3, sent_d))]
    ff_mine, ff_other, branch, *branch_sent = ff_grads(
        links, normed_two, active, grad_hidden, cot, fc2, rows
    )
    ff_theirs = links.core(tie(ff_other, received))
    grad_middle, grad_branch, sums = middle_back(
        links, own, received, middle, got[0], small_f, slots, count
    )
    ff_sent, ff_own = line_sum(links, ff_mine, ff_theirs)
    grad_branch = lax.all_gather(grad_branch, "rep", axis=0)
    ff_sum = line_send(links, ff_sent, ff_own)
    branch_sent = tie(branch_sent, grad_branch)

    attn_mine, attn_other, own, *sent = attn_back(
        links,
        grad_branch,
        got,
        proj,
        weights,
        normed_one,
        qkv,
        probs,
        attended,
        sums,
        bias_sums,
        rows,
    )
    attn_theirs = links.core(tie(attn_other, ff_sum))
    attn_sent, attn_own = line_sum(links, attn_mine, attn_theirs)
    attn_sum = line_send(links, attn_sent, attn_own)

    for k in range(1, 4):
        branch = branch + links.rep(branch_sent[k - 1], k).astype(F32)
        own = own + links.rep(sent[k - 1], k).astype(F32)
    live = (jnp.arange(slots) < jnp.sum(lengths)).astype(F32)[:, None]
    mixed_out = ((middle + branch + small_f[7]) * live).astype(LOW)
    unit_rows, scale = unit(tokens.astype(F32))
    grad_tokens = grad_middle + norm_back(own, small_f[0], unit_rows, scale)

    fc_out, fc2_out = ff_results(links, links.rep_gather(ff_sum.astype(LOW)), rows)
    qkv_out, proj_out, gains_out, shifts_out, bias_out = attn_results(
        links, place, links.rep_gather(attn_sum.astype(LOW)), rows
    )
    return (
        mixed_out,
        grad_tokens,
        gains_out,
        shifts_out,
        qkv_out,
        proj_out,
        fc_out,
        bias_out.reshape(-1),
        fc2_out,
    )


def solution(mesh):
    return jax.shard_map(
        local,
        mesh=mesh,
        in_specs=(
            P(("rep", "shard"), None),
            P(("rep", "shard"), None),
            P(("rep", "shard"), None),
            P(None, "shard"),
            P(None, "shard"),
            P("shard", None),
            P("shard", None),
            P("shard", None),
            P("shard"),
            P("shard", None),
        ),
        out_specs=(
            P(("rep", "shard"), None),
            P(("rep", "shard"), None),
            P(None, "shard"),
            P(None, "shard"),
            P("shard", None),
            P("shard", None),
            P("shard", None),
            P("shard"),
            P("shard", None),
        ),
        check_vma=False,
    )
```

profile of v0, /device:TPU:0, one launch (start us, length us, event | category | flops | bytes accessed | tf_op | source)
XLA Modules:
  0.0 182.6 jit_solution(8103642012241266107)
XLA Ops:
  2.6 2.5 %shard_map.169 = (bf16[112,768]{1,0:T(8,128)(2,1)}, bf16[272,768]{1,0:T(8,128)(2,1)}) custom-call(s32[4]{0:T(128)} %pad_add_fusion.1.scalar_ref, bf16[128,768]{1,0:T(8,128)(2,1)} %tok.1, bf16[128,768]{1,0:T(8,128)(2,1)} %cot.1, s32[1,4]{1,0:T(1,128)} %len_ref.1, bf16[2,96]{1,0:T(2,128)(2,1)} %gain.1, bf16[6,96]{1,0:T(8,128)(2,1)} %shift.1, ...), custom_call_target="tpu_custom_call" | custom-call | flops 1 | bytes 1 | tf_op jit(solution)/shard_map/pallas_call | solution.py:69
  5.0 2.9 %collective-permute-start.3 = (bf16[272,768]{1,0:T(8,128)(2,1)}, bf16[272,768]{1,0:T(8,128)(2,1)S(1)}, u32[]{:S(2)}, u32[]{:S(2)}) collective-permute-start(bf16[272,768]{1,0:T(8,128)(2,1)} %get-tuple-element.76.refs_0_.got_ref.refs_1_), channel_id=1, source_target_pairs={{0,8},{8,0},{16,24},{24,16},{1,9},{9,1},{17,25},{25,17},{2,10},{10... | collective-permute-start | bytes 1253384 | tf_op jit(solution)/shard_map/ppermute | solution.py:58
  11.5 2.6 %collective-permute-start.1 = (bf16[112,768]{1,0:T(8,128)(2,1)}, bf16[112,768]{1,0:T(8,128)(2,1)S(1)}, u32[]{:S(2)}, u32[]{:S(2)}) collective-permute-start(bf16[112,768]{1,0:T(8,128)(2,1)} %get-tuple-element.80.refs_4_.refs_0_), channel_id=1, source_target_pairs={{0,4},{1,5},{2,6},{3,7},{4,0},{5,1},{6,2},{7,3},{8,12},{9,13},{10,... | collective-permute-start | bytes 516104 | tf_op jit(solution)/shard_map/ppermute | solution.py:55
  14.1 5.0 %collective-permute-done.refs_5_.refs_1_ = bf16[112,768]{1,0:T(8,128)(2,1)S(1)} collective-permute-done((bf16[112,768]{1,0:T(8,128)(2,1)}, bf16[112,768]{1,0:T(8,128)(2,1)S(1)}, u32[]{:S(2)}, u32[]{:S(2)}) %collective-permute-start) | collective-permute-done | bytes 172064 | tf_op jit(solution)/shard_map/ppermute | solution.py:55
  20.5 2.8 %shard_map.170.refs_9_ = bf16[192,768]{1,0:T(8,128)(2,1)} custom-call(s32[3]{0:T(128)} %pad_add_fusion.scalar_ref, bf16[96,3072]{1,0:T(8,128)(2,1)} %fc_ref, bf16[384,768]{1,0:T(8,128)(2,1)} %fc2_ref), custom_call_target="tpu_custom_call" | custom-call | flops 1 | bytes 1 | tf_op jit(solution)/shard_map/pallas_call | solution.py:69
  24.8 4.3 %collective-permute-done.2.refs_7_.refs_3_ = bf16[112,768]{1,0:T(8,128)(2,1)S(1)} collective-permute-done((bf16[112,768]{1,0:T(8,128)(2,1)}, bf16[112,768]{1,0:T(8,128)(2,1)S(1)}, u32[]{:S(2)}, u32[]{:S(2)}) %collective-permute-start.2) | collective-permute-done | bytes 172064 | tf_op jit(solution)/shard_map/ppermute | solution.py:55
  34.4 2.5 %collective-permute-start.15 = (bf16[192,768]{1,0:T(8,128)(2,1)}, bf16[192,768]{1,0:T(8,128)(2,1)S(1)}, u32[]{:S(2)}, u32[]{:S(2)}) collective-permute-start(bf16[192,768]{1,0:T(8,128)(2,1)} %shard_map.170.refs_9_), channel_id=1, source_target_pairs={{0,6},{1,7},{2,0},{3,1},{4,2},{5,3},{6,4},{7,5},{8,14},{9,15},{10,... | collective-permute-start | bytes 884744 | tf_op jit(solution)/shard_map/ppermute | solution.py:55
  43.6 6.3 %shard_map.171 = (bf16[768,768]{1,0:T(8,128)(2,1)}, bf16[4,128,768]{2,1,0:T(8,128)(2,1)}, bf16[4,128,576]{2,1,0:T(8,128)(2,1)}, f32[4,3,128,128]{3,2,1,0:T(8,128...) custom-call(s32[3]{0:T(128)} %pad_add_fusion.scalar_ref, bf16[272,768]{1,0:T(8,128)(2,1)} %get-tuple-element.76.refs_0_.got_ref.refs_1_, ...), custom_call_target="tpu_custom_call" | custom-call | flops 1 | bytes 1 | tf_op jit(solution)/shard_map/pallas_call | solution.py:69
  50.5 3.5 %collective-permute-done.14.refs_11_ = bf16[192,768]{1,0:T(8,128)(2,1)S(1)} collective-permute-done((bf16[192,768]{1,0:T(8,128)(2,1)}, bf16[192,768]{1,0:T(8,128)(2,1)S(1)}, u32[]{:S(2)}, u32[]{:S(2)}) %collective-permute-start.14) | collective-permute-done | bytes 294944 | tf_op jit(solution)/shard_map/ppermute | solution.py:55
  55.1 14.4 %all-gather = bf16[512,768]{1,0:T(8,128)(2,1)} all-gather(bf16[128,768]{1,0:T(8,128)(2,1)} %get-tuple-element.84), channel_id=2, replica_groups=mesh['rep'=4,'shard'=8] {'rep'}, dimensions={0}, use_global_device_ids=true | all-gather | bytes 983040 | tf_op jit(solution)/shard_map/all_gather | solution.py:603
  70.6 10.0 %shard_map.173 = (bf16[4,128,768]{2,1,0:T(8,128)(2,1)}, f32[128,768]{1,0:T(8,128)}, bf16[4,128,768]{2,1,0:T(8,128)(2,1)}, bf16[4,128,768]{2,1,0:T(8,128)(2,1)}, ...) custom-call(s32[3]{0:T(128)} %pad_add_fusion.scalar_ref, ...), custom_call_target="tpu_custom_call" | custom-call | flops 1 | bytes 1 | tf_op jit(solution)/shard_map/pallas_call | solution.py:69
  84.1 7.2 %shard_map.174 = (bf16[4,192,768]{2,1,0:T(8,128)(2,1)}, bf16[4,192,768]{2,1,0:T(8,128)(2,1)}, f32[128,768]{1,0:T(8,128)}, bf16[128,768]{1,0:T(8,128)(2,1)}, bf16...) custom-call(s32[3]{0:T(128)} %pad_add_fusion.scalar_ref, bf16[4,128,768]{2,1,0:T(8,128)(2,1)} %get-tuple-element.92.refs_0_, ...), custom_call_target="tpu_custom_call" | custom-call | flops 1 | bytes 1 | tf_op jit(solution)/shard_map/pallas_call | solution.py:69
  94.9 6.8 %collective-permute-start.30 = (bf16[192,768]{1,0:T(8,128)(2,1)S(1)}, bf16[192,768]{1,0:T(8,128)(2,1)S(1)}, u32[]{:S(2)}, u32[]{:S(2)}) collective-permute-start(bf16[192,768]{1,0:T(8,128)(2,1)S(1)} %get-tuple-element.140), channel_id=1, source_target_pairs={{0,2},{1,3},{2,4},{3,5},{4,6},{5,7},{6,0},{7,1},{8,10},{9,11},{10,... | collective-permute-start | bytes 884744 | tf_op jit(solution)/shard_map/ppermute | solution.py:55
  101.7 3.0 %collective-permute-start.31 = (bf16[192,768]{1,0:T(8,128)(2,1)S(1)}, bf16[192,768]{1,0:T(8,128)(2,1)S(1)}, u32[]{:S(2)}, u32[]{:S(2)}) collective-permute-start(bf16[192,768]{1,0:T(8,128)(2,1)S(1)} %get-tuple-element.142), channel_id=1, source_target_pairs={{0,4},{1,5},{2,6},{3,7},{4,0},{5,1},{6,2},{7,3},{8,12},{9,13},{10,... | collective-permute-start | bytes 884744 | tf_op jit(solution)/shard_map/ppermute | solution.py:55
  104.7 2.9 %shard_map.175 = (f32[128,768]{1,0:T(8,128)}, bf16[128,768]{1,0:T(8,128)(2,1)}, f32[4,768]{1,0:T(4,128)}) custom-call(s32[3]{0:T(128)} %pad_add_fusion.scalar_ref, f32[128,768]{1,0:T(8,128)} %get-tuple-element.101.own_ref, bf16[128,768]{1,0:T(8,128)(2,1)} %copy-done.35, bf16[128,768]{1,0:T(8,128)(2,1)} %copy-done.36, bf16[128,768]{1,0:T(8,128)(2,1)} %copy-done.37, ...), custom_call_target="tpu_custom_call" | custom-call | flops 1 | bytes 1 | tf_op jit(solution)/shard_map/pallas_call | solution.py:69
  107.5 12.3 %all-gather.1 = bf16[512,768]{1,0:T(8,128)(2,1)} all-gather(bf16[128,768]{1,0:T(8,128)(2,1)} %get-tuple-element.105), channel_id=3, replica_groups=mesh['rep'=4,'shard'=8] {'rep'}, dimensions={0}, use_global_device_ids=true | all-gather | bytes 983040 | tf_op jit(solution)/shard_map/all_gather | solution.py:628
  122.0 12.3 %shard_map.176 = (bf16[4,112,768]{2,1,0:T(8,128)(2,1)}, bf16[4,112,768]{2,1,0:T(8,128)(2,1)}, f32[128,768]{1,0:T(8,128)}, bf16[128,768]{1,0:T(8,128)(2,1)}, bf16...) custom-call(s32[3]{0:T(128)} %pad_add_fusion.scalar_ref, bf16[4,128,768]{2,1,0:T(8,128)(2,1)} %bitcast.33, ...), custom_call_target="tpu_custom_call" | custom-call | flops 1 | bytes 1 | tf_op jit(solution)/shard_map/pallas_call | solution.py:69
  142.3 3.4 %collective-permute-done.26 = bf16[128,768]{1,0:T(8,128)(2,1)S(1)} collective-permute-done((bf16[128,768]{1,0:T(8,128)(2,1)S(1)}, bf16[128,768]{1,0:T(8,128)(2,1)S(1)}, u32[]{:S(2)}, u32[]{:S(2)}) %collective-permute-start.26) | collective-permute-done | bytes 196640 | tf_op jit(solution)/shard_map/ppermute | solution.py:58
  145.7 4.5 %collective-permute-done.27 = bf16[128,768]{1,0:T(8,128)(2,1)S(1)} collective-permute-done((bf16[128,768]{1,0:T(8,128)(2,1)S(1)}, bf16[128,768]{1,0:T(8,128)(2,1)S(1)}, u32[]{:S(2)}, u32[]{:S(2)}) %collective-permute-start.27) | collective-permute-done | bytes 196640 | tf_op jit(solution)/shard_map/ppermute | solution.py:58
  153.7 2.5 %collective-permute-start.36 = (bf16[112,768]{1,0:T(8,128)(2,1)S(1)}, bf16[112,768]{1,0:T(8,128)(2,1)S(1)}, u32[]{:S(2)}, u32[]{:S(2)}) collective-permute-start(bf16[112,768]{1,0:T(8,128)(2,1)S(1)} %get-tuple-element.144), channel_id=1, source_target_pairs={{0,6},{1,7},{2,0},{3,1},{4,2},{5,3},{6,4},{7,5},{8,14},{9,15},{10,... | collective-permute-start | bytes 516104 | tf_op jit(solution)/shard_map/ppermute | solution.py:55
  157.3 3.7 %collective-permute-done.34 = bf16[112,768]{1,0:T(8,128)(2,1)S(1)} collective-permute-done((bf16[112,768]{1,0:T(8,128)(2,1)S(1)}, bf16[112,768]{1,0:T(8,128)(2,1)S(1)}, u32[]{:S(2)}, u32[]{:S(2)}) %collective-permute-start.34) | collective-permute-done | bytes 172064 | tf_op jit(solution)/shard_map/ppermute | solution.py:55
  162.4 4.2 %collective-permute-done.35 = bf16[112,768]{1,0:T(8,128)(2,1)S(1)} collective-permute-done((bf16[112,768]{1,0:T(8,128)(2,1)S(1)}, bf16[112,768]{1,0:T(8,128)(2,1)S(1)}, u32[]{:S(2)}, u32[]{:S(2)}) %collective-permute-start.35) | collective-permute-done | bytes 172064 | tf_op jit(solution)/shard_map/ppermute | solution.py:55
  172.7 3.1 %shard_map.178 = (f32[96,3072]{1,0:T(8,128)}, f32[384,768]{1,0:T(8,128)}) custom-call(s32[3]{0:T(128)} %pad_add_fusion.scalar_ref, bf16[192,768]{1,0:T(8,128)(2,1)} %copy-done.6, bf16[192,768]{1,0:T(8,128)(2,1)} %copy-done.32, bf16[192,768]{1,0:T(8,128)(2,1)} %copy-done.33, bf16[192,768]{1,0:T(8,128)(2,1)} %copy-done.34), custom_call_target="tpu_custom_call" | custom-call | flops 1 | bytes 1 | tf_op jit(solution)/shard_map/pallas_call | solution.py:69
  178.6 2.7 %shard_map.177 = (f32[96,2304]{1,0:T(8,128)}, f32[96,768]{1,0:T(8,128)}, f32[2,96]{1,0:T(2,128)}, f32[6,96]{1,0:T(8,128)}, f32[1,384]{1,0:T(1,128)}) custom-call(s32[4]{0:T(128)} %pad_add_fusion.1.scalar_ref, bf16[112,768]{1,0:T(8,128)(2,1)} %copy-done.18, bf16[112,768]{1,0:T(8,128)(2,1)} %copy-done.38, bf16[112,768]{1,0:T(8,128)(2,1)} %copy-done.39, ...), custom_call_target="tpu_custom_call" | custom-call | flops 1 | bytes 1 | tf_op jit(solution)/shard_map/pallas_call | solution.py:69
  (193 shorter events, 56.0 us)
Async XLA Ops:
  5.0 24.0 %collective-permute-start.3 = (bf16[272,768]{1,0:T(8,128)(2,1)}, bf16[272,768]{1,0:T(8,128)(2,1)S(1)}, u32[]{:S(2)}, u32[]{:S(2)}) collective-permute-start(bf16[272,768]{1,0:T(8,128)(2,1)} %get-tuple-element.76.refs_0_.got_ref.refs_1_), channel_id=1, source_target_pairs={{0,8},{8,0},{16,24},{24,16},{1,9},{9,1},{17,25},{25,17},{2,10},{10... | collective-permute-start | bytes 1253384 | tf_op jit(solution)/shard_map/ppermute | solution.py:58
  8.0 21.1 %collective-permute-start.4 = (bf16[272,768]{1,0:T(8,128)(2,1)}, bf16[272,768]{1,0:T(8,128)(2,1)S(1)}, u32[]{:S(2)}, u32[]{:S(2)}) collective-permute-start(bf16[272,768]{1,0:T(8,128)(2,1)} %get-tuple-element.76.refs_0_.got_ref.refs_1_), channel_id=1, source_target_pairs={{0,16},{8,24},{16,0},{24,8},{1,17},{9,25},{17,1},{25,9},{2,18},{10... | collective-permute-start | bytes 1253384 | tf_op jit(solution)/shard_map/ppermute | solution.py:58
  9.5 19.6 %collective-permute-start.5 = (bf16[272,768]{1,0:T(8,128)(2,1)}, bf16[272,768]{1,0:T(8,128)(2,1)S(1)}, u32[]{:S(2)}, u32[]{:S(2)}) collective-permute-start(bf16[272,768]{1,0:T(8,128)(2,1)} %get-tuple-element.76.refs_0_.got_ref.refs_1_), channel_id=1, source_target_pairs={{0,24},{8,16},{16,8},{24,0},{1,25},{9,17},{17,9},{25,1},{2,26},{10... | collective-permute-start | bytes 1253384 | tf_op jit(solution)/shard_map/ppermute | solution.py:58
  11.5 13.2 %collective-permute-start.1 = (bf16[112,768]{1,0:T(8,128)(2,1)}, bf16[112,768]{1,0:T(8,128)(2,1)S(1)}, u32[]{:S(2)}, u32[]{:S(2)}) collective-permute-start(bf16[112,768]{1,0:T(8,128)(2,1)} %get-tuple-element.80.refs_4_.refs_0_), channel_id=1, source_target_pairs={{0,4},{1,5},{2,6},{3,7},{4,0},{5,1},{6,2},{7,3},{8,12},{9,13},{10,... | collective-permute-start | bytes 516104 | tf_op jit(solution)/shard_map/ppermute | solution.py:55
  30.2 19.7 %collective-permute-start.13 = (bf16[192,768]{1,0:T(8,128)(2,1)}, bf16[192,768]{1,0:T(8,128)(2,1)S(1)}, u32[]{:S(2)}, u32[]{:S(2)}) collective-permute-start(bf16[192,768]{1,0:T(8,128)(2,1)} %shard_map.170.refs_9_), channel_id=1, source_target_pairs={{0,2},{1,3},{2,4},{3,5},{4,6},{5,7},{6,0},{7,1},{8,10},{9,11},{10,... | collective-permute-start | bytes 884744 | tf_op jit(solution)/shard_map/ppermute | solution.py:55
  32.6 21.4 %collective-permute-start.14 = (bf16[192,768]{1,0:T(8,128)(2,1)}, bf16[192,768]{1,0:T(8,128)(2,1)S(1)}, u32[]{:S(2)}, u32[]{:S(2)}) collective-permute-start(bf16[192,768]{1,0:T(8,128)(2,1)} %shard_map.170.refs_9_), channel_id=1, source_target_pairs={{0,4},{1,5},{2,6},{3,7},{4,0},{5,1},{6,2},{7,3},{8,12},{9,13},{10,... | collective-permute-start | bytes 884744 | tf_op jit(solution)/shard_map/ppermute | solution.py:55
  34.4 19.6 %collective-permute-start.15 = (bf16[192,768]{1,0:T(8,128)(2,1)}, bf16[192,768]{1,0:T(8,128)(2,1)S(1)}, u32[]{:S(2)}, u32[]{:S(2)}) collective-permute-start(bf16[192,768]{1,0:T(8,128)(2,1)} %shard_map.170.refs_9_), channel_id=1, source_target_pairs={{0,6},{1,7},{2,0},{3,1},{4,2},{5,3},{6,4},{7,5},{8,14},{9,15},{10,... | collective-permute-start | bytes 884744 | tf_op jit(solution)/shard_map/ppermute | solution.py:55
  40.6 13.9 %collective-permute-start.10 = (bf16[192,768]{1,0:T(8,128)(2,1)}, bf16[192,768]{1,0:T(8,128)(2,1)S(1)}, u32[]{:S(2)}, u32[]{:S(2)}) collective-permute-start(bf16[192,768]{1,0:T(8,128)(2,1)} %shard_map.172.refs_5_), channel_id=1, source_target_pairs={{0,8},{8,0},{16,24},{24,16},{1,9},{9,1},{17,25},{25,17},{2,10},{10... | collective-permute-start | bytes 884744 | tf_op jit(solution)/shard_map/ppermute | solution.py:58
  42.1 12.5 %collective-permute-start.11 = (bf16[192,768]{1,0:T(8,128)(2,1)}, bf16[192,768]{1,0:T(8,128)(2,1)S(1)}, u32[]{:S(2)}, u32[]{:S(2)}) collective-permute-start(bf16[192,768]{1,0:T(8,128)(2,1)} %shard_map.172.refs_5_), channel_id=1, source_target_pairs={{0,16},{8,24},{16,0},{24,8},{1,17},{9,25},{17,1},{25,9},{2,18},{10... | collective-permute-start | bytes 884744 | tf_op jit(solution)/shard_map/ppermute | solution.py:58
  50.0 19.5 %collective-permute-start.12 = (bf16[192,768]{1,0:T(8,128)(2,1)S(1)}, bf16[192,768]{1,0:T(8,128)(2,1)S(1)}, u32[]{:S(2)}, u32[]{:S(2)}) collective-permute-start(bf16[192,768]{1,0:T(8,128)(2,1)S(1)} %copy-done.8), channel_id=1, source_target_pairs={{0,24},{8,16},{16,8},{24,0},{1,25},{9,17},{17,9},{25,1},{2,26},{10... | collective-permute-start | bytes 884744 | tf_op jit(solution)/shard_map/ppermute | solution.py:58
  54.0 15.5 %collective-permute-start.16 = (bf16[192,768]{1,0:T(8,128)(2,1)S(1)}, bf16[192,768]{1,0:T(8,128)(2,1)S(1)}, u32[]{:S(2)}, u32[]{:S(2)}) collective-permute-start(bf16[192,768]{1,0:T(8,128)(2,1)S(1)} %copy-done.7), channel_id=1, source_target_pairs={{0,1},{1,0},{2,3},{3,2},{4,5},{5,4},{6,7},{7,6},{8,9},{9,8},{10,11... | collective-permute-start | bytes 884744 | tf_op jit(solution)/shard_map/ppermute | solution.py:51
  54.0 15.4 %collective-permute-start.17 = (bf16[192,768]{1,0:T(8,128)(2,1)S(1)}, bf16[192,768]{1,0:T(8,128)(2,1)S(1)}, u32[]{:S(2)}, u32[]{:S(2)}) collective-permute-start(bf16[192,768]{1,0:T(8,128)(2,1)S(1)} %collective-permute-done.13.refs_10_), channel_id=1, source_target_pairs={{0,1},{1,0},{2,3},{3,2},{4,5},{5,4},{6,7},{7,6},{8,9},{9,8},{10,11... | collective-permute-start | bytes 884744 | tf_op jit(solution)/shard_map/ppermute | solution.py:51
  54.6 15.0 %collective-permute-start.18 = (bf16[192,768]{1,0:T(8,128)(2,1)S(1)}, bf16[192,768]{1,0:T(8,128)(2,1)S(1)}, u32[]{:S(2)}, u32[]{:S(2)}) collective-permute-start(bf16[192,768]{1,0:T(8,128)(2,1)S(1)} %collective-permute-done.14.refs_11_), channel_id=1, source_target_pairs={{0,1},{1,0},{2,3},{3,2},{4,5},{5,4},{6,7},{7,6},{8,9},{9,8},{10,11... | collective-permute-start | bytes 884744 | tf_op jit(solution)/shard_map/ppermute | solution.py:51
  54.6 14.9 %collective-permute-start.19 = (bf16[192,768]{1,0:T(8,128)(2,1)S(1)}, bf16[192,768]{1,0:T(8,128)(2,1)S(1)}, u32[]{:S(2)}, u32[]{:S(2)}) collective-permute-start(bf16[192,768]{1,0:T(8,128)(2,1)S(1)} %collective-permute-done.15.refs_12_), channel_id=1, source_target_pairs={{0,1},{1,0},{2,3},{3,2},{4,5},{5,4},{6,7},{7,6},{8,9},{9,8},{10,11... | collective-permute-start | bytes 884744 | tf_op jit(solution)/shard_map/ppermute | solution.py:51
  94.9 39.4 %collective-permute-start.30 = (bf16[192,768]{1,0:T(8,128)(2,1)S(1)}, bf16[192,768]{1,0:T(8,128)(2,1)S(1)}, u32[]{:S(2)}, u32[]{:S(2)}) collective-permute-start(bf16[192,768]{1,0:T(8,128)(2,1)S(1)} %get-tuple-element.140), channel_id=1, source_target_pairs={{0,2},{1,3},{2,4},{3,5},{4,6},{5,7},{6,0},{7,1},{8,10},{9,11},{10,... | collective-permute-start | bytes 884744 | tf_op jit(solution)/shard_map/ppermute | solution.py:55
  101.7 34.2 %collective-permute-start.31 = (bf16[192,768]{1,0:T(8,128)(2,1)S(1)}, bf16[192,768]{1,0:T(8,128)(2,1)S(1)}, u32[]{:S(2)}, u32[]{:S(2)}) collective-permute-start(bf16[192,768]{1,0:T(8,128)(2,1)S(1)} %get-tuple-element.142), channel_id=1, source_target_pairs={{0,4},{1,5},{2,6},{3,7},{4,0},{5,1},{6,2},{7,3},{8,12},{9,13},{10,... | collective-permute-start | bytes 884744 | tf_op jit(solution)/shard_map/ppermute | solution.py:55
  104.7 31.3 %collective-permute-start.32 = (bf16[192,768]{1,0:T(8,128)(2,1)S(1)}, bf16[192,768]{1,0:T(8,128)(2,1)S(1)}, u32[]{:S(2)}, u32[]{:S(2)}) collective-permute-start(bf16[192,768]{1,0:T(8,128)(2,1)S(1)} %get-tuple-element.141), channel_id=1, source_target_pairs={{0,6},{1,7},{2,0},{3,1},{4,2},{5,3},{6,4},{7,5},{8,14},{9,15},{10,... | collective-permute-start | bytes 884744 | tf_op jit(solution)/shard_map/ppermute | solution.py:55
  119.9 19.2 %collective-permute-start.23 = (bf16[128,768]{1,0:T(8,128)(2,1)S(1)}, bf16[128,768]{1,0:T(8,128)(2,1)S(1)}, u32[]{:S(2)}, u32[]{:S(2)}) collective-permute-start(bf16[128,768]{1,0:T(8,128)(2,1)S(1)} %copy-done.45), channel_id=1, source_target_pairs={{0,8},{8,0},{16,24},{24,16},{1,9},{9,1},{17,25},{25,17},{2,10},{10... | collective-permute-start | bytes 589832 | tf_op jit(solution)/shard_map/ppermute | solution.py:58
  121.1 18.9 %collective-permute-start.24 = (bf16[128,768]{1,0:T(8,128)(2,1)S(1)}, bf16[128,768]{1,0:T(8,128)(2,1)S(1)}, u32[]{:S(2)}, u32[]{:S(2)}) collective-permute-start(bf16[128,768]{1,0:T(8,128)(2,1)S(1)} %copy-done.44), channel_id=1, source_target_pairs={{0,16},{8,24},{16,0},{24,8},{1,17},{9,25},{17,1},{25,9},{2,18},{10... | collective-permute-start | bytes 589832 | tf_op jit(solution)/shard_map/ppermute | solution.py:58
  136.1 15.2 %collective-permute-start.33 = (bf16[4,112,768]{2,1,0:T(8,128)(2,1)S(1)}, bf16[4,112,768]{2,1,0:T(8,128)(2,1)S(1)}, u32[]{:S(2)}, u32[]{:S(2)}) collective-permute-start(bf16[4,112,768]{2,1,0:T(8,128)(2,1)S(1)} %copy-done.42), channel_id=1, source_target_pairs={{0,1},{1,0},{2,3},{3,2},{4,5},{5,4},{6,7},{7,6},{8,9},{9,8},{10,11... | collective-permute-start | bytes 2064392 | tf_op jit(solution)/shard_map/ppermute | solution.py:51
  150.4 18.4 %collective-permute-start.40 = (bf16[192,768]{1,0:T(8,128)(2,1)S(1)}, bf16[192,768]{1,0:T(8,128)(2,1)S(1)}, u32[]{:S(2)}, u32[]{:S(2)}) collective-permute-start(bf16[192,768]{1,0:T(8,128)(2,1)S(1)} %fusion.1.refs_0_), channel_id=1, source_target_pairs={{0,8},{8,0},{16,24},{24,16},{1,9},{9,1},{17,25},{25,17},{2,10},{10... | collective-permute-start | bytes 884744 | tf_op jit(solution)/shard_map/ppermute | solution.py:58
  153.5 13.2 %collective-permute-start.35 = (bf16[112,768]{1,0:T(8,128)(2,1)S(1)}, bf16[112,768]{1,0:T(8,128)(2,1)S(1)}, u32[]{:S(2)}, u32[]{:S(2)}) collective-permute-start(bf16[112,768]{1,0:T(8,128)(2,1)S(1)} %get-tuple-element.145), channel_id=1, source_target_pairs={{0,4},{1,5},{2,6},{3,7},{4,0},{5,1},{6,2},{7,3},{8,12},{9,13},{10,... | collective-permute-start | bytes 516104 | tf_op jit(solution)/shard_map/ppermute | solution.py:55
  153.7 12.9 %collective-permute-start.36 = (bf16[112,768]{1,0:T(8,128)(2,1)S(1)}, bf16[112,768]{1,0:T(8,128)(2,1)S(1)}, u32[]{:S(2)}, u32[]{:S(2)}) collective-permute-start(bf16[112,768]{1,0:T(8,128)(2,1)S(1)} %get-tuple-element.144), channel_id=1, source_target_pairs={{0,6},{1,7},{2,0},{3,1},{4,2},{5,3},{6,4},{7,5},{8,14},{9,15},{10,... | collective-permute-start | bytes 516104 | tf_op jit(solution)/shard_map/ppermute | solution.py:55
  156.2 15.0 %collective-permute-start.41 = (bf16[192,768]{1,0:T(8,128)(2,1)S(1)}, bf16[192,768]{1,0:T(8,128)(2,1)S(1)}, u32[]{:S(2)}, u32[]{:S(2)}) collective-permute-start(bf16[192,768]{1,0:T(8,128)(2,1)S(1)} %fusion.1.refs_0_), channel_id=1, source_target_pairs={{0,16},{8,24},{16,0},{24,8},{1,17},{9,25},{17,1},{25,9},{2,18},{10... | collective-permute-start | bytes 884744 | tf_op jit(solution)/shard_map/ppermute | solution.py:58
  (68 other events, 556.7 us)
where the time goes:
time: 185 us; the launch traced here: 183 us
  starting transfers between devices  54.6 us (30%)
  Pallas kernels  52.1 us (28%)
  waiting for transfers between devices  33.5 us (18%)
  blocking collectives  26.7 us (14%)
  local copies, waits for them, and re-layouts  7.29 us (4%)
  other arithmetic  7.11 us (4%)
    pallas_call x10, Pallas kernels, run(): pl.pallas_call(kernel, out_shape=[jax.ShapeDtypeStruct(shape, dtype) for...  52.1 us
    ppermute x12, starting transfers between devices, along(): return lax.ppermute(v, 'shard', [(i, (i + 2 * hop) % n) for i in range(n)])  26.4 us
    ppermute x21, starting transfers between devices, rep(): return lax.ppermute(v, 'rep', [(i, i ^ k) for i in range(4)])  25.9 us
    ppermute x12, waiting for transfers between devices, along(): return lax.ppermute(v, 'shard', [(i, (i + 2 * hop) % n) for i in range(n)])  22.1 us
    all_gather x1, blocking collectives, local(): attended = lax.all_gather(sent, 'rep', axis=0)  14.4 us
    all_gather x1, blocking collectives, local(): grad_branch = lax.all_gather(grad_branch, 'rep', axis=0)  12.3 us
    ppermute x21, waiting for transfers between devices, rep(): return lax.ppermute(v, 'rep', [(i, i ^ k) for i in range(4)])  9.45 us
    unnamed x98, local copies, waits for them, and re-layouts  5.21 us
  transfers between devices with their start and end apart: 43, of which 10 were waited for; matrix products, arithmetic and copies ran while one was open for 3% of the time, Pallas kernels for 20%

commit v1 on v0

v1 whole, which is shorter than its diff:
```python
from functools import partial

import jax
import jax.numpy as jnp
from jax import lax
from jax.experimental import pallas as pl
from jax.experimental.pallas import tpu as pltpu
from jax.sharding import PartitionSpec as P

HEAD_DIM = 64
EPS = 1e-05
LOW = jnp.bfloat16
F32 = jnp.float32


def normalize(values, gain_row, shift_row):
    row_mean = jnp.mean(values, axis=-1, keepdims=True)
    centered = values - row_mean
    variance = jnp.mean(centered * centered, axis=-1, keepdims=True)
    return centered * lax.rsqrt(variance + EPS) * gain_row + shift_row


def contract(left_rows, right_rows):
    return lax.dot_general(
        left_rows, right_rows, (((0,), (0,)), ((), ())), preferred_element_type=F32
    )


def back_mult(grad_rows, weight):
    return lax.dot_general(
        grad_rows, weight, (((1,), (1,)), ((), ())), preferred_element_type=F32
    )


def mult(left, right):
    return jnp.dot(left, right, preferred_element_type=F32)


class Links:
    def __init__(self):
        self.shards = lax.axis_size("shard")
        self.line = self.shards // 2
        place = lax.axis_index("shard")
        self.z = place // 2
        self.c = place % 2
        self.j = lax.axis_index("rep")
        self.scalars = jnp.stack([self.z, self.c, self.j, place]).astype(jnp.int32)
        assert lax.axis_size("rep") == 4

    def core(self, v):
        return lax.ppermute(v, "shard", [(i, i ^ 1) for i in range(self.shards)])

    def along(self, v, hop):
        n = self.shards
        return lax.ppermute(v, "shard", [(i, (i + 2 * hop) % n) for i in range(n)])

    def rep(self, v, k):
        return lax.ppermute(v, "rep", [(i, i ^ k) for i in range(4)])

    def rep_gather(self, v):
        return [v] + [self.rep(v, k) for k in range(1, 4)]


def pick(stack, index, axis=0):
    return lax.dynamic_index_in_dim(stack, index, axis, keepdims=False)


def run(kernel, out_shapes, scalars, args, scratch=()):
    return pl.pallas_call(
        kernel,
        out_shape=[jax.ShapeDtypeStruct(shape, dtype) for shape, dtype in out_shapes],
        in_specs=[pl.BlockSpec(memory_space=pltpu.SMEM)]
        + [pl.BlockSpec(memory_space=pltpu.VMEM)] * len(args),
        out_specs=[pl.BlockSpec(memory_space=pltpu.VMEM)] * len(out_shapes),
        scratch_shapes=list(scratch),
        compiler_params=pltpu.CompilerParams(vmem_limit_bytes=56 * 1024 * 1024),
        cost_estimate=pl.CostEstimate(flops=1, bytes_accessed=1, transcendentals=0),
    )(scalars, *args)


def tie(value, *others):
    return lax.optimization_barrier((value, others))[0]


def line_gather(links, block, end=None):
    return [block] + [links.along(block, hop) for hop in range(1, end or links.line)]


def with_partners(links, mine):
    return mine + [links.core(v) for v in mine]


def assemble(scalar_ref, refs, out, start, rows):
    line = len(refs) // 2
    z, c = scalar_ref[0], scalar_ref[1]
    for hop in range(line):
        at = lax.rem(z + line - hop, line)
        for side in range(2):
            to = (2 * at + c) if side == 0 else (2 * at + 1 - c)
            block = refs[side * line + hop][pl.ds(start, rows), :]
            if rows % 16 == 0:
                out[pl.ds(pl.multiple_of(to * rows, 16), rows), :] = block
                continue
            for s in range(2 * line):

                @pl.when(to == s)
                def _(block=block, s=s):
                    out[s * rows : (s + 1) * rows, :] = block


def store_pieces(scalar_ref, scratch, first, outs, start):
    mine, other = outs
    rows = scratch.shape[1]
    line = scratch.shape[0] // 2
    pitch = mine.shape[0] // line
    for s in range(2 * line):
        scratch[s] = first[s * rows : (s + 1) * rows]
    z, c = scalar_ref[0], scalar_ref[1]
    for hop in range(line):
        at = 2 * lax.rem(z + hop, line)
        to = pl.ds(hop * pitch + start, rows)
        mine[to, :] = scratch[at + c].astype(LOW)
        other[to, :] = scratch[at + 1 - c].astype(LOW)


def line_sum(line, mine, theirs):
    rows = mine.shape[0] // line
    both = [
        mine[hop * rows : (hop + 1) * rows].astype(F32)
        + theirs[hop * rows : (hop + 1) * rows].astype(F32)
        for hop in range(line)
    ]
    return [v.astype(LOW) for v in both[1:]], both[0]


def line_send(links, sent, own):
    for hop, value in enumerate(sent, start=1):
        own = own + links.along(value, hop).astype(F32)
    return own


def pad_rows(v, rows):
    return v if v.shape[0] == rows else jnp.pad(v, ((0, rows - v.shape[0]), (0, 0)))


def unit(values):
    row_mean = jnp.mean(values, axis=-1, keepdims=True)
    centered = values - row_mean
    variance = jnp.mean(centered * centered, axis=-1, keepdims=True)
    scale = lax.rsqrt(variance + EPS)
    return centered * scale, scale


def norm_back(cotangent, gain, unit_rows, scale):
    weighted = cotangent * gain
    return scale * (
        weighted
        - jnp.mean(weighted, axis=-1, keepdims=True)
        - unit_rows * jnp.mean(weighted * unit_rows, axis=-1, keepdims=True)
    )


def gelu_pair(x):
    root = 0.7978845608028654
    square = x * x
    bend = jnp.tanh(root * x * (1.0 + 0.044715 * square))
    half = 0.5 * (1.0 + bend)
    slope = half + 0.5 * x * (1.0 - bend * bend) * root * (1.0 + 3 * 0.044715 * square)
    return x * half, slope


def choose(index, options):
    value = options[0]
    for k in range(1, len(options)):
        value = jnp.where(index == k, options[k], value)
    return value


def live_rows(got, slots, count):
    total = jnp.zeros((1, 1), F32)
    for s in range(count):
        total = total + got[slots : slots + 1, s : s + 1].astype(F32)
    place = lax.broadcasted_iota(jnp.int32, (slots, 1), 0).astype(F32)
    return (place < total).astype(F32)


def pack_attn(links, args, rows, part, full):
    gains, shifts, bias, w_qkv, w_proj = args
    model = w_proj.shape[1]

    def kernel(scalar_ref, gain, shift, bias_ref, qkv_ref, p_ref, out):
        j, s_here = scalar_ref[2], scalar_ref[3]
        for t in range(3):
            out[pl.ds(0, rows), t * part : (t + 1) * part] = choose(
                j,
                [
                    qkv_ref[:, t * model + p * part : t * model + (p + 1) * part]
                    for p in range(4)
                ],
            )
        out[pl.ds(0, rows), 3 * part :] = choose(
            j, [p_ref[:, p * part : (p + 1) * part] for p in range(4)]
        )
        bias_row = bias_ref[...].reshape(1, 4 * rows)
        mine = choose(j, [bias_row[:, p * rows : (p + 1) * rows] for p in range(4)])
        small = jnp.concatenate(
            [v.astype(F32) for v in (gain[...], shift[...], mine)] + [jnp.zeros((7, rows), F32)]
        )
        small = jnp.concatenate([small] * links.shards, axis=1)
        lane = lax.broadcasted_iota(jnp.int32, small.shape, 1)
        here = (lane >= s_here * rows) & (lane < (s_here + 1) * rows)
        out[pl.ds(full, 16), :] = jnp.where(here, small, 0.0).astype(LOW)

    return run(kernel, [((full + 16, model), LOW)], links.scalars, args)[0]


def pack_slots(links, tokens, lengths):
    slots, model = tokens.shape
    count = lengths.shape[1]

    def kernel(scalar_ref, tok, len_ref, sent):
        sent[pl.ds(0, slots), :] = tok[...]
        sent[pl.ds(slots, 16), :] = jnp.zeros((16, model), LOW)
        sent[slots : slots + 1, :count] = len_ref[...].astype(F32).astype(LOW)

    shapes = [((slots + 16, model), LOW)]
    return run(kernel, shapes, links.scalars, [tokens, lengths])[0]


def pack_ff(links, w_fc, w_fc2, rows, full):
    model = w_fc2.shape[1]

    def kernel(scalar_ref, fc_ref, fc2_ref, out):
        j = scalar_ref[2]
        for s in range(links.shards):
            out[pl.ds(0, rows), s * rows : (s + 1) * rows] = choose(
                j,
                [fc_ref[:, (4 * s + p) * rows : (4 * s + p + 1) * rows] for p in range(4)],
            )
        out[pl.ds(full, rows), :] = choose(
            j, [fc2_ref[p * rows : (p + 1) * rows, :] for p in range(4)]
        )

    return run(kernel, [((full + rows, model), LOW)], links.scalars, [w_fc, w_fc2])[0]


def proj_lanes(links, blocks, out_grad, rows, part):
    model = blocks[0].shape[1]
    line = links.line

    def kernel(scalar_ref, *refs):
        ins, cot, mine, other, scratch = refs[:-4], *refs[-4:]
        mine[pl.ds(part // 2, cot.shape[0]), :] = cot[...]
        assemble(scalar_ref, [ref.at[:, pl.ds(512, 256)] for ref in ins], scratch, 0, rows)
        c = scalar_ref[1]
        for out, side in ((mine, c), (other, 1 - c)):
            for g in range(4):
                at = pl.ds(pl.multiple_of(g * part + side * (part // 2), 16), part // 2)
                out[pl.ds(0, part // 2), g * part : (g + 1) * part] = scratch[at, 64:]

    shapes = [((part // 2 + out_grad.shape[0], model), LOW), ((part // 2, model), LOW)]
    scratch = [pltpu.VMEM((model, 256), LOW)]
    return run(kernel, shapes, links.scalars, [*blocks, out_grad], scratch)


def attn_forward(links, got, blocks, slots, heads, count, rows):
    model = blocks[0].shape[1]
    part = heads * HEAD_DIM
    full = -(-rows // 16) * 16

    def kernel(scalar_ref, *refs):
        ins, parts = refs[:4], refs[4 : 4 + len(blocks)]
        w_ref, unit_out, qkv_out, probs_out, sent_out, small_out = refs[4 + len(blocks) :]
        j = scalar_ref[2]
        assemble(scalar_ref, parts, w_ref, 0, rows)
        small_sum = jnp.zeros(small_out.shape, F32)
        for ref in parts:
            small_sum = small_sum + ref[pl.ds(full, 16), :].astype(F32)
        small_out[...] = small_sum
        cut = lambda row: choose(
            j, [small_sum[row : row + 1, p * part : (p + 1) * part] for p in range(4)]
        )
        q_bias, v_bias = cut(4), cut(5)
        rows_at = lax.broadcasted_iota(jnp.int32, (slots, slots), 0).astype(F32)
        cols_at = lax.broadcasted_iota(jnp.int32, (slots, slots), 1).astype(F32)
        for k in range(4):
            normed = unit(ins[k][:slots].astype(F32))[0] * small_sum[0:1] + small_sum[2:3]
            unit_out[k * slots : (k + 1) * slots] = normed.astype(LOW)
        qkv = mult(unit_out[...], w_ref[:, : 3 * part])
        qkv_out[:, :part] = (qkv[:, :part] + q_bias).astype(LOW)
        qkv_out[:, part : 2 * part] = qkv[:, part : 2 * part].astype(LOW)
        qkv_out[:, 2 * part :] = (qkv[:, 2 * part :] + v_bias).astype(LOW)
        for k in range(4):
            block = slice(k * slots, (k + 1) * slots)
            end = jnp.zeros((1, 1), F32)
            row_seq, col_seq = jnp.zeros((slots, slots), F32), jnp.zeros((slots, slots), F32)
            for s in range(count):
                end = end + ins[k][slots : slots + 1, s : s + 1].astype(F32)
                row_seq = row_seq + (end <= rows_at).astype(F32)
                col_seq = col_seq + (end <= cols_at).astype(F32)
            allowed = (row_seq == col_seq) & (cols_at <= rows_at)
            for h in range(heads):
                at = h * HEAD_DIM
                query = qkv_out[block, at : at + HEAD_DIM]
                keys = qkv_out[block, part + at : part + at + HEAD_DIM]
                values = qkv_out[block, 2 * part + at : 2 * part + at + HEAD_DIM]
                scores = back_mult(query, keys) * (HEAD_DIM**-0.5)
                scores = jnp.where(allowed, scores, -1000000000.0)
                exponent = jnp.exp(scores - jnp.max(scores, axis=-1, keepdims=True))
                probs = exponent / jnp.sum(exponent, axis=-1, keepdims=True)
                probs_out[k, h] = probs
                attended = mult(probs.astype(LOW), values)
                to = k * part + at
                sent_out[:, to : to + HEAD_DIM] = attended.astype(LOW)

    shapes = [
        ((model, model), LOW),
        ((4 * slots, model), LOW),
        ((4 * slots, 3 * part), LOW),
        ((4, heads, slots, slots), F32),
        ((slots, 4 * part), LOW),
        ((16, model), F32),
    ]
    return run(kernel, shapes, links.scalars, [*got, *blocks])


def ff_both(links, got, attended, proj, blocks, small, slots, count, rows):
    model = blocks[0].shape[1]
    part = model // 4
    full = -(-rows // 16) * 16
    held = 4 + 1 + 8 + len(blocks) + 1

    def kernel(scalar_ref, *refs):
        ins, att, p_parts, parts, small_ref = (
            refs[:4],
            refs[4],
            refs[5:13],
            refs[13 : held - 1],
            refs[held - 1],
        )
        att_out, middle_out, normed_out, active_out, hidden_out, cot_out = refs[held : held + 6]
        own_out, *sent_out = refs[held + 6 : held + 10]
        sums_out, p_ref, fc2_ref, fc_ref = refs[held + 10 :]
        c, j = scalar_ref[1], scalar_ref[2]
        assemble(scalar_ref, parts, fc_ref, 0, rows)
        assemble(scalar_ref, parts, fc2_ref, full, rows)
        for p in range(4):
            for g in range(4):
                for side, half in ((c, p_parts[:4]), (1 - c, p_parts[4:])):
                    at = pl.ds(pl.multiple_of(g * part + side * (part // 2), 16), part // 2)
                    p_ref[at, p * part : (p + 1) * part] = choose(
                        j ^ p, [ref[: part // 2, g * part : (g + 1) * part] for ref in half]
                    )
        total = jnp.zeros((1, model), F32)
        for k in range(4):
            for p in range(4):
                att_out[k * slots : (k + 1) * slots, p * part : (p + 1) * part] = choose(
                    j ^ p, [att[p, :, (k ^ m) * part : ((k ^ m) + 1) * part] for m in range(4)]
                )
        for first in (0, 2):
            both = (first, first + 1)
            block = slice(first * slots, (first + 2) * slots)
            middle = jnp.concatenate([ins[k][:slots].astype(F32) for k in both])
            middle = middle + mult(att_out[block], p_ref[...]) + small_ref[6:7]
            if first == 0:
                middle_out[...] = middle[:slots]
            normed = (unit(middle)[0] * small_ref[1:2] + small_ref[3:4]).astype(LOW)
            normed_out[block] = normed
            hidden = mult(normed, fc_ref[...]) + small_ref[8:9]
            active, slope = gelu_pair(hidden)
            active_out[block] = active.astype(LOW)
            cot = jnp.concatenate(
                [
                    p_parts[k][part // 2 :].astype(F32) * live_rows(ins[k], slots, count)
                    for k in both
                ]
            ).astype(LOW)
            cot_out[block] = cot
            grad_hidden = (back_mult(cot, fc2_ref[...]) * slope).astype(LOW)
            hidden_out[block] = grad_hidden
            total = total + jnp.sum(grad_hidden.astype(F32), axis=0, keepdims=True)
            grad_normed = back_mult(grad_hidden, fc_ref[...])
            for k in both:
                grad_rows = grad_normed[(k - first) * slots : (k - first + 1) * slots]
                if k == 0:
                    own_out[...] = grad_rows
                else:
                    sent_out[k - 1][...] = grad_rows.astype(LOW)
        sums_out[...] = total

    shapes = [
        ((4 * slots, model), LOW),
        ((slots, model), F32),
        ((4 * slots, model), LOW),
        ((4 * slots, model), LOW),
        ((4 * slots, model), LOW),
        ((4 * slots, model), LOW),
        ((slots, model), F32),
        *[((slots, model), LOW)] * 3,
        ((1, model), F32),
        ((model, model), LOW),
        ((model, model), LOW),
    ]
    args = [*got, attended, *proj, *blocks, small]
    return run(kernel, shapes, links.scalars, args, [pltpu.VMEM((model, model), LOW)])


def ff_grads(links, normed, active, hidden, cot, fc2, slots, rows):
    model = normed.shape[1]
    line = links.line
    full = -(-rows // 16) * 16

    def kernel(scalar_ref, *refs):
        normed_ref, active_ref, hidden_ref, cot_ref, fc2_ref = refs[:5]
        pieces = refs[5:7]
        branch_own, *branch_sent, scratch = refs[7:]
        for start, left, right in ((0, normed_ref, hidden_ref), (full, active_ref, cot_ref)):
            store_pieces(scalar_ref, scratch, contract(left[...], right[...]), pieces, start)
        branch = mult(active_ref[...], fc2_ref[...])
        branch_own[...] = branch[:slots]
        for k in range(1, 4):
            branch_sent[k - 1][...] = branch[k * slots : (k + 1) * slots].astype(LOW)

    shapes = [
        *[((line * (full + rows), model), LOW)] * 2,
        ((slots, model), F32),
        *[((slots, model), LOW)] * 3,
    ]
    args = [normed, active, hidden, cot, fc2]
    return run(kernel, shapes, links.scalars, args, [pltpu.VMEM((2 * line, rows, model), F32)])


def middle_back(links, own, received, middle, got, out_grad, small, slots, count):
    def kernel(scalar_ref, own_ref, r1, r2, r3, middle_ref, got_ref, cot_ref, small_ref, *outs):
        grad_out, branch_out, sums_out = outs
        cotangent = own_ref[...] + r1[...].astype(F32) + r2[...].astype(F32) + r3[...].astype(F32)
        unit_rows, scale = unit(middle_ref[...])
        live = live_rows(got_ref, slots, count)
        cot = cot_ref[...].astype(F32) * live
        grad = cot + norm_back(cotangent, small_ref[1:2], unit_rows, scale)
        grad_out[...] = grad
        branch = grad.astype(LOW)
        branch_out[...] = branch
        sums_out[0:1] = jnp.sum(cotangent * unit_rows, axis=0, keepdims=True)
        sums_out[1:2] = jnp.sum(cotangent, axis=0, keepdims=True)
        sums_out[2:3] = jnp.sum(branch.astype(F32), axis=0, keepdims=True)
        sums_out[3:4] = jnp.sum(cot, axis=0, keepdims=True)

    model = own.shape[1]
    shapes = [((slots, model), F32), ((slots, model), LOW), ((4, model), F32)]
    return run(kernel, shapes, links.scalars, [own, *received, middle, got, out_grad, small])


def attn_back(
    links,
    grads,
    got,
    proj,
    weights,
    normed,
    qkv,
    probs,
    attended,
    sums,
    bias,
    slots,
    rows,
):
    model = normed.shape[1]
    heads = probs.shape[1]
    part = heads * HEAD_DIM
    line = links.line
    full = -(-rows // 16) * 16
    scale = HEAD_DIM**-0.5

    def kernel(scalar_ref, *refs):
        grad_ref, ins = refs[0], refs[1:5]
        p_ref, w_ref, normed_ref, qkv_ref, probs_ref, att_ref, sums_ref, bias_ref = refs[5:13]
        pieces = refs[13:15]
        own_out, *sent_out, scratch, grad_qkv, branch, cols = refs[15:]
        j = scalar_ref[2]
        for k in range(4):
            block = slice(k * slots, (k + 1) * slots)
            branch[block] = grad_ref[j ^ k]
            cols[block] = choose(
                j, [grad_ref[j ^ k, :, p * part : (p + 1) * part] for p in range(4)]
            )
        proj_rows = p_ref[pl.ds(pl.multiple_of(j * part, part), part), :]
        grad_att = back_mult(branch[...], proj_rows).astype(LOW)
        for k in range(4):
            block = slice(k * slots, (k + 1) * slots)
            for h in range(heads):
                at = h * HEAD_DIM
                query = qkv_ref[block, at : at + HEAD_DIM]
                keys = qkv_ref[block, part + at : part + at + HEAD_DIM]
                values = qkv_ref[block, 2 * part + at : 2 * part + at + HEAD_DIM]
                prob = probs_ref[k, h]
                cot = grad_att[block, at : at + HEAD_DIM]
                grad_probs = back_mult(cot, values)
                inner = jnp.sum(prob * grad_probs, axis=-1, keepdims=True)
                grad_scores = (prob * (grad_probs - inner)).astype(LOW)
                grad_qkv[block, at : at + HEAD_DIM] = (mult(grad_scores, keys) * scale).astype(LOW)
                grad_qkv[block, part + at : part + at + HEAD_DIM] = (
                    contract(grad_scores, query) * scale
                ).astype(LOW)
                grad_qkv[block, 2 * part + at : 2 * part + at + HEAD_DIM] = contract(
                    prob.astype(LOW), cot
                ).astype(LOW)
        grad_rows = grad_qkv[...]
        qkv_sum = jnp.sum(grad_rows.astype(F32), axis=0, keepdims=True)
        grad_normed = back_mult(grad_rows, w_ref[:, : 3 * part])
        own_out[...] = grad_normed[:slots]
        for k in range(1, 4):
            sent_out[k - 1][...] = grad_normed[k * slots : (k + 1) * slots].astype(LOW)
        gain_sum = jnp.zeros((1, model), F32)
        for k in range(4):
            unit_rows = unit(ins[k][:slots].astype(F32))[0]
            block = slice(k * slots, (k + 1) * slots)
            gain_sum = gain_sum + jnp.sum(grad_normed[block] * unit_rows, axis=0, keepdims=True)
        shift_sum = jnp.sum(grad_normed, axis=0, keepdims=True)
        total = jnp.concatenate(
            [contract(normed_ref[...], grad_rows), contract(att_ref[...], cols[...])], axis=1
        )
        store_pieces(scalar_ref, scratch, total, pieces, 0)
        spread = lambda v: jnp.concatenate(
            [jnp.where(j == p, v, jnp.zeros_like(v)) for p in range(4)], axis=1
        )
        vectors = jnp.concatenate(
            [
                gain_sum,
                sums_ref[0:1],
                shift_sum,
                sums_ref[1:2],
                spread(qkv_sum[:, :part]),
                spread(qkv_sum[:, 2 * part :]),
                sums_ref[2:4],
                bias_ref[...],
                jnp.zeros((7, model), F32),
            ]
        ).astype(LOW)
        for out in pieces:
            for hop in range(line):
                out[pl.ds(hop * (full + 16) + full, 16), :] = vectors

    shapes = [
        *[((line * (full + 16), model), LOW)] * 2,
        ((slots, model), F32),
        *[((slots, model), LOW)] * 3,
    ]
    args = [grads, *got, proj, weights, normed, qkv, probs, attended, sums, bias]
    scratch = [
        pltpu.VMEM((2 * line, rows, model), F32),
        pltpu.VMEM((4 * slots, 3 * part), LOW),
        pltpu.VMEM((4 * slots, model), LOW),
        pltpu.VMEM((4 * slots, part), LOW),
    ]
    return run(kernel, shapes, links.scalars, args, scratch)


def ff_results(links, parts, rows):
    model = parts[0].shape[1]
    shards = links.shards
    full = -(-rows // 16) * 16

    def kernel(scalar_ref, *refs):
        ins, fc_out, fc2_out = refs[:4], refs[4], refs[5]
        j = scalar_ref[2]
        for p in range(4):
            left = choose(j ^ p, [ref[pl.ds(0, rows), :].astype(F32) for ref in ins])
            for s in range(shards):
                at = (s * 4 + p) * rows
                fc_out[:, at : at + rows] = left[:, s * rows : (s + 1) * rows]
            fc2_out[pl.ds(p * rows, rows), :] = choose(
                j ^ p, [ref[pl.ds(full, rows), :].astype(F32) for ref in ins]
            )

    shapes = [((rows, 4 * model), F32), ((4 * rows, model), F32)]
    return run(kernel, shapes, links.scalars, parts)


def attn_results(links, parts, rows):
    model = parts[0].shape[1]
    shards = links.shards
    part = model // 4
    full = -(-rows // 16) * 16

    def kernel(scalar_ref, *refs):
        ins, qkv_out, proj_out, gains_out, shifts_out, bias_out = refs[:4], *refs[4:]
        j, s_here = scalar_ref[2], scalar_ref[3]
        for p in range(4):
            block = choose(j ^ p, [ref[pl.ds(0, rows), :].astype(F32) for ref in ins])
            for t in range(3):
                at = t * model + p * part
                qkv_out[:, at : at + part] = block[:, t * part : (t + 1) * part]
            proj_out[:, p * part : (p + 1) * part] = block[:, 3 * part :]
        cut = lambda v: choose(s_here, [v[:, s * rows : (s + 1) * rows] for s in range(shards)])
        low = [cut(ref[pl.ds(full, 16), :].astype(F32)) for ref in ins]
        sums = low[0] + low[1] + low[2] + low[3]
        gains_out[...] = sums[:2]
        shifts_out[...] = sums[2:8]
        bias = jnp.concatenate([choose(j ^ p, [v[8:9] for v in low]) for p in range(4)], axis=1)
        bias_out[...] = bias.reshape(bias_out.shape)

    shapes = [
        ((rows, 3 * model), F32),
        ((rows, model), F32),
        ((2, rows), F32),
        ((6, rows), F32),
        ((4 * rows,), F32),
    ]
    return run(kernel, shapes, links.scalars, parts)


def local(tokens, out_grad, lengths, gains, shifts, w_qkv, w_proj, w_fc, bias_fc, w_fc2):
    links = Links()
    line, shards = links.line, links.shards
    z, c, j = links.z, links.c, links.j
    slots, model = tokens.shape
    count = lengths.shape[1]
    rows = w_proj.shape[0]
    quarter = w_fc2.shape[0] // 4
    assert quarter == rows and w_fc.shape[1] == 4 * model
    heads = model // HEAD_DIM // 4
    part = heads * HEAD_DIM
    full_rows = -(-rows // 16) * 16

    attn_block = pack_attn(links, [gains, shifts, bias_fc, w_qkv, w_proj], rows, part, full_rows)
    sent = pack_slots(links, tie(tokens, attn_block), lengths)
    w_fc, w_fc2 = tie((w_fc, w_fc2), sent)
    ff_block = pack_ff(links, w_fc, w_fc2, rows, full_rows)

    attn_mine = line_gather(links, attn_block)
    got = links.rep_gather(sent)
    attn_mine, got, ff_block = lax.optimization_barrier((attn_mine, got, ff_block))
    attn_blocks = with_partners(links, attn_mine)
    ff_mine = line_gather(links, ff_block, links.line - 1)

    proj_mine, proj_other = proj_lanes(links, attn_blocks, out_grad, rows, part)
    proj = links.rep_gather(proj_mine)
    attn_blocks = tie(attn_blocks, proj_mine)
    weights, normed_one, qkv, probs, sent, small_f = attn_forward(
        links, got, attn_blocks, slots, heads, count, rows
    )
    ff_mine.append(links.along(tie(ff_block, sent), line - 1))
    attended = lax.all_gather(sent, "rep", axis=0)
    proj, ff_mine = tie((proj, ff_mine), attended)
    proj = proj + [proj_other] + [links.core(v) for v in proj[1:]]
    ff_blocks = with_partners(links, ff_mine)
    (
        attended,
        middle,
        normed_two,
        active,
        grad_hidden,
        cot,
        own,
        sent_x,
        sent_y,
        sent_d,
        bias_sums,
        proj,
        fc2,
    ) = ff_both(links, got, attended, proj, ff_blocks, small_f, slots, count, rows)
    received = [links.rep(v, k) for k, v in ((1, sent_x), (2, sent_y), (3, sent_d))]
    ff_mine, ff_other, branch, sent_x, sent_y, sent_d = ff_grads(
        links, normed_two, active, grad_hidden, cot, fc2, slots, rows
    )
    branch_sent = [sent_x, sent_y, sent_d]
    ff_other = tie(ff_other, received)
    ff_theirs = links.core(ff_other)
    ff_sent, ff_own = line_sum(line, ff_mine, ff_theirs)
    grad_middle, grad_branch, sums = middle_back(
        links, own, received, middle, got[0], out_grad, small_f, slots, count
    )
    grad_branch = lax.all_gather(grad_branch, "rep", axis=0)
    branch_got = [links.rep(v, k) for k, v in enumerate(branch_sent, start=1)]
    grad_branch = tie(grad_branch, branch_got)
    ff_sum = line_send(links, ff_sent, ff_own)

    attn_mine, attn_other, own, sent_x, sent_y, sent_d = attn_back(
        links,
        grad_branch,
        got,
        proj,
        weights,
        normed_one,
        qkv,
        probs,
        attended,
        sums,
        bias_sums,
        slots,
        rows,
    )
    attn_other = tie(attn_other, ff_sum)
    attn_theirs = links.core(attn_other)
    attn_sent, attn_own = line_sum(line, attn_mine, attn_theirs)
    attn_sent = tie(attn_sent, ff_sum)
    attn_sum = line_send(links, attn_sent, attn_own)

    own_sent = [sent_x, sent_y, sent_d]
    own_got = []
    for k in range(1, 4):
        own_got.append(links.rep(own_sent[k - 1], k))
        own = own + own_got[-1].astype(F32)
        branch = branch + branch_got[k - 1].astype(F32)
    live = (jnp.arange(slots) < jnp.sum(lengths)).astype(F32)[:, None]
    mixed_out = ((middle + branch + small_f[7]) * live).astype(LOW)
    unit_rows, scale = unit(tokens.astype(F32))
    grad_tokens = grad_middle + norm_back(own, small_f[0], unit_rows, scale)

    fc_out, fc2_out = ff_results(links, links.rep_gather(tie(ff_sum.astype(LOW), own_got)), rows)
    qkv_out, proj_out, gains_out, shifts_out, bias_out = attn_results(
        links, links.rep_gather(attn_sum.astype(LOW)), rows
    )
    return (
        mixed_out,
        grad_tokens,
        gains_out,
        shifts_out,
        qkv_out,
        proj_out,
        fc_out,
        bias_out,
        fc2_out,
    )


def solution(mesh):
    return jax.shard_map(
        local,
        mesh=mesh,
        in_specs=(
            P(("rep", "shard"), None),
            P(("rep", "shard"), None),
            P(("rep", "shard"), None),
            P(None, "shard"),
            P(None, "shard"),
            P("shard", None),
            P("shard", None),
            P("shard", None),
            P("shard"),
            P("shard", None),
        ),
        out_specs=(
            P(("rep", "shard"), None),
            P(("rep", "shard"), None),
            P(None, "shard"),
            P(None, "shard"),
            P("shard", None),
            P("shard", None),
            P("shard", None),
            P("shard"),
            P("shard", None),
        ),
        check_vma=False,
    )
```

time: 185 us -> 169 us (0.914)
  waiting for transfers between devices: 33.5 us -> 28 us
  starting transfers between devices: 54.6 us -> 49.2 us
  Pallas kernels: 52.1 us -> 49.7 us
    ppermute x12, waiting for transfers between devices: 22.1 us -> 12.5 us  [along(): return lax.ppermute(v, 'shard', [(i, (i + 2 * hop) % n) for i in range(n)])]
    ppermute x12, starting transfers between devices: 26.4 us -> 21.9 us  [along(): return lax.ppermute(v, 'shard', [(i, (i + 2 * hop) % n) for i in range(n)])]
    pallas_call x10 -> x11, Pallas kernels: 52.1 us -> 49.7 us  [run(): pl.pallas_call(kernel, out_shape=[jax.ShapeDtypeStruct(shape, dtype) for...]
    ppermute x10 -> x13, waiting for transfers between devices: 2.02 us -> 4.09 us  [core(): return lax.ppermute(v, 'shard', [(i, i ^ 1) for i in range(self.shards)])]
    ppermute x21, waiting for transfers between devices: 9.45 us -> 11.3 us  [rep(): return lax.ppermute(v, 'rep', [(i, i ^ k) for i in range(4)])]
    unnamed x98 -> x90, local copies, waits for them, and re-layouts: 5.21 us -> 4.9 us
  transfers between devices with their start and end apart: 43 -> 46, of which waited for: 10 -> 16; matrix products, arithmetic and copies ran while one was open for 3% -> 4% of each run, Pallas kernels for 20% -> 21%
where the time goes in v1:
time: 169 us; the launch traced here: 168 us
  Pallas kernels  49.7 us (29%)
  starting transfers between devices  49.2 us (29%)
  waiting for transfers between devices  28 us (17%)
  blocking collectives  26.2 us (16%)
  other arithmetic  8.11 us (5%)
  local copies, waits for them, and re-layouts  5.74 us (3%)
    pallas_call x11, Pallas kernels, run(): pl.pallas_call(kernel, out_shape=[jax.ShapeDtypeStruct(shape, dtype) for...  49.7 us
    ppermute x21, starting transfers between devices, rep(): return lax.ppermute(v, 'rep', [(i, i ^ k) for i in range(4)])  24.7 us
    ppermute x12, starting transfers between devices, along(): return lax.ppermute(v, 'shard', [(i, (i + 2 * hop) % n) for i in range(n)])  21.9 us
    all_gather x1, blocking collectives, local(): attended = lax.all_gather(sent, 'rep', axis=0)  14.1 us
    ppermute x12, waiting for transfers between devices, along(): return lax.ppermute(v, 'shard', [(i, (i + 2 * hop) % n) for i in range(n)])  12.5 us
    all_gather x1, blocking collectives, local(): grad_branch = lax.all_gather(grad_branch, 'rep', axis=0)  12 us
    ppermute x21, waiting for transfers between devices, rep(): return lax.ppermute(v, 'rep', [(i, i ^ k) for i in range(4)])  11.3 us
    unnamed x90, local copies, waits for them, and re-layouts  4.9 us
  transfers between devices with their start and end apart: 46, of which 16 were waited for; matrix products, arithmetic and copies ran while one was open for 4% of the time, Pallas kernels for 21%

profile of v1, /device:TPU:0, one launch (start us, length us, event | category | flops | bytes accessed | tf_op | source)
XLA Modules:
  0.0 168.1 jit_solution(12725945689802853595)
XLA Ops:
  1.3 2.1 %shard_map.169.refs_0_.refs_4_ = bf16[112,768]{1,0:T(8,128)(2,1)} custom-call(s32[4]{0:T(128)} %pad_add_fusion.scalar_ref, bf16[2,96]{1,0:T(2,128)(2,1)} %gain.1, bf16[6,96]{1,0:T(8,128)(2,1)} %shift.1, bf16[384]{0:T(512)(128)(2,1)} %bias_ref.1, bf16[96,2304]{1,0:T(8,128)(2,1)} %qkv_ref.1, bf16[96,768]{1,0:T(8,128)(2,1)} %p_ref.1), custom_call_target="tpu_custom_call" | custom-call | flops 1 | bytes 1 | tf_op jit(solution)/shard_map/pallas_call | solution.py:69
  3.4 3.0 %collective-permute-start = (bf16[112,768]{1,0:T(8,128)(2,1)}, bf16[112,768]{1,0:T(8,128)(2,1)S(1)}, u32[]{:S(2)}, u32[]{:S(2)}) collective-permute-start(bf16[112,768]{1,0:T(8,128)(2,1)} %shard_map.169.refs_0_.refs_4_), channel_id=1, source_target_pairs={{0,2},{1,3},{2,4},{3,5},{4,6},{5,7},{6,0},{7,1},{8,10},{9,11},{10,... | collective-permute-start | bytes 516104 | tf_op jit(solution)/shard_map/ppermute | solution.py:55
  11.6 2.6 %collective-permute-start.1 = (bf16[112,768]{1,0:T(8,128)(2,1)}, bf16[112,768]{1,0:T(8,128)(2,1)S(1)}, u32[]{:S(2)}, u32[]{:S(2)}) collective-permute-start(bf16[112,768]{1,0:T(8,128)(2,1)} %shard_map.169.refs_0_.refs_4_), channel_id=1, source_target_pairs={{0,4},{1,5},{2,6},{3,7},{4,0},{5,1},{6,2},{7,3},{8,12},{9,13},{10,... | collective-permute-start | bytes 516104 | tf_op jit(solution)/shard_map/ppermute | solution.py:55
  15.5 2.8 %shard_map.171.refs_13_ = bf16[192,768]{1,0:T(8,128)(2,1)} custom-call(s32[4]{0:T(128)} %pad_add_fusion.scalar_ref, bf16[96,3072]{1,0:T(8,128)(2,1)} %fc_ref, bf16[384,768]{1,0:T(8,128)(2,1)} %fc2_ref), custom_call_target="tpu_custom_call" | custom-call | flops 1 | bytes 1 | tf_op jit(solution)/shard_map/pallas_call | solution.py:69
  18.3 4.3 %collective-permute-done.1.refs_2_.refs_6_ = bf16[112,768]{1,0:T(8,128)(2,1)S(1)} collective-permute-done((bf16[112,768]{1,0:T(8,128)(2,1)}, bf16[112,768]{1,0:T(8,128)(2,1)S(1)}, u32[]{:S(2)}, u32[]{:S(2)}) %collective-permute-start.1) | collective-permute-done | bytes 172064 | tf_op jit(solution)/shard_map/ppermute | solution.py:55
  22.6 3.1 %collective-permute-start.13 = (bf16[192,768]{1,0:T(8,128)(2,1)}, bf16[192,768]{1,0:T(8,128)(2,1)S(1)}, u32[]{:S(2)}, u32[]{:S(2)}) collective-permute-start(bf16[192,768]{1,0:T(8,128)(2,1)} %shard_map.171.refs_13_), channel_id=1, source_target_pairs={{0,2},{1,3},{2,4},{3,5},{4,6},{5,7},{6,0},{7,1},{8,10},{9,11},{10,... | collective-permute-start | bytes 884744 | tf_op jit(solution)/shard_map/ppermute | solution.py:55
  29.0 2.4 %shard_map.172 = (bf16[224,768]{1,0:T(8,128)(2,1)}, bf16[96,768]{1,0:T(8,128)(2,1)}) custom-call(s32[4]{0:T(128)} %pad_add_fusion.scalar_ref, bf16[112,768]{1,0:T(8,128)(2,1)} %shard_map.169.refs_0_.refs_4_, bf16[112,768]{1,0:T(8,128)(2,1)} %copy-done.10, bf16[112,768]{1,0:T(8,128)(2,1)} %copy-done.11, bf16[112,768]{1,0:T(8,128)(2,1)} %copy-done.12, ...), custom_call_target="tpu_custom_call" | custom-call | flops 1 | bytes 1 | tf_op jit(solution)/shard_map/pallas_call | solution.py:69
  34.8 2.4 %collective-permute-start.14 = (bf16[192,768]{1,0:T(8,128)(2,1)S(1)}, bf16[192,768]{1,0:T(8,128)(2,1)S(1)}, u32[]{:S(2)}, u32[]{:S(2)}) collective-permute-start(bf16[192,768]{1,0:T(8,128)(2,1)S(1)} %copy-done.7), channel_id=1, source_target_pairs={{0,4},{1,5},{2,6},{3,7},{4,0},{5,1},{6,2},{7,3},{8,12},{9,13},{10,... | collective-permute-start | bytes 884744 | tf_op jit(solution)/shard_map/ppermute | solution.py:55
  37.2 7.1 %shard_map.173 = (bf16[768,768]{1,0:T(8,128)(2,1)}, bf16[512,768]{1,0:T(8,128)(2,1)}, bf16[512,576]{1,0:T(8,128)(2,1)}, f32[4,3,128,128]{3,2,1,0:T(8,128)}, bf16[128,768]{1,0:T(8,128)(2,1)}, /*index=5*/f32[16,768]{1,0:T(8,128)}) custom-call(s32[4]{0:T(128)} %pad_add_fusion.scalar_ref, bf16[144,768]{1,0:T(8,128)(2,1)} %shard_map.170.refs_0_.got_ref.refs_1_, ...), custom_call_target="tpu_custom_call" | custom-call | flops 1 | bytes 1 | tf_op jit(solution)/shard_map/pallas_call | solution.py:69
  44.4 14.1 %all-gather = bf16[512,768]{1,0:T(8,128)(2,1)} all-gather(bf16[128,768]{1,0:T(8,128)(2,1)} %get-tuple-element.108), channel_id=2, replica_groups=mesh['rep'=4,'shard'=8] {'rep'}, dimensions={0}, use_global_device_ids=true | all-gather | bytes 983040 | tf_op jit(solution)/shard_map/all_gather | solution.py:645
  64.1 8.9 %shard_map.174 = (bf16[512,768]{1,0:T(8,128)(2,1)}, f32[128,768]{1,0:T(8,128)}, bf16[512,768]{1,0:T(8,128)(2,1)}, bf16[512,768]{1,0:T(8,128)(2,1)}, bf16[512,768...) custom-call(s32[4]{0:T(128)} %pad_add_fusion.scalar_ref, ...), custom_call_target="tpu_custom_call" | custom-call | flops 1 | bytes 1 | tf_op jit(solution)/shard_map/pallas_call | solution.py:69
  76.6 5.8 %shard_map.175 = (bf16[768,768]{1,0:T(8,128)(2,1)}, bf16[768,768]{1,0:T(8,128)(2,1)}, f32[128,768]{1,0:T(8,128)}, bf16[128,768]{1,0:T(8,128)(2,1)}, bf16[128,768]{1,0:T(8,128)(2,1)}, /*index=5*/bf16[128,768]{1,0:T(8,128)(2,1)}) custom-call(s32[4]{0:T(128)} %pad_add_fusion.scalar_ref, bf16[512,768]{1,0:T(8,128)(2,1)} %get-tuple-element.122.refs_0_, ...), custom_call_target="tpu_custom_call" | custom-call | flops 1 | bytes 1 | tf_op jit(solution)/shard_map/pallas_call | solution.py:69
  82.4 2.9 %collective-permute-done.27.r2 = bf16[128,768]{1,0:T(8,128)(2,1)S(1)} collective-permute-done((bf16[128,768]{1,0:T(8,128)(2,1)}, bf16[128,768]{1,0:T(8,128)(2,1)S(1)}, u32[]{:S(2)}, u32[]{:S(2)}) %collective-permute-start.27) | collective-permute-done | bytes 196640 | tf_op jit(solution)/shard_map/ppermute | solution.py:58
  90.9 2.6 %collective-permute-start.34 = (bf16[192,768]{1,0:T(8,128)(2,1)S(1)}, bf16[192,768]{1,0:T(8,128)(2,1)S(1)}, u32[]{:S(2)}, u32[]{:S(2)}) collective-permute-start(bf16[192,768]{1,0:T(8,128)(2,1)S(1)} %get-tuple-element.174), channel_id=1, source_target_pairs={{0,4},{1,5},{2,6},{3,7},{4,0},{5,1},{6,2},{7,3},{8,12},{9,13},{10,... | collective-permute-start | bytes 884744 | tf_op jit(solution)/shard_map/ppermute | solution.py:55
  93.7 2.7 %collective-permute-start.35 = (bf16[192,768]{1,0:T(8,128)(2,1)S(1)}, bf16[192,768]{1,0:T(8,128)(2,1)S(1)}, u32[]{:S(2)}, u32[]{:S(2)}) collective-permute-start(bf16[192,768]{1,0:T(8,128)(2,1)S(1)} %get-tuple-element.173), channel_id=1, source_target_pairs={{0,6},{1,7},{2,0},{3,1},{4,2},{5,3},{6,4},{7,5},{8,14},{9,15},{10,... | collective-permute-start | bytes 884744 | tf_op jit(solution)/shard_map/ppermute | solution.py:55
  97.0 2.8 %shard_map.176 = (f32[128,768]{1,0:T(8,128)}, bf16[128,768]{1,0:T(8,128)(2,1)}, f32[4,768]{1,0:T(4,128)}) custom-call(s32[4]{0:T(128)} %pad_add_fusion.scalar_ref, f32[128,768]{1,0:T(8,128)} %get-tuple-element.131.own_ref, bf16[128,768]{1,0:T(8,128)(2,1)} %copy-done.36, bf16[128,768]{1,0:T(8,128)(2,1)} %copy-done.37, bf16[128,768]{1,0:T(8,128)(2,1)} %copy-done.38, ...), custom_call_target="tpu_custom_call" | custom-call | flops 1 | bytes 1 | tf_op jit(solution)/shard_map/pallas_call | solution.py:69
  99.8 12.0 %all-gather.1 = bf16[512,768]{1,0:T(8,128)(2,1)} all-gather(bf16[128,768]{1,0:T(8,128)(2,1)} %get-tuple-element.136), channel_id=3, replica_groups=mesh['rep'=4,'shard'=8] {'rep'}, dimensions={0}, use_global_device_ids=true | all-gather | bytes 983040 | tf_op jit(solution)/shard_map/all_gather | solution.py:675
  111.8 10.4 %shard_map.177 = (bf16[448,768]{1,0:T(8,128)(2,1)}, bf16[448,768]{1,0:T(8,128)(2,1)}, f32[128,768]{1,0:T(8,128)}, bf16[128,768]{1,0:T(8,128)(2,1)}, bf16[128,768]{1,0:T(8,128)(2,1)}, /*index=5*/bf16[128,768]{1,0:T(8,128)(2,1)}) custom-call(s32[4]{0:T(128)} %pad_add_fusion.scalar_ref, bf16[4,128,768]{2,1,0:T(8,128)(2,1)} %bitcast.6, ...), custom_call_target="tpu_custom_call" | custom-call | flops 1 | bytes 1 | tf_op jit(solution)/shard_map/pallas_call | solution.py:69
  130.6 2.7 %collective-permute-done.29 = bf16[128,768]{1,0:T(8,128)(2,1)S(1)} collective-permute-done((bf16[128,768]{1,0:T(8,128)(2,1)}, bf16[128,768]{1,0:T(8,128)(2,1)S(1)}, u32[]{:S(2)}, u32[]{:S(2)}) %collective-permute-start.29) | collective-permute-done | bytes 196640 | tf_op jit(solution)/shard_map/ppermute | solution.py:58
  133.3 4.5 %collective-permute-done.30 = bf16[128,768]{1,0:T(8,128)(2,1)S(1)} collective-permute-done((bf16[128,768]{1,0:T(8,128)(2,1)}, bf16[128,768]{1,0:T(8,128)(2,1)S(1)}, u32[]{:S(2)}, u32[]{:S(2)}) %collective-permute-start.30) | collective-permute-done | bytes 196640 | tf_op jit(solution)/shard_map/ppermute | solution.py:58
  144.1 4.2 %collective-permute-done.37 = bf16[112,768]{1,0:T(8,128)(2,1)S(1)} collective-permute-done((bf16[112,768]{1,0:T(8,128)(2,1)S(1)}, bf16[112,768]{1,0:T(8,128)(2,1)S(1)}, u32[]{:S(2)}, u32[]{:S(2)}) %collective-permute-start.37) | collective-permute-done | bytes 172064 | tf_op jit(solution)/shard_map/ppermute | solution.py:55
  149.8 4.0 %collective-permute-done.38 = bf16[112,768]{1,0:T(8,128)(2,1)S(1)} collective-permute-done((bf16[112,768]{1,0:T(8,128)(2,1)S(1)}, bf16[112,768]{1,0:T(8,128)(2,1)S(1)}, u32[]{:S(2)}, u32[]{:S(2)}) %collective-permute-start.38) | collective-permute-done | bytes 172064 | tf_op jit(solution)/shard_map/ppermute | solution.py:55
  159.9 3.1 %shard_map.179 = (f32[96,3072]{1,0:T(8,128)}, f32[384,768]{1,0:T(8,128)}) custom-call(s32[4]{0:T(128)} %pad_add_fusion.scalar_ref, bf16[192,768]{1,0:T(8,128)(2,1)} %copy-done.6, bf16[192,768]{1,0:T(8,128)(2,1)} %copy-done.26, bf16[192,768]{1,0:T(8,128)(2,1)} %copy-done.27, bf16[192,768]{1,0:T(8,128)(2,1)} %copy-done.28), custom_call_target="tpu_custom_call" | custom-call | flops 1 | bytes 1 | tf_op jit(solution)/shard_map/pallas_call | solution.py:69
  165.4 2.7 %shard_map.178 = (f32[96,2304]{1,0:T(8,128)}, f32[96,768]{1,0:T(8,128)}, f32[2,96]{1,0:T(2,128)}, f32[6,96]{1,0:T(8,128)}, f32[384]{0:T(512)}) custom-call(s32[4]{0:T(128)} %pad_add_fusion.scalar_ref, bf16[112,768]{1,0:T(8,128)(2,1)} %copy-done.9, bf16[112,768]{1,0:T(8,128)(2,1)} %copy-done.39, bf16[112,768]{1,0:T(8,128)(2,1)} %copy-done.40, ...), custom_call_target="tpu_custom_call" | custom-call | flops 1 | bytes 1 | tf_op jit(solution)/shard_map/pallas_call | solution.py:69
  (187 shorter events, 53.8 us)
Async XLA Ops:
  3.4 10.7 %collective-permute-start = (bf16[112,768]{1,0:T(8,128)(2,1)}, bf16[112,768]{1,0:T(8,128)(2,1)S(1)}, u32[]{:S(2)}, u32[]{:S(2)}) collective-permute-start(bf16[112,768]{1,0:T(8,128)(2,1)} %shard_map.169.refs_0_.refs_4_), channel_id=1, source_target_pairs={{0,2},{1,3},{2,4},{3,5},{4,6},{5,7},{6,0},{7,1},{8,10},{9,11},{10,... | collective-permute-start | bytes 516104 | tf_op jit(solution)/shard_map/ppermute | solution.py:55
  8.1 14.5 %collective-permute-start.3 = (bf16[144,768]{1,0:T(8,128)(2,1)}, bf16[144,768]{1,0:T(8,128)(2,1)S(1)}, u32[]{:S(2)}, u32[]{:S(2)}) collective-permute-start(bf16[144,768]{1,0:T(8,128)(2,1)} %shard_map.170.refs_0_.got_ref.refs_1_), channel_id=1, source_target_pairs={{0,8},{8,0},{16,24},{24,16},{1,9},{9,1},{17,25},{25,17},{2,10},{10... | collective-permute-start | bytes 663560 | tf_op jit(solution)/shard_map/ppermute | solution.py:58
  9.6 13.0 %collective-permute-start.4 = (bf16[144,768]{1,0:T(8,128)(2,1)}, bf16[144,768]{1,0:T(8,128)(2,1)S(1)}, u32[]{:S(2)}, u32[]{:S(2)}) collective-permute-start(bf16[144,768]{1,0:T(8,128)(2,1)} %shard_map.170.refs_0_.got_ref.refs_1_), channel_id=1, source_target_pairs={{0,16},{8,24},{16,0},{24,8},{1,17},{9,25},{17,1},{25,9},{2,18},{10... | collective-permute-start | bytes 663560 | tf_op jit(solution)/shard_map/ppermute | solution.py:58
  11.1 11.5 %collective-permute-start.5 = (bf16[144,768]{1,0:T(8,128)(2,1)}, bf16[144,768]{1,0:T(8,128)(2,1)S(1)}, u32[]{:S(2)}, u32[]{:S(2)}) collective-permute-start(bf16[144,768]{1,0:T(8,128)(2,1)} %shard_map.170.refs_0_.got_ref.refs_1_), channel_id=1, source_target_pairs={{0,24},{8,16},{16,8},{24,0},{1,25},{9,17},{17,9},{25,1},{2,26},{10... | collective-permute-start | bytes 663560 | tf_op jit(solution)/shard_map/ppermute | solution.py:58
  11.6 11.0 %collective-permute-start.1 = (bf16[112,768]{1,0:T(8,128)(2,1)}, bf16[112,768]{1,0:T(8,128)(2,1)S(1)}, u32[]{:S(2)}, u32[]{:S(2)}) collective-permute-start(bf16[112,768]{1,0:T(8,128)(2,1)} %shard_map.169.refs_0_.refs_4_), channel_id=1, source_target_pairs={{0,4},{1,5},{2,6},{3,7},{4,0},{5,1},{6,2},{7,3},{8,12},{9,13},{10,... | collective-permute-start | bytes 516104 | tf_op jit(solution)/shard_map/ppermute | solution.py:55
  22.6 21.7 %collective-permute-start.13 = (bf16[192,768]{1,0:T(8,128)(2,1)}, bf16[192,768]{1,0:T(8,128)(2,1)S(1)}, u32[]{:S(2)}, u32[]{:S(2)}) collective-permute-start(bf16[192,768]{1,0:T(8,128)(2,1)} %shard_map.171.refs_13_), channel_id=1, source_target_pairs={{0,2},{1,3},{2,4},{3,5},{4,6},{5,7},{6,0},{7,1},{8,10},{9,11},{10,... | collective-permute-start | bytes 884744 | tf_op jit(solution)/shard_map/ppermute | solution.py:55
  31.3 27.3 %collective-permute-start.10 = (bf16[224,768]{1,0:T(8,128)(2,1)}, bf16[224,768]{1,0:T(8,128)(2,1)S(1)}, u32[]{:S(2)}, u32[]{:S(2)}) collective-permute-start(bf16[224,768]{1,0:T(8,128)(2,1)} %get-tuple-element.111.refs_5_), channel_id=1, source_target_pairs={{0,8},{8,0},{16,24},{24,16},{1,9},{9,1},{17,25},{25,17},{2,10},{10... | collective-permute-start | bytes 1032200 | tf_op jit(solution)/shard_map/ppermute | solution.py:58
  32.8 25.8 %collective-permute-start.11 = (bf16[224,768]{1,0:T(8,128)(2,1)}, bf16[224,768]{1,0:T(8,128)(2,1)S(1)}, u32[]{:S(2)}, u32[]{:S(2)}) collective-permute-start(bf16[224,768]{1,0:T(8,128)(2,1)} %get-tuple-element.111.refs_5_), channel_id=1, source_target_pairs={{0,16},{8,24},{16,0},{24,8},{1,17},{9,25},{17,1},{25,9},{2,18},{10... | collective-permute-start | bytes 1032200 | tf_op jit(solution)/shard_map/ppermute | solution.py:58
  34.4 24.3 %collective-permute-start.12 = (bf16[224,768]{1,0:T(8,128)(2,1)}, bf16[224,768]{1,0:T(8,128)(2,1)S(1)}, u32[]{:S(2)}, u32[]{:S(2)}) collective-permute-start(bf16[224,768]{1,0:T(8,128)(2,1)} %get-tuple-element.111.refs_5_), channel_id=1, source_target_pairs={{0,24},{8,16},{16,8},{24,0},{1,25},{9,17},{17,9},{25,1},{2,26},{10... | collective-permute-start | bytes 1032200 | tf_op jit(solution)/shard_map/ppermute | solution.py:58
  34.8 23.7 %collective-permute-start.14 = (bf16[192,768]{1,0:T(8,128)(2,1)S(1)}, bf16[192,768]{1,0:T(8,128)(2,1)S(1)}, u32[]{:S(2)}, u32[]{:S(2)}) collective-permute-start(bf16[192,768]{1,0:T(8,128)(2,1)S(1)} %copy-done.7), channel_id=1, source_target_pairs={{0,4},{1,5},{2,6},{3,7},{4,0},{5,1},{6,2},{7,3},{8,12},{9,13},{10,... | collective-permute-start | bytes 884744 | tf_op jit(solution)/shard_map/ppermute | solution.py:55
  44.3 14.3 %collective-permute-start.15 = (bf16[192,768]{1,0:T(8,128)(2,1)S(1)}, bf16[192,768]{1,0:T(8,128)(2,1)S(1)}, u32[]{:S(2)}, u32[]{:S(2)}) collective-permute-start(bf16[192,768]{1,0:T(8,128)(2,1)S(1)} %copy-done.7), channel_id=1, source_target_pairs={{0,6},{1,7},{2,0},{3,1},{4,2},{5,3},{6,4},{7,5},{8,14},{9,15},{10,... | collective-permute-start | bytes 884744 | tf_op jit(solution)/shard_map/ppermute | solution.py:55
  74.2 11.1 %collective-permute-start.27 = (bf16[128,768]{1,0:T(8,128)(2,1)}, bf16[128,768]{1,0:T(8,128)(2,1)S(1)}, u32[]{:S(2)}, u32[]{:S(2)}) collective-permute-start(bf16[128,768]{1,0:T(8,128)(2,1)} %get-tuple-element.133), channel_id=1, source_target_pairs={{0,16},{8,24},{16,0},{24,8},{1,17},{9,25},{17,1},{25,9},{2,18},{10... | collective-permute-start | bytes 589832 | tf_op jit(solution)/shard_map/ppermute | solution.py:58
  86.7 25.1 %collective-permute-start.24 = (bf16[128,768]{1,0:T(8,128)(2,1)}, bf16[128,768]{1,0:T(8,128)(2,1)S(1)}, u32[]{:S(2)}, u32[]{:S(2)}) collective-permute-start(bf16[128,768]{1,0:T(8,128)(2,1)} %get-tuple-element.129), channel_id=1, source_target_pairs={{0,16},{8,24},{16,0},{24,8},{1,17},{9,25},{17,1},{25,9},{2,18},{10... | collective-permute-start | bytes 589832 | tf_op jit(solution)/shard_map/ppermute | solution.py:58
  87.8 24.0 %collective-permute-start.25 = (bf16[128,768]{1,0:T(8,128)(2,1)}, bf16[128,768]{1,0:T(8,128)(2,1)}, u32[]{:S(2)}, u32[]{:S(2)}) collective-permute-start(bf16[128,768]{1,0:T(8,128)(2,1)} %get-tuple-element.130), channel_id=1, source_target_pairs={{0,24},{8,16},{16,8},{24,0},{1,25},{9,17},{17,9},{25,1},{2,26},{10... | collective-permute-start | bytes 589832 | tf_op jit(solution)/shard_map/ppermute | solution.py:58
  90.6 31.6 %collective-permute-start.33 = (bf16[192,768]{1,0:T(8,128)(2,1)S(1)}, bf16[192,768]{1,0:T(8,128)(2,1)S(1)}, u32[]{:S(2)}, u32[]{:S(2)}) collective-permute-start(bf16[192,768]{1,0:T(8,128)(2,1)S(1)} %get-tuple-element.172), channel_id=1, source_target_pairs={{0,2},{1,3},{2,4},{3,5},{4,6},{5,7},{6,0},{7,1},{8,10},{9,11},{10,... | collective-permute-start | bytes 884744 | tf_op jit(solution)/shard_map/ppermute | solution.py:55
  90.9 31.3 %collective-permute-start.34 = (bf16[192,768]{1,0:T(8,128)(2,1)S(1)}, bf16[192,768]{1,0:T(8,128)(2,1)S(1)}, u32[]{:S(2)}, u32[]{:S(2)}) collective-permute-start(bf16[192,768]{1,0:T(8,128)(2,1)S(1)} %get-tuple-element.174), channel_id=1, source_target_pairs={{0,4},{1,5},{2,6},{3,7},{4,0},{5,1},{6,2},{7,3},{8,12},{9,13},{10,... | collective-permute-start | bytes 884744 | tf_op jit(solution)/shard_map/ppermute | solution.py:55
  93.7 28.6 %collective-permute-start.35 = (bf16[192,768]{1,0:T(8,128)(2,1)S(1)}, bf16[192,768]{1,0:T(8,128)(2,1)S(1)}, u32[]{:S(2)}, u32[]{:S(2)}) collective-permute-start(bf16[192,768]{1,0:T(8,128)(2,1)S(1)} %get-tuple-element.173), channel_id=1, source_target_pairs={{0,6},{1,7},{2,0},{3,1},{4,2},{5,3},{6,4},{7,5},{8,14},{9,15},{10,... | collective-permute-start | bytes 884744 | tf_op jit(solution)/shard_map/ppermute | solution.py:55
  123.6 15.4 %collective-permute-start.36 = (bf16[448,768]{1,0:T(8,128)(2,1)S(1)}, bf16[448,768]{1,0:T(8,128)(2,1)S(1)}, u32[]{:S(2)}, u32[]{:S(2)}) collective-permute-start(bf16[448,768]{1,0:T(8,128)(2,1)S(1)} %copy-done.43), channel_id=1, source_target_pairs={{0,1},{1,0},{2,3},{3,2},{4,5},{5,4},{6,7},{7,6},{8,9},{9,8},{10,11... | collective-permute-start | bytes 2064392 | tf_op jit(solution)/shard_map/ppermute | solution.py:51
  126.4 11.3 %collective-permute-start.30 = (bf16[128,768]{1,0:T(8,128)(2,1)}, bf16[128,768]{1,0:T(8,128)(2,1)S(1)}, u32[]{:S(2)}, u32[]{:S(2)}) collective-permute-start(bf16[128,768]{1,0:T(8,128)(2,1)} %get-tuple-element.148), channel_id=1, source_target_pairs={{0,16},{8,24},{16,0},{24,8},{1,17},{9,25},{17,1},{25,9},{2,18},{10... | collective-permute-start | bytes 589832 | tf_op jit(solution)/shard_map/ppermute | solution.py:58
  127.4 10.4 %collective-permute-start.31 = (bf16[128,768]{1,0:T(8,128)(2,1)S(1)}, bf16[128,768]{1,0:T(8,128)(2,1)S(1)}, u32[]{:S(2)}, u32[]{:S(2)}) collective-permute-start(bf16[128,768]{1,0:T(8,128)(2,1)S(1)} %copy-done.44), channel_id=1, source_target_pairs={{0,24},{8,16},{16,8},{24,0},{1,25},{9,17},{17,9},{25,1},{2,26},{10... | collective-permute-start | bytes 589832 | tf_op jit(solution)/shard_map/ppermute | solution.py:58
  138.0 18.0 %collective-permute-start.43 = (bf16[192,768]{1,0:T(8,128)(2,1)S(1)}, bf16[192,768]{1,0:T(8,128)(2,1)S(1)}, u32[]{:S(2)}, u32[]{:S(2)}) collective-permute-start(bf16[192,768]{1,0:T(8,128)(2,1)S(1)} %convert_add_fusion.refs_0_), channel_id=1, source_target_pairs={{0,8},{8,0},{16,24},{24,16},{1,9},{9,1},{17,25},{25,17},{2,10},{10... | collective-permute-start | bytes 884744 | tf_op jit(solution)/shard_map/ppermute | solution.py:58
  139.2 14.6 %collective-permute-start.38 = (bf16[112,768]{1,0:T(8,128)(2,1)S(1)}, bf16[112,768]{1,0:T(8,128)(2,1)S(1)}, u32[]{:S(2)}, u32[]{:S(2)}) collective-permute-start(bf16[112,768]{1,0:T(8,128)(2,1)S(1)} %get-tuple-element.157), channel_id=1, source_target_pairs={{0,4},{1,5},{2,6},{3,7},{4,0},{5,1},{6,2},{7,3},{8,12},{9,13},{10,... | collective-permute-start | bytes 516104 | tf_op jit(solution)/shard_map/ppermute | solution.py:55
  141.2 12.6 %collective-permute-start.39 = (bf16[112,768]{1,0:T(8,128)(2,1)S(1)}, bf16[112,768]{1,0:T(8,128)(2,1)S(1)}, u32[]{:S(2)}, u32[]{:S(2)}) collective-permute-start(bf16[112,768]{1,0:T(8,128)(2,1)S(1)} %get-tuple-element.158), channel_id=1, source_target_pairs={{0,6},{1,7},{2,0},{3,1},{4,2},{5,3},{6,4},{7,5},{8,14},{9,15},{10,... | collective-permute-start | bytes 516104 | tf_op jit(solution)/shard_map/ppermute | solution.py:55
  143.0 15.5 %collective-permute-start.44 = (bf16[192,768]{1,0:T(8,128)(2,1)S(1)}, bf16[192,768]{1,0:T(8,128)(2,1)S(1)}, u32[]{:S(2)}, u32[]{:S(2)}) collective-permute-start(bf16[192,768]{1,0:T(8,128)(2,1)S(1)} %convert_add_fusion.refs_0_), channel_id=1, source_target_pairs={{0,16},{8,24},{16,0},{24,8},{1,17},{9,25},{17,1},{25,9},{2,18},{10... | collective-permute-start | bytes 884744 | tf_op jit(solution)/shard_map/ppermute | solution.py:58
  (67 other events, 415.2 us)

commit v2 on v1

--- a/solution.py
+++ b/solution.py
@@ -566,39 +566,39 @@
         ins, fc_out, fc2_out = refs[:4], refs[4], refs[5]
         j = scalar_ref[2]
         for p in range(4):
-            left = choose(j ^ p, [ref[pl.ds(0, rows), :].astype(F32) for ref in ins])
+            left = choose(j ^ p, [ref[pl.ds(0, rows), :] for ref in ins]).astype(F32)
             for s in range(shards):
                 at = (s * 4 + p) * rows
                 fc_out[:, at : at + rows] = left[:, s * rows : (s + 1) * rows]
             fc2_out[pl.ds(p * rows, rows), :] = choose(
-                j ^ p, [ref[pl.ds(full, rows), :].astype(F32) for ref in ins]
-            )
+                j ^ p, [ref[pl.ds(full, rows), :] for ref in ins]
+            ).astype(F32)
 
     shapes = [((rows, 4 * model), F32), ((4 * rows, model), F32)]
     return run(kernel, shapes, links.scalars, parts)
 
 
-def attn_results(links, parts, rows):
-    model = parts[0].shape[1]
+def attn_results(links, got, rows):
+    model = got.shape[2]
     shards = links.shards
     part = model // 4
     full = -(-rows // 16) * 16
 
     def kernel(scalar_ref, *refs):
-        ins, qkv_out, proj_out, gains_out, shifts_out, bias_out = refs[:4], *refs[4:]
-        j, s_here = scalar_ref[2], scalar_ref[3]
+        got_ref, qkv_out, proj_out, gains_out, shifts_out, bias_out = refs
+        s_here = scalar_ref[3]
         for p in range(4):
-            block = choose(j ^ p, [ref[pl.ds(0, rows), :].astype(F32) for ref in ins])
+            block = got_ref[p, pl.ds(0, rows), :].astype(F32)
             for t in range(3):
                 at = t * model + p * part
                 qkv_out[:, at : at + part] = block[:, t * part : (t + 1) * part]
             proj_out[:, p * part : (p + 1) * part] = block[:, 3 * part :]
         cut = lambda v: choose(s_here, [v[:, s * rows : (s + 1) * rows] for s in range(shards)])
-        low = [cut(ref[pl.ds(full, 16), :].astype(F32)) for ref in ins]
+        low = [cut(got_ref[p, pl.ds(full, 16), :].astype(F32)) for p in range(4)]
         sums = low[0] + low[1] + low[2] + low[3]
         gains_out[...] = sums[:2]
         shifts_out[...] = sums[2:8]
-        bias = jnp.concatenate([choose(j ^ p, [v[8:9] for v in low]) for p in range(4)], axis=1)
+        bias = jnp.concatenate([v[8:9] for v in low], axis=1)
         bias_out[...] = bias.reshape(bias_out.shape)
 
     shapes = [
@@ -608,7 +608,7 @@
         ((6, rows), F32),
         ((4 * rows,), F32),
     ]
-    return run(kernel, shapes, links.scalars, parts)
+    return run(kernel, shapes, links.scalars, [got])
 
 
 def local(tokens, out_grad, lengths, gains, shifts, w_qkv, w_proj, w_fc, bias_fc, w_fc2):
@@ -672,9 +672,9 @@
     grad_middle, grad_branch, sums = middle_back(
         links, own, received, middle, got[0], out_grad, small_f, slots, count
     )
-    grad_branch = lax.all_gather(grad_branch, "rep", axis=0)
     branch_got = [links.rep(v, k) for k, v in enumerate(branch_sent, start=1)]
     grad_branch = tie(grad_branch, branch_got)
+    grad_branch = lax.all_gather(grad_branch, "rep", axis=0)
     ff_sum = line_send(links, ff_sent, ff_own)
 
     attn_mine, attn_other, own, sent_x, sent_y, sent_d = attn_back(
@@ -711,7 +711,7 @@
 
     fc_out, fc2_out = ff_results(links, links.rep_gather(tie(ff_sum.astype(LOW), own_got)), rows)
     qkv_out, proj_out, gains_out, shifts_out, bias_out = attn_results(
-        links, links.rep_gather(attn_sum.astype(LOW)), rows
+        links, lax.all_gather(attn_sum.astype(LOW), "rep", axis=0), rows
     )
     return (
         mixed_out,

time: 169 us -> 165 us (0.976)
  blocking collectives: 26.2 us -> 36.9 us
  waiting for transfers between devices: 28 us -> 19.8 us
  starting transfers between devices: 49.2 us -> 45.5 us
    all_gather x0 -> x1, blocking collectives: none -> 10.8 us  [local(): lax.all_gather(attn_sum.astype(LOW), 'rep', axis=0)]
    ppermute x12, waiting for transfers between devices: 12.5 us -> 4.29 us  [along(): return lax.ppermute(v, 'shard', [(i, (i + 2 * hop) % n) for i in range(n)])]
    ppermute x21 -> x18, starting transfers between devices: 24.7 us -> 21.2 us  [rep(): return lax.ppermute(v, 'rep', [(i, i ^ k) for i in range(4)])]
    unnamed x90 -> x80, local copies, waits for them, and re-layouts: 4.9 us -> 3.6 us
    ppermute x21 -> x18, waiting for transfers between devices: 11.3 us -> 11.4 us  [rep(): return lax.ppermute(v, 'rep', [(i, i ^ k) for i in range(4)])]
  transfers between devices with their start and end apart: 46 -> 43, of which waited for: 16 -> 15; matrix products, arithmetic and copies ran while one was open for 4% -> 4% of each run, Pallas kernels for 21% -> 22%
where the time goes in v2:
time: 165 us; the launch traced here: 164 us
  Pallas kernels  49.5 us (30%)
  starting transfers between devices  45.5 us (28%)
  blocking collectives  36.9 us (22%)
  waiting for transfers between devices  19.8 us (12%)
  other arithmetic  6.9 us (4%)
  local copies, waits for them, and re-layouts  4.44 us (3%)
    pallas_call x11, Pallas kernels, run(): pl.pallas_call(kernel, out_shape=[jax.ShapeDtypeStruct(shape, dtype) for...  49.5 us
    ppermute x12, starting transfers between devices, along(): return lax.ppermute(v, 'shard', [(i, (i + 2 * hop) % n) for i in range(n)])  21.7 us
    ppermute x18, starting transfers between devices, rep(): return lax.ppermute(v, 'rep', [(i, i ^ k) for i in range(4)])  21.2 us
    all_gather x1, blocking collectives, local(): attended = lax.all_gather(sent, 'rep', axis=0)  14.1 us
    all_gather x1, blocking collectives, local(): grad_branch = lax.all_gather(grad_branch, 'rep', axis=0)  12 us
    ppermute x18, waiting for transfers between devices, rep(): return lax.ppermute(v, 'rep', [(i, i ^ k) for i in range(4)])  11.4 us
    all_gather x1, blocking collectives, local(): lax.all_gather(attn_sum.astype(LOW), 'rep', axis=0)  10.8 us
    ppermute x12, waiting for transfers between devices, along(): return lax.ppermute(v, 'shard', [(i, (i + 2 * hop) % n) for i in range(n)])  4.29 us
  transfers between devices with their start and end apart: 43, of which 15 were waited for; matrix products, arithmetic and copies ran while one was open for 4% of the time, Pallas kernels for 22%

profile of v2, /device:TPU:0, one launch (start us, length us, event | category | flops | bytes accessed | tf_op | source)
XLA Modules:
  0.0 164.3 jit_solution(16227803803220754413)
XLA Ops:
  1.2 2.1 %shard_map.169.refs_0_.refs_4_ = bf16[112,768]{1,0:T(8,128)(2,1)} custom-call(s32[4]{0:T(128)} %pad_add_fusion.scalar_ref, bf16[2,96]{1,0:T(2,128)(2,1)} %gain.1, bf16[6,96]{1,0:T(8,128)(2,1)} %shift.1, bf16[384]{0:T(512)(128)(2,1)} %bias_ref.1, bf16[96,2304]{1,0:T(8,128)(2,1)} %qkv_ref.1, bf16[96,768]{1,0:T(8,128)(2,1)} %p_ref.1), custom_call_target="tpu_custom_call" | custom-call | flops 1 | bytes 1 | tf_op jit(solution)/shard_map/pallas_call | solution.py:69
  3.4 3.0 %collective-permute-start = (bf16[112,768]{1,0:T(8,128)(2,1)}, bf16[112,768]{1,0:T(8,128)(2,1)S(1)}, u32[]{:S(2)}, u32[]{:S(2)}) collective-permute-start(bf16[112,768]{1,0:T(8,128)(2,1)} %shard_map.169.refs_0_.refs_4_), channel_id=1, source_target_pairs={{0,2},{1,3},{2,4},{3,5},{4,6},{5,7},{6,0},{7,1},{8,10},{9,11},{10,... | collective-permute-start | bytes 516104 | tf_op jit(solution)/shard_map/ppermute | solution.py:55
  11.5 2.6 %collective-permute-start.1 = (bf16[112,768]{1,0:T(8,128)(2,1)}, bf16[112,768]{1,0:T(8,128)(2,1)S(1)}, u32[]{:S(2)}, u32[]{:S(2)}) collective-permute-start(bf16[112,768]{1,0:T(8,128)(2,1)} %shard_map.169.refs_0_.refs_4_), channel_id=1, source_target_pairs={{0,4},{1,5},{2,6},{3,7},{4,0},{5,1},{6,2},{7,3},{8,12},{9,13},{10,... | collective-permute-start | bytes 516104 | tf_op jit(solution)/shard_map/ppermute | solution.py:55
  15.5 2.8 %shard_map.171.refs_13_ = bf16[192,768]{1,0:T(8,128)(2,1)} custom-call(s32[4]{0:T(128)} %pad_add_fusion.scalar_ref, bf16[96,3072]{1,0:T(8,128)(2,1)} %fc_ref, bf16[384,768]{1,0:T(8,128)(2,1)} %fc2_ref), custom_call_target="tpu_custom_call" | custom-call | flops 1 | bytes 1 | tf_op jit(solution)/shard_map/pallas_call | solution.py:69
  18.2 4.3 %collective-permute-done.1.refs_2_.refs_6_ = bf16[112,768]{1,0:T(8,128)(2,1)S(1)} collective-permute-done((bf16[112,768]{1,0:T(8,128)(2,1)}, bf16[112,768]{1,0:T(8,128)(2,1)S(1)}, u32[]{:S(2)}, u32[]{:S(2)}) %collective-permute-start.1) | collective-permute-done | bytes 172064 | tf_op jit(solution)/shard_map/ppermute | solution.py:55
  22.6 3.1 %collective-permute-start.13 = (bf16[192,768]{1,0:T(8,128)(2,1)}, bf16[192,768]{1,0:T(8,128)(2,1)S(1)}, u32[]{:S(2)}, u32[]{:S(2)}) collective-permute-start(bf16[192,768]{1,0:T(8,128)(2,1)} %shard_map.171.refs_13_), channel_id=1, source_target_pairs={{0,2},{1,3},{2,4},{3,5},{4,6},{5,7},{6,0},{7,1},{8,10},{9,11},{10,... | collective-permute-start | bytes 884744 | tf_op jit(solution)/shard_map/ppermute | solution.py:55
  28.9 2.4 %shard_map.172 = (bf16[224,768]{1,0:T(8,128)(2,1)}, bf16[96,768]{1,0:T(8,128)(2,1)}) custom-call(s32[4]{0:T(128)} %pad_add_fusion.scalar_ref, bf16[112,768]{1,0:T(8,128)(2,1)} %shard_map.169.refs_0_.refs_4_, bf16[112,768]{1,0:T(8,128)(2,1)} %copy-done.9, bf16[112,768]{1,0:T(8,128)(2,1)} %copy-done.10, bf16[112,768]{1,0:T(8,128)(2,1)} %copy-done.11, ...), custom_call_target="tpu_custom_call" | custom-call | flops 1 | bytes 1 | tf_op jit(solution)/shard_map/pallas_call | solution.py:69
  34.8 2.4 %collective-permute-start.14 = (bf16[192,768]{1,0:T(8,128)(2,1)S(1)}, bf16[192,768]{1,0:T(8,128)(2,1)S(1)}, u32[]{:S(2)}, u32[]{:S(2)}) collective-permute-start(bf16[192,768]{1,0:T(8,128)(2,1)S(1)} %copy-done.7), channel_id=1, source_target_pairs={{0,4},{1,5},{2,6},{3,7},{4,0},{5,1},{6,2},{7,3},{8,12},{9,13},{10,... | collective-permute-start | bytes 884744 | tf_op jit(solution)/shard_map/ppermute | solution.py:55
  37.2 7.1 %shard_map.173 = (bf16[768,768]{1,0:T(8,128)(2,1)}, bf16[512,768]{1,0:T(8,128)(2,1)}, bf16[512,576]{1,0:T(8,128)(2,1)}, f32[4,3,128,128]{3,2,1,0:T(8,128)}, bf16[128,768]{1,0:T(8,128)(2,1)}, /*index=5*/f32[16,768]{1,0:T(8,128)}) custom-call(s32[4]{0:T(128)} %pad_add_fusion.scalar_ref, bf16[144,768]{1,0:T(8,128)(2,1)} %shard_map.170.refs_0_.got_ref.refs_1_, ...), custom_call_target="tpu_custom_call" | custom-call | flops 1 | bytes 1 | tf_op jit(solution)/shard_map/pallas_call | solution.py:69
  44.4 14.1 %all-gather = bf16[512,768]{1,0:T(8,128)(2,1)} all-gather(bf16[128,768]{1,0:T(8,128)(2,1)} %get-tuple-element.108), channel_id=2, replica_groups=mesh['rep'=4,'shard'=8] {'rep'}, dimensions={0}, use_global_device_ids=true | all-gather | bytes 983040 | tf_op jit(solution)/shard_map/all_gather | solution.py:645
  64.1 8.9 %shard_map.174 = (bf16[512,768]{1,0:T(8,128)(2,1)}, f32[128,768]{1,0:T(8,128)}, bf16[512,768]{1,0:T(8,128)(2,1)}, bf16[512,768]{1,0:T(8,128)(2,1)}, bf16[512,768...) custom-call(s32[4]{0:T(128)} %pad_add_fusion.scalar_ref, ...), custom_call_target="tpu_custom_call" | custom-call | flops 1 | bytes 1 | tf_op jit(solution)/shard_map/pallas_call | solution.py:69
  76.6 5.8 %shard_map.175 = (bf16[768,768]{1,0:T(8,128)(2,1)}, bf16[768,768]{1,0:T(8,128)(2,1)}, f32[128,768]{1,0:T(8,128)}, bf16[128,768]{1,0:T(8,128)(2,1)}, bf16[128,768]{1,0:T(8,128)(2,1)}, /*index=5*/bf16[128,768]{1,0:T(8,128)(2,1)}) custom-call(s32[4]{0:T(128)} %pad_add_fusion.scalar_ref, bf16[512,768]{1,0:T(8,128)(2,1)} %get-tuple-element.122.refs_0_, ...), custom_call_target="tpu_custom_call" | custom-call | flops 1 | bytes 1 | tf_op jit(solution)/shard_map/pallas_call | solution.py:69
  82.4 2.9 %collective-permute-done.27.r2 = bf16[128,768]{1,0:T(8,128)(2,1)S(1)} collective-permute-done((bf16[128,768]{1,0:T(8,128)(2,1)}, bf16[128,768]{1,0:T(8,128)(2,1)S(1)}, u32[]{:S(2)}, u32[]{:S(2)}) %collective-permute-start.27) | collective-permute-done | bytes 196640 | tf_op jit(solution)/shard_map/ppermute | solution.py:58
  91.5 2.6 %collective-permute-start.34 = (bf16[192,768]{1,0:T(8,128)(2,1)S(1)}, bf16[192,768]{1,0:T(8,128)(2,1)S(1)}, u32[]{:S(2)}, u32[]{:S(2)}) collective-permute-start(bf16[192,768]{1,0:T(8,128)(2,1)S(1)} %get-tuple-element.174), channel_id=1, source_target_pairs={{0,4},{1,5},{2,6},{3,7},{4,0},{5,1},{6,2},{7,3},{8,12},{9,13},{10,... | collective-permute-start | bytes 884744 | tf_op jit(solution)/shard_map/ppermute | solution.py:55
  94.3 2.6 %collective-permute-start.35 = (bf16[192,768]{1,0:T(8,128)(2,1)S(1)}, bf16[192,768]{1,0:T(8,128)(2,1)S(1)}, u32[]{:S(2)}, u32[]{:S(2)}) collective-permute-start(bf16[192,768]{1,0:T(8,128)(2,1)S(1)} %get-tuple-element.173), channel_id=1, source_target_pairs={{0,6},{1,7},{2,0},{3,1},{4,2},{5,3},{6,4},{7,5},{8,14},{9,15},{10,... | collective-permute-start | bytes 884744 | tf_op jit(solution)/shard_map/ppermute | solution.py:55
  98.4 2.8 %shard_map.176 = (f32[128,768]{1,0:T(8,128)}, bf16[128,768]{1,0:T(8,128)(2,1)}, f32[4,768]{1,0:T(4,128)}) custom-call(s32[4]{0:T(128)} %pad_add_fusion.scalar_ref, f32[128,768]{1,0:T(8,128)} %get-tuple-element.131.own_ref, bf16[128,768]{1,0:T(8,128)(2,1)} %copy-done.35, bf16[128,768]{1,0:T(8,128)(2,1)} %copy-done.36, bf16[128,768]{1,0:T(8,128)(2,1)} %copy-done.37, ...), custom_call_target="tpu_custom_call" | custom-call | flops 1 | bytes 1 | tf_op jit(solution)/shard_map/pallas_call | solution.py:69
  101.2 12.0 %all-gather.1 = bf16[512,768]{1,0:T(8,128)(2,1)} all-gather(bf16[128,768]{1,0:T(8,128)(2,1)} %get-tuple-element.137), channel_id=3, replica_groups=mesh['rep'=4,'shard'=8] {'rep'}, dimensions={0}, use_global_device_ids=true | all-gather | bytes 983040 | tf_op jit(solution)/shard_map/all_gather | solution.py:677
  113.3 10.4 %shard_map.177 = (bf16[448,768]{1,0:T(8,128)(2,1)}, bf16[448,768]{1,0:T(8,128)(2,1)}, f32[128,768]{1,0:T(8,128)}, bf16[128,768]{1,0:T(8,128)(2,1)}, bf16[128,768]{1,0:T(8,128)(2,1)}, /*index=5*/bf16[128,768]{1,0:T(8,128)(2,1)}) custom-call(s32[4]{0:T(128)} %pad_add_fusion.scalar_ref, bf16[4,128,768]{2,1,0:T(8,128)(2,1)} %bitcast.7, ...), custom_call_target="tpu_custom_call" | custom-call | flops 1 | bytes 1 | tf_op jit(solution)/shard_map/pallas_call | solution.py:69
  130.4 2.9 %collective-permute-done.30 = bf16[128,768]{1,0:T(8,128)(2,1)S(1)} collective-permute-done((bf16[128,768]{1,0:T(8,128)(2,1)}, bf16[128,768]{1,0:T(8,128)(2,1)S(1)}, u32[]{:S(2)}, u32[]{:S(2)}) %collective-permute-start.30) | collective-permute-done | bytes 196640 | tf_op jit(solution)/shard_map/ppermute | solution.py:58
  137.3 2.1 %collective-permute-start.38 = (bf16[112,768]{1,0:T(8,128)(2,1)S(1)}, bf16[112,768]{1,0:T(8,128)(2,1)S(1)}, u32[]{:S(2)}, u32[]{:S(2)}) collective-permute-start(bf16[112,768]{1,0:T(8,128)(2,1)S(1)} %get-tuple-element.157), channel_id=1, source_target_pairs={{0,4},{1,5},{2,6},{3,7},{4,0},{5,1},{6,2},{7,3},{8,12},{9,13},{10,... | collective-permute-start | bytes 516104 | tf_op jit(solution)/shard_map/ppermute | solution.py:55
  139.4 2.9 %collective-permute-done.40.refs_1_ = bf16[192,768]{1,0:T(8,128)(2,1)S(1)} collective-permute-done((bf16[192,768]{1,0:T(8,128)(2,1)S(1)}, bf16[192,768]{1,0:T(8,128)(2,1)S(1)}, u32[]{:S(2)}, u32[]{:S(2)}) %collective-permute-start.40) | collective-permute-done | bytes 294944 | tf_op jit(solution)/shard_map/ppermute | solution.py:58
  147.7 3.0 %shard_map.179 = (f32[96,3072]{1,0:T(8,128)}, f32[384,768]{1,0:T(8,128)}) custom-call(s32[4]{0:T(128)} %pad_add_fusion.scalar_ref, bf16[192,768]{1,0:T(8,128)(2,1)} %copy-done.6, bf16[192,768]{1,0:T(8,128)(2,1)} %copy-done.25, bf16[192,768]{1,0:T(8,128)(2,1)} %copy-done.26, bf16[192,768]{1,0:T(8,128)(2,1)} %copy-done.27), custom_call_target="tpu_custom_call" | custom-call | flops 1 | bytes 1 | tf_op jit(solution)/shard_map/pallas_call | solution.py:69
  150.9 10.8 %all-gather.2 = bf16[448,768]{1,0:T(8,128)(2,1)} all-gather(bf16[112,768]{1,0:T(8,128)(2,1)S(1)} %add_convert_fusion.3), channel_id=4, replica_groups=mesh['rep'=4,'shard'=8] {'rep'}, dimensions={0}, use_global_device_ids=true | all-gather | bytes 860160 | tf_op jit(solution)/shard_map/all_gather | solution.py:714
  161.6 2.6 %shard_map.178 = (f32[96,2304]{1,0:T(8,128)}, f32[96,768]{1,0:T(8,128)}, f32[2,96]{1,0:T(2,128)}, f32[6,96]{1,0:T(8,128)}, f32[384]{0:T(512)}) custom-call(s32[4]{0:T(128)} %pad_add_fusion.scalar_ref, bf16[4,112,768]{2,1,0:T(8,128)(2,1)} %bitcast.9), custom_call_target="tpu_custom_call" | custom-call | flops 1 | bytes 1 | tf_op jit(solution)/shard_map/pallas_call | solution.py:69
  (172 shorter events, 47.0 us)
Async XLA Ops:
  3.4 10.8 %collective-permute-start = (bf16[112,768]{1,0:T(8,128)(2,1)}, bf16[112,768]{1,0:T(8,128)(2,1)S(1)}, u32[]{:S(2)}, u32[]{:S(2)}) collective-permute-start(bf16[112,768]{1,0:T(8,128)(2,1)} %shard_map.169.refs_0_.refs_4_), channel_id=1, source_target_pairs={{0,2},{1,3},{2,4},{3,5},{4,6},{5,7},{6,0},{7,1},{8,10},{9,11},{10,... | collective-permute-start | bytes 516104 | tf_op jit(solution)/shard_map/ppermute | solution.py:55
  8.0 14.5 %collective-permute-start.3 = (bf16[144,768]{1,0:T(8,128)(2,1)}, bf16[144,768]{1,0:T(8,128)(2,1)S(1)}, u32[]{:S(2)}, u32[]{:S(2)}) collective-permute-start(bf16[144,768]{1,0:T(8,128)(2,1)} %shard_map.170.refs_0_.got_ref.refs_1_), channel_id=1, source_target_pairs={{0,8},{8,0},{16,24},{24,16},{1,9},{9,1},{17,25},{25,17},{2,10},{10... | collective-permute-start | bytes 663560 | tf_op jit(solution)/shard_map/ppermute | solution.py:58
  9.5 13.0 %collective-permute-start.4 = (bf16[144,768]{1,0:T(8,128)(2,1)}, bf16[144,768]{1,0:T(8,128)(2,1)S(1)}, u32[]{:S(2)}, u32[]{:S(2)}) collective-permute-start(bf16[144,768]{1,0:T(8,128)(2,1)} %shard_map.170.refs_0_.got_ref.refs_1_), channel_id=1, source_target_pairs={{0,16},{8,24},{16,0},{24,8},{1,17},{9,25},{17,1},{25,9},{2,18},{10... | collective-permute-start | bytes 663560 | tf_op jit(solution)/shard_map/ppermute | solution.py:58
  11.1 11.5 %collective-permute-start.5 = (bf16[144,768]{1,0:T(8,128)(2,1)}, bf16[144,768]{1,0:T(8,128)(2,1)S(1)}, u32[]{:S(2)}, u32[]{:S(2)}) collective-permute-start(bf16[144,768]{1,0:T(8,128)(2,1)} %shard_map.170.refs_0_.got_ref.refs_1_), channel_id=1, source_target_pairs={{0,24},{8,16},{16,8},{24,0},{1,25},{9,17},{17,9},{25,1},{2,26},{10... | collective-permute-start | bytes 663560 | tf_op jit(solution)/shard_map/ppermute | solution.py:58
  11.5 11.0 %collective-permute-start.1 = (bf16[112,768]{1,0:T(8,128)(2,1)}, bf16[112,768]{1,0:T(8,128)(2,1)S(1)}, u32[]{:S(2)}, u32[]{:S(2)}) collective-permute-start(bf16[112,768]{1,0:T(8,128)(2,1)} %shard_map.169.refs_0_.refs_4_), channel_id=1, source_target_pairs={{0,4},{1,5},{2,6},{3,7},{4,0},{5,1},{6,2},{7,3},{8,12},{9,13},{10,... | collective-permute-start | bytes 516104 | tf_op jit(solution)/shard_map/ppermute | solution.py:55
  22.6 21.7 %collective-permute-start.13 = (bf16[192,768]{1,0:T(8,128)(2,1)}, bf16[192,768]{1,0:T(8,128)(2,1)S(1)}, u32[]{:S(2)}, u32[]{:S(2)}) collective-permute-start(bf16[192,768]{1,0:T(8,128)(2,1)} %shard_map.171.refs_13_), channel_id=1, source_target_pairs={{0,2},{1,3},{2,4},{3,5},{4,6},{5,7},{6,0},{7,1},{8,10},{9,11},{10,... | collective-permute-start | bytes 884744 | tf_op jit(solution)/shard_map/ppermute | solution.py:55
  31.3 27.3 %collective-permute-start.10 = (bf16[224,768]{1,0:T(8,128)(2,1)}, bf16[224,768]{1,0:T(8,128)(2,1)S(1)}, u32[]{:S(2)}, u32[]{:S(2)}) collective-permute-start(bf16[224,768]{1,0:T(8,128)(2,1)} %get-tuple-element.111.refs_5_), channel_id=1, source_target_pairs={{0,8},{8,0},{16,24},{24,16},{1,9},{9,1},{17,25},{25,17},{2,10},{10... | collective-permute-start | bytes 1032200 | tf_op jit(solution)/shard_map/ppermute | solution.py:58
  32.8 25.8 %collective-permute-start.11 = (bf16[224,768]{1,0:T(8,128)(2,1)}, bf16[224,768]{1,0:T(8,128)(2,1)S(1)}, u32[]{:S(2)}, u32[]{:S(2)}) collective-permute-start(bf16[224,768]{1,0:T(8,128)(2,1)} %get-tuple-element.111.refs_5_), channel_id=1, source_target_pairs={{0,16},{8,24},{16,0},{24,8},{1,17},{9,25},{17,1},{25,9},{2,18},{10... | collective-permute-start | bytes 1032200 | tf_op jit(solution)/shard_map/ppermute | solution.py:58
  34.3 24.3 %collective-permute-start.12 = (bf16[224,768]{1,0:T(8,128)(2,1)}, bf16[224,768]{1,0:T(8,128)(2,1)S(1)}, u32[]{:S(2)}, u32[]{:S(2)}) collective-permute-start(bf16[224,768]{1,0:T(8,128)(2,1)} %get-tuple-element.111.refs_5_), channel_id=1, source_target_pairs={{0,24},{8,16},{16,8},{24,0},{1,25},{9,17},{17,9},{25,1},{2,26},{10... | collective-permute-start | bytes 1032200 | tf_op jit(solution)/shard_map/ppermute | solution.py:58
  34.8 23.7 %collective-permute-start.14 = (bf16[192,768]{1,0:T(8,128)(2,1)S(1)}, bf16[192,768]{1,0:T(8,128)(2,1)S(1)}, u32[]{:S(2)}, u32[]{:S(2)}) collective-permute-start(bf16[192,768]{1,0:T(8,128)(2,1)S(1)} %copy-done.7), channel_id=1, source_target_pairs={{0,4},{1,5},{2,6},{3,7},{4,0},{5,1},{6,2},{7,3},{8,12},{9,13},{10,... | collective-permute-start | bytes 884744 | tf_op jit(solution)/shard_map/ppermute | solution.py:55
  44.3 14.3 %collective-permute-start.15 = (bf16[192,768]{1,0:T(8,128)(2,1)S(1)}, bf16[192,768]{1,0:T(8,128)(2,1)S(1)}, u32[]{:S(2)}, u32[]{:S(2)}) collective-permute-start(bf16[192,768]{1,0:T(8,128)(2,1)S(1)} %copy-done.7), channel_id=1, source_target_pairs={{0,6},{1,7},{2,0},{3,1},{4,2},{5,3},{6,4},{7,5},{8,14},{9,15},{10,... | collective-permute-start | bytes 884744 | tf_op jit(solution)/shard_map/ppermute | solution.py:55
  73.0 9.4 %collective-permute-start.26 = (bf16[128,768]{1,0:T(8,128)(2,1)}, bf16[128,768]{1,0:T(8,128)(2,1)S(1)}, u32[]{:S(2)}, u32[]{:S(2)}) collective-permute-start(bf16[128,768]{1,0:T(8,128)(2,1)} %get-tuple-element.132), channel_id=1, source_target_pairs={{0,8},{8,0},{16,24},{24,16},{1,9},{9,1},{17,25},{25,17},{2,10},{10... | collective-permute-start | bytes 589832 | tf_op jit(solution)/shard_map/ppermute | solution.py:58
  74.2 11.1 %collective-permute-start.27 = (bf16[128,768]{1,0:T(8,128)(2,1)}, bf16[128,768]{1,0:T(8,128)(2,1)S(1)}, u32[]{:S(2)}, u32[]{:S(2)}) collective-permute-start(bf16[128,768]{1,0:T(8,128)(2,1)} %get-tuple-element.133), channel_id=1, source_target_pairs={{0,16},{8,24},{16,0},{24,8},{1,17},{9,25},{17,1},{25,9},{2,18},{10... | collective-permute-start | bytes 589832 | tf_op jit(solution)/shard_map/ppermute | solution.py:58
  75.1 10.2 %collective-permute-start.28 = (bf16[128,768]{1,0:T(8,128)(2,1)}, bf16[128,768]{1,0:T(8,128)(2,1)S(1)}, u32[]{:S(2)}, u32[]{:S(2)}) collective-permute-start(bf16[128,768]{1,0:T(8,128)(2,1)} %get-tuple-element.134), channel_id=1, source_target_pairs={{0,24},{8,16},{16,8},{24,0},{1,25},{9,17},{17,9},{25,1},{2,26},{10... | collective-permute-start | bytes 589832 | tf_op jit(solution)/shard_map/ppermute | solution.py:58
  87.3 13.9 %collective-permute-start.24 = (bf16[128,768]{1,0:T(8,128)(2,1)}, bf16[128,768]{1,0:T(8,128)(2,1)S(1)}, u32[]{:S(2)}, u32[]{:S(2)}) collective-permute-start(bf16[128,768]{1,0:T(8,128)(2,1)} %get-tuple-element.129), channel_id=1, source_target_pairs={{0,16},{8,24},{16,0},{24,8},{1,17},{9,25},{17,1},{25,9},{2,18},{10... | collective-permute-start | bytes 589832 | tf_op jit(solution)/shard_map/ppermute | solution.py:58
  88.4 12.8 %collective-permute-start.25 = (bf16[128,768]{1,0:T(8,128)(2,1)}, bf16[128,768]{1,0:T(8,128)(2,1)S(1)}, u32[]{:S(2)}, u32[]{:S(2)}) collective-permute-start(bf16[128,768]{1,0:T(8,128)(2,1)} %get-tuple-element.130), channel_id=1, source_target_pairs={{0,24},{8,16},{16,8},{24,0},{1,25},{9,17},{17,9},{25,1},{2,26},{10... | collective-permute-start | bytes 589832 | tf_op jit(solution)/shard_map/ppermute | solution.py:58
  91.3 34.5 %collective-permute-start.33 = (bf16[192,768]{1,0:T(8,128)(2,1)S(1)}, bf16[192,768]{1,0:T(8,128)(2,1)S(1)}, u32[]{:S(2)}, u32[]{:S(2)}) collective-permute-start(bf16[192,768]{1,0:T(8,128)(2,1)S(1)} %get-tuple-element.172), channel_id=1, source_target_pairs={{0,2},{1,3},{2,4},{3,5},{4,6},{5,7},{6,0},{7,1},{8,10},{9,11},{10,... | collective-permute-start | bytes 884744 | tf_op jit(solution)/shard_map/ppermute | solution.py:55
  91.5 35.7 %collective-permute-start.34 = (bf16[192,768]{1,0:T(8,128)(2,1)S(1)}, bf16[192,768]{1,0:T(8,128)(2,1)S(1)}, u32[]{:S(2)}, u32[]{:S(2)}) collective-permute-start(bf16[192,768]{1,0:T(8,128)(2,1)S(1)} %get-tuple-element.174), channel_id=1, source_target_pairs={{0,4},{1,5},{2,6},{3,7},{4,0},{5,1},{6,2},{7,3},{8,12},{9,13},{10,... | collective-permute-start | bytes 884744 | tf_op jit(solution)/shard_map/ppermute | solution.py:55
  94.3 33.0 %collective-permute-start.35 = (bf16[192,768]{1,0:T(8,128)(2,1)S(1)}, bf16[192,768]{1,0:T(8,128)(2,1)S(1)}, u32[]{:S(2)}, u32[]{:S(2)}) collective-permute-start(bf16[192,768]{1,0:T(8,128)(2,1)S(1)} %get-tuple-element.173), channel_id=1, source_target_pairs={{0,6},{1,7},{2,0},{3,1},{4,2},{5,3},{6,4},{7,5},{8,14},{9,15},{10,... | collective-permute-start | bytes 884744 | tf_op jit(solution)/shard_map/ppermute | solution.py:55
  133.5 8.8 %collective-permute-start.40 = (bf16[192,768]{1,0:T(8,128)(2,1)S(1)}, bf16[192,768]{1,0:T(8,128)(2,1)S(1)}, u32[]{:S(2)}, u32[]{:S(2)}) collective-permute-start(bf16[192,768]{1,0:T(8,128)(2,1)S(1)} %convert_add_fusion.refs_0_), channel_id=1, source_target_pairs={{0,8},{8,0},{16,24},{24,16},{1,9},{9,1},{17,25},{25,17},{2,10},{10... | collective-permute-start | bytes 884744 | tf_op jit(solution)/shard_map/ppermute | solution.py:58
  134.5 11.7 %collective-permute-start.41 = (bf16[192,768]{1,0:T(8,128)(2,1)S(1)}, bf16[192,768]{1,0:T(8,128)(2,1)S(1)}, u32[]{:S(2)}, u32[]{:S(2)}) collective-permute-start(bf16[192,768]{1,0:T(8,128)(2,1)S(1)} %convert_add_fusion.refs_0_), channel_id=1, source_target_pairs={{0,16},{8,24},{16,0},{24,8},{1,17},{9,25},{17,1},{25,9},{2,18},{10... | collective-permute-start | bytes 884744 | tf_op jit(solution)/shard_map/ppermute | solution.py:58
  135.6 10.6 %collective-permute-start.42 = (bf16[192,768]{1,0:T(8,128)(2,1)S(1)}, bf16[192,768]{1,0:T(8,128)(2,1)S(1)}, u32[]{:S(2)}, u32[]{:S(2)}) collective-permute-start(bf16[192,768]{1,0:T(8,128)(2,1)S(1)} %convert_add_fusion.refs_0_), channel_id=1, source_target_pairs={{0,24},{8,16},{16,8},{24,0},{1,25},{9,17},{17,9},{25,1},{2,26},{10... | collective-permute-start | bytes 884744 | tf_op jit(solution)/shard_map/ppermute | solution.py:58
  137.2 13.5 %collective-permute-start.37 = (bf16[112,768]{1,0:T(8,128)(2,1)S(1)}, bf16[112,768]{1,0:T(8,128)(2,1)S(1)}, u32[]{:S(2)}, u32[]{:S(2)}) collective-permute-start(bf16[112,768]{1,0:T(8,128)(2,1)S(1)} %get-tuple-element.156), channel_id=1, source_target_pairs={{0,2},{1,3},{2,4},{3,5},{4,6},{5,7},{6,0},{7,1},{8,10},{9,11},{10,... | collective-permute-start | bytes 516104 | tf_op jit(solution)/shard_map/ppermute | solution.py:55
  137.3 13.4 %collective-permute-start.38 = (bf16[112,768]{1,0:T(8,128)(2,1)S(1)}, bf16[112,768]{1,0:T(8,128)(2,1)S(1)}, u32[]{:S(2)}, u32[]{:S(2)}) collective-permute-start(bf16[112,768]{1,0:T(8,128)(2,1)S(1)} %get-tuple-element.157), channel_id=1, source_target_pairs={{0,4},{1,5},{2,6},{3,7},{4,0},{5,1},{6,2},{7,3},{8,12},{9,13},{10,... | collective-permute-start | bytes 516104 | tf_op jit(solution)/shard_map/ppermute | solution.py:55
  (59 other events, 336.0 us)

commit v3 on v2

--- a/solution.py
+++ b/solution.py
@@ -672,6 +672,7 @@
     grad_middle, grad_branch, sums = middle_back(
         links, own, received, middle, got[0], out_grad, small_f, slots, count
     )
+    ff_sent = tie(ff_sent, grad_branch)
     branch_got = [links.rep(v, k) for k, v in enumerate(branch_sent, start=1)]
     grad_branch = tie(grad_branch, branch_got)
     grad_branch = lax.all_gather(grad_branch, "rep", axis=0)

time: 165 us -> 163 us (0.988)
  other arithmetic: 6.9 us -> 4.79 us
    unnamed x80 -> x84, local copies, waits for them, and re-layouts: 3.6 us -> 3.64 us
  transfers between devices with their start and end apart: 43 -> 43, of which waited for: 15 -> 15; matrix products, arithmetic and copies ran while one was open for 4% -> 3% of each run, Pallas kernels for 22% -> 22%
where the time goes in v3:
time: 163 us; the launch traced here: 162 us
  Pallas kernels  49.6 us (30%)
  starting transfers between devices  44.8 us (27%)
  blocking collectives  36.6 us (22%)
  waiting for transfers between devices  20.8 us (13%)
  other arithmetic  4.79 us (3%)
  local copies, waits for them, and re-layouts  4.47 us (3%)
    pallas_call x11, Pallas kernels, run(): pl.pallas_call(kernel, out_shape=[jax.ShapeDtypeStruct(shape, dtype) for...  49.6 us
    ppermute x18, starting transfers between devices, rep(): return lax.ppermute(v, 'rep', [(i, i ^ k) for i in range(4)])  21.2 us
    ppermute x12, starting transfers between devices, along(): return lax.ppermute(v, 'shard', [(i, (i + 2 * hop) % n) for i in range(n)])  21 us
    all_gather x1, blocking collectives, local(): attended = lax.all_gather(sent, 'rep', axis=0)  14.1 us
    ppermute x18, waiting for transfers between devices, rep(): return lax.ppermute(v, 'rep', [(i, i ^ k) for i in range(4)])  12.4 us
    all_gather x1, blocking collectives, local(): grad_branch = lax.all_gather(grad_branch, 'rep', axis=0)  11.6 us
    all_gather x1, blocking collectives, local(): lax.all_gather(attn_sum.astype(LOW), 'rep', axis=0)  10.9 us
    ppermute x12, waiting for transfers between devices, along(): return lax.ppermute(v, 'shard', [(i, (i + 2 * hop) % n) for i in range(n)])  4.29 us
  transfers between devices with their start and end apart: 43, of which 15 were waited for; matrix products, arithmetic and copies ran while one was open for 3% of the time, Pallas kernels for 22%

profile of v3, /device:TPU:0, one launch (start us, length us, event | category | flops | bytes accessed | tf_op | source)
XLA Modules:
  0.0 162.2 jit_solution(12636944666429383724)
XLA Ops:
  1.2 2.1 %shard_map.169.refs_0_.refs_4_ = bf16[112,768]{1,0:T(8,128)(2,1)} custom-call(s32[4]{0:T(128)} %pad_add_fusion.scalar_ref, bf16[2,96]{1,0:T(2,128)(2,1)} %gain.1, bf16[6,96]{1,0:T(8,128)(2,1)} %shift.1, bf16[384]{0:T(512)(128)(2,1)} %bias_ref.1, bf16[96,2304]{1,0:T(8,128)(2,1)} %qkv_ref.1, bf16[96,768]{1,0:T(8,128)(2,1)} %p_ref.1), custom_call_target="tpu_custom_call" | custom-call | flops 1 | bytes 1 | tf_op jit(solution)/shard_map/pallas_call | solution.py:69
  3.4 3.0 %collective-permute-start = (bf16[112,768]{1,0:T(8,128)(2,1)}, bf16[112,768]{1,0:T(8,128)(2,1)S(1)}, u32[]{:S(2)}, u32[]{:S(2)}) collective-permute-start(bf16[112,768]{1,0:T(8,128)(2,1)} %shard_map.169.refs_0_.refs_4_), channel_id=1, source_target_pairs={{0,2},{1,3},{2,4},{3,5},{4,6},{5,7},{6,0},{7,1},{8,10},{9,11},{10,... | collective-permute-start | bytes 516104 | tf_op jit(solution)/shard_map/ppermute | solution.py:55
  11.5 2.6 %collective-permute-start.1 = (bf16[112,768]{1,0:T(8,128)(2,1)}, bf16[112,768]{1,0:T(8,128)(2,1)S(1)}, u32[]{:S(2)}, u32[]{:S(2)}) collective-permute-start(bf16[112,768]{1,0:T(8,128)(2,1)} %shard_map.169.refs_0_.refs_4_), channel_id=1, source_target_pairs={{0,4},{1,5},{2,6},{3,7},{4,0},{5,1},{6,2},{7,3},{8,12},{9,13},{10,... | collective-permute-start | bytes 516104 | tf_op jit(solution)/shard_map/ppermute | solution.py:55
  15.5 2.8 %shard_map.171.refs_13_ = bf16[192,768]{1,0:T(8,128)(2,1)} custom-call(s32[4]{0:T(128)} %pad_add_fusion.scalar_ref, bf16[96,3072]{1,0:T(8,128)(2,1)} %fc_ref, bf16[384,768]{1,0:T(8,128)(2,1)} %fc2_ref), custom_call_target="tpu_custom_call" | custom-call | flops 1 | bytes 1 | tf_op jit(solution)/shard_map/pallas_call | solution.py:69
  18.2 4.3 %collective-permute-done.1.refs_2_.refs_6_ = bf16[112,768]{1,0:T(8,128)(2,1)S(1)} collective-permute-done((bf16[112,768]{1,0:T(8,128)(2,1)}, bf16[112,768]{1,0:T(8,128)(2,1)S(1)}, u32[]{:S(2)}, u32[]{:S(2)}) %collective-permute-start.1) | collective-permute-done | bytes 172064 | tf_op jit(solution)/shard_map/ppermute | solution.py:55
  22.6 3.1 %collective-permute-start.13 = (bf16[192,768]{1,0:T(8,128)(2,1)}, bf16[192,768]{1,0:T(8,128)(2,1)S(1)}, u32[]{:S(2)}, u32[]{:S(2)}) collective-permute-start(bf16[192,768]{1,0:T(8,128)(2,1)} %shard_map.171.refs_13_), channel_id=1, source_target_pairs={{0,2},{1,3},{2,4},{3,5},{4,6},{5,7},{6,0},{7,1},{8,10},{9,11},{10,... | collective-permute-start | bytes 884744 | tf_op jit(solution)/shard_map/ppermute | solution.py:55
  28.9 2.4 %shard_map.172 = (bf16[224,768]{1,0:T(8,128)(2,1)}, bf16[96,768]{1,0:T(8,128)(2,1)}) custom-call(s32[4]{0:T(128)} %pad_add_fusion.scalar_ref, bf16[112,768]{1,0:T(8,128)(2,1)} %shard_map.169.refs_0_.refs_4_, bf16[112,768]{1,0:T(8,128)(2,1)} %copy-done.10, bf16[112,768]{1,0:T(8,128)(2,1)} %copy-done.11, bf16[112,768]{1,0:T(8,128)(2,1)} %copy-done.12, ...), custom_call_target="tpu_custom_call" | custom-call | flops 1 | bytes 1 | tf_op jit(solution)/shard_map/pallas_call | solution.py:69
  34.8 2.4 %collective-permute-start.14 = (bf16[192,768]{1,0:T(8,128)(2,1)S(1)}, bf16[192,768]{1,0:T(8,128)(2,1)S(1)}, u32[]{:S(2)}, u32[]{:S(2)}) collective-permute-start(bf16[192,768]{1,0:T(8,128)(2,1)S(1)} %copy-done.8), channel_id=1, source_target_pairs={{0,4},{1,5},{2,6},{3,7},{4,0},{5,1},{6,2},{7,3},{8,12},{9,13},{10,... | collective-permute-start | bytes 884744 | tf_op jit(solution)/shard_map/ppermute | solution.py:55
  37.2 7.1 %shard_map.173 = (bf16[768,768]{1,0:T(8,128)(2,1)}, bf16[512,768]{1,0:T(8,128)(2,1)}, bf16[512,576]{1,0:T(8,128)(2,1)}, f32[4,3,128,128]{3,2,1,0:T(8,128)}, bf16[128,768]{1,0:T(8,128)(2,1)}, /*index=5*/f32[16,768]{1,0:T(8,128)}) custom-call(s32[4]{0:T(128)} %pad_add_fusion.scalar_ref, bf16[144,768]{1,0:T(8,128)(2,1)} %shard_map.170.refs_0_.got_ref.refs_1_, ...), custom_call_target="tpu_custom_call" | custom-call | flops 1 | bytes 1 | tf_op jit(solution)/shard_map/pallas_call | solution.py:69
  44.4 14.1 %all-gather = bf16[512,768]{1,0:T(8,128)(2,1)} all-gather(bf16[128,768]{1,0:T(8,128)(2,1)} %get-tuple-element.111), channel_id=2, replica_groups=mesh['rep'=4,'shard'=8] {'rep'}, dimensions={0}, use_global_device_ids=true | all-gather | bytes 983040 | tf_op jit(solution)/shard_map/all_gather | solution.py:645
  64.2 8.9 %shard_map.174 = (bf16[512,768]{1,0:T(8,128)(2,1)}, f32[128,768]{1,0:T(8,128)}, bf16[512,768]{1,0:T(8,128)(2,1)}, bf16[512,768]{1,0:T(8,128)(2,1)}, bf16[512,768...) custom-call(s32[4]{0:T(128)} %pad_add_fusion.scalar_ref, ...), custom_call_target="tpu_custom_call" | custom-call | flops 1 | bytes 1 | tf_op jit(solution)/shard_map/pallas_call | solution.py:69
  76.7 5.8 %shard_map.175 = (bf16[768,768]{1,0:T(8,128)(2,1)}, bf16[768,768]{1,0:T(8,128)(2,1)}, f32[128,768]{1,0:T(8,128)}, bf16[128,768]{1,0:T(8,128)(2,1)}, bf16[128,768]{1,0:T(8,128)(2,1)}, /*index=5*/bf16[128,768]{1,0:T(8,128)(2,1)}) custom-call(s32[4]{0:T(128)} %pad_add_fusion.scalar_ref, bf16[512,768]{1,0:T(8,128)(2,1)} %get-tuple-element.125.refs_0_, ...), custom_call_target="tpu_custom_call" | custom-call | flops 1 | bytes 1 | tf_op jit(solution)/shard_map/pallas_call | solution.py:69
  82.5 2.9 %collective-permute-done.27.r2 = bf16[128,768]{1,0:T(8,128)(2,1)S(1)} collective-permute-done((bf16[128,768]{1,0:T(8,128)(2,1)}, bf16[128,768]{1,0:T(8,128)(2,1)S(1)}, u32[]{:S(2)}, u32[]{:S(2)}) %collective-permute-start.27) | collective-permute-done | bytes 196640 | tf_op jit(solution)/shard_map/ppermute | solution.py:58
  90.0 2.8 %shard_map.176 = (f32[128,768]{1,0:T(8,128)}, bf16[128,768]{1,0:T(8,128)(2,1)}, f32[4,768]{1,0:T(4,128)}) custom-call(s32[4]{0:T(128)} %pad_add_fusion.scalar_ref, f32[128,768]{1,0:T(8,128)} %get-tuple-element.134.own_ref, bf16[128,768]{1,0:T(8,128)(2,1)} %copy-done.36, bf16[128,768]{1,0:T(8,128)(2,1)} %copy-done.37, bf16[128,768]{1,0:T(8,128)(2,1)} %copy-done.38, ...), custom_call_target="tpu_custom_call" | custom-call | flops 1 | bytes 1 | tf_op jit(solution)/shard_map/pallas_call | solution.py:69
  93.3 2.6 %collective-permute-start.34 = (bf16[192,768]{1,0:T(8,128)(2,1)S(1)}, bf16[192,768]{1,0:T(8,128)(2,1)S(1)}, u32[]{:S(2)}, u32[]{:S(2)}) collective-permute-start(bf16[192,768]{1,0:T(8,128)(2,1)S(1)} %get-tuple-element.159), channel_id=1, source_target_pairs={{0,4},{1,5},{2,6},{3,7},{4,0},{5,1},{6,2},{7,3},{8,12},{9,13},{10,... | collective-permute-start | bytes 884744 | tf_op jit(solution)/shard_map/ppermute | solution.py:55
  95.8 2.8 %collective-permute-start.35 = (bf16[192,768]{1,0:T(8,128)(2,1)S(1)}, bf16[192,768]{1,0:T(8,128)(2,1)S(1)}, u32[]{:S(2)}, u32[]{:S(2)}) collective-permute-start(bf16[192,768]{1,0:T(8,128)(2,1)S(1)} %get-tuple-element.160), channel_id=1, source_target_pairs={{0,6},{1,7},{2,0},{3,1},{4,2},{5,3},{6,4},{7,5},{8,14},{9,15},{10,... | collective-permute-start | bytes 884744 | tf_op jit(solution)/shard_map/ppermute | solution.py:55
  100.2 11.6 %all-gather.1 = bf16[512,768]{1,0:T(8,128)(2,1)} all-gather(bf16[128,768]{1,0:T(8,128)(2,1)S(1)} %copy-done.39), channel_id=3, replica_groups=mesh['rep'=4,'shard'=8] {'rep'}, dimensions={0}, use_global_device_ids=true | all-gather | bytes 983040 | tf_op jit(solution)/shard_map/all_gather | solution.py:678
  111.8 10.4 %shard_map.177 = (bf16[448,768]{1,0:T(8,128)(2,1)}, bf16[448,768]{1,0:T(8,128)(2,1)}, f32[128,768]{1,0:T(8,128)}, bf16[128,768]{1,0:T(8,128)(2,1)}, bf16[128,768]{1,0:T(8,128)(2,1)}, /*index=5*/bf16[128,768]{1,0:T(8,128)(2,1)}) custom-call(s32[4]{0:T(128)} %pad_add_fusion.scalar_ref, bf16[4,128,768]{2,1,0:T(8,128)(2,1)} %bitcast.7, ...), custom_call_target="tpu_custom_call" | custom-call | flops 1 | bytes 1 | tf_op jit(solution)/shard_map/pallas_call | solution.py:69
  128.6 2.6 %collective-permute-done.30 = bf16[128,768]{1,0:T(8,128)(2,1)S(1)} collective-permute-done((bf16[128,768]{1,0:T(8,128)(2,1)}, bf16[128,768]{1,0:T(8,128)(2,1)S(1)}, u32[]{:S(2)}, u32[]{:S(2)}) %collective-permute-start.30) | collective-permute-done | bytes 196640 | tf_op jit(solution)/shard_map/ppermute | solution.py:58
  137.5 2.7 %collective-permute-done.40.refs_1_ = bf16[192,768]{1,0:T(8,128)(2,1)S(1)} collective-permute-done((bf16[192,768]{1,0:T(8,128)(2,1)S(1)}, bf16[192,768]{1,0:T(8,128)(2,1)S(1)}, u32[]{:S(2)}, u32[]{:S(2)}) %collective-permute-start.40) | collective-permute-done | bytes 294944 | tf_op jit(solution)/shard_map/ppermute | solution.py:58
  142.0 2.1 %collective-permute-done.41.refs_2_ = bf16[192,768]{1,0:T(8,128)(2,1)S(1)} collective-permute-done((bf16[192,768]{1,0:T(8,128)(2,1)S(1)}, bf16[192,768]{1,0:T(8,128)(2,1)S(1)}, u32[]{:S(2)}, u32[]{:S(2)}) %collective-permute-start.41) | collective-permute-done | bytes 294944 | tf_op jit(solution)/shard_map/ppermute | solution.py:58
  145.5 3.0 %shard_map.179 = (f32[96,3072]{1,0:T(8,128)}, f32[384,768]{1,0:T(8,128)}) custom-call(s32[4]{0:T(128)} %pad_add_fusion.scalar_ref, bf16[192,768]{1,0:T(8,128)(2,1)} %copy-done.6, bf16[192,768]{1,0:T(8,128)(2,1)} %copy-done.26, bf16[192,768]{1,0:T(8,128)(2,1)} %copy-done.27, bf16[192,768]{1,0:T(8,128)(2,1)} %copy-done.28), custom_call_target="tpu_custom_call" | custom-call | flops 1 | bytes 1 | tf_op jit(solution)/shard_map/pallas_call | solution.py:69
  148.7 10.9 %all-gather.2 = bf16[448,768]{1,0:T(8,128)(2,1)} all-gather(bf16[112,768]{1,0:T(8,128)(2,1)S(1)} %add_convert_fusion.3), channel_id=4, replica_groups=mesh['rep'=4,'shard'=8] {'rep'}, dimensions={0}, use_global_device_ids=true | all-gather | bytes 860160 | tf_op jit(solution)/shard_map/all_gather | solution.py:715
  159.6 2.6 %shard_map.178 = (f32[96,2304]{1,0:T(8,128)}, f32[96,768]{1,0:T(8,128)}, f32[2,96]{1,0:T(2,128)}, f32[6,96]{1,0:T(8,128)}, f32[384]{0:T(512)}) custom-call(s32[4]{0:T(128)} %pad_add_fusion.scalar_ref, bf16[4,112,768]{2,1,0:T(8,128)(2,1)} %bitcast.9), custom_call_target="tpu_custom_call" | custom-call | flops 1 | bytes 1 | tf_op jit(solution)/shard_map/pallas_call | solution.py:69
  (176 shorter events, 45.4 us)
Async XLA Ops:
  3.4 10.8 %collective-permute-start = (bf16[112,768]{1,0:T(8,128)(2,1)}, bf16[112,768]{1,0:T(8,128)(2,1)S(1)}, u32[]{:S(2)}, u32[]{:S(2)}) collective-permute-start(bf16[112,768]{1,0:T(8,128)(2,1)} %shard_map.169.refs_0_.refs_4_), channel_id=1, source_target_pairs={{0,2},{1,3},{2,4},{3,5},{4,6},{5,7},{6,0},{7,1},{8,10},{9,11},{10,... | collective-permute-start | bytes 516104 | tf_op jit(solution)/shard_map/ppermute | solution.py:55
  8.1 14.5 %collective-permute-start.3 = (bf16[144,768]{1,0:T(8,128)(2,1)}, bf16[144,768]{1,0:T(8,128)(2,1)S(1)}, u32[]{:S(2)}, u32[]{:S(2)}) collective-permute-start(bf16[144,768]{1,0:T(8,128)(2,1)} %shard_map.170.refs_0_.got_ref.refs_1_), channel_id=1, source_target_pairs={{0,8},{8,0},{16,24},{24,16},{1,9},{9,1},{17,25},{25,17},{2,10},{10... | collective-permute-start | bytes 663560 | tf_op jit(solution)/shard_map/ppermute | solution.py:58
  9.5 13.0 %collective-permute-start.4 = (bf16[144,768]{1,0:T(8,128)(2,1)}, bf16[144,768]{1,0:T(8,128)(2,1)S(1)}, u32[]{:S(2)}, u32[]{:S(2)}) collective-permute-start(bf16[144,768]{1,0:T(8,128)(2,1)} %shard_map.170.refs_0_.got_ref.refs_1_), channel_id=1, source_target_pairs={{0,16},{8,24},{16,0},{24,8},{1,17},{9,25},{17,1},{25,9},{2,18},{10... | collective-permute-start | bytes 663560 | tf_op jit(solution)/shard_map/ppermute | solution.py:58
  11.1 11.5 %collective-permute-start.5 = (bf16[144,768]{1,0:T(8,128)(2,1)}, bf16[144,768]{1,0:T(8,128)(2,1)S(1)}, u32[]{:S(2)}, u32[]{:S(2)}) collective-permute-start(bf16[144,768]{1,0:T(8,128)(2,1)} %shard_map.170.refs_0_.got_ref.refs_1_), channel_id=1, source_target_pairs={{0,24},{8,16},{16,8},{24,0},{1,25},{9,17},{17,9},{25,1},{2,26},{10... | collective-permute-start | bytes 663560 | tf_op jit(solution)/shard_map/ppermute | solution.py:58
  11.5 11.0 %collective-permute-start.1 = (bf16[112,768]{1,0:T(8,128)(2,1)}, bf16[112,768]{1,0:T(8,128)(2,1)S(1)}, u32[]{:S(2)}, u32[]{:S(2)}) collective-permute-start(bf16[112,768]{1,0:T(8,128)(2,1)} %shard_map.169.refs_0_.refs_4_), channel_id=1, source_target_pairs={{0,4},{1,5},{2,6},{3,7},{4,0},{5,1},{6,2},{7,3},{8,12},{9,13},{10,... | collective-permute-start | bytes 516104 | tf_op jit(solution)/shard_map/ppermute | solution.py:55
  22.6 21.7 %collective-permute-start.13 = (bf16[192,768]{1,0:T(8,128)(2,1)}, bf16[192,768]{1,0:T(8,128)(2,1)S(1)}, u32[]{:S(2)}, u32[]{:S(2)}) collective-permute-start(bf16[192,768]{1,0:T(8,128)(2,1)} %shard_map.171.refs_13_), channel_id=1, source_target_pairs={{0,2},{1,3},{2,4},{3,5},{4,6},{5,7},{6,0},{7,1},{8,10},{9,11},{10,... | collective-permute-start | bytes 884744 | tf_op jit(solution)/shard_map/ppermute | solution.py:55
  31.3 27.3 %collective-permute-start.10 = (bf16[224,768]{1,0:T(8,128)(2,1)}, bf16[224,768]{1,0:T(8,128)(2,1)S(1)}, u32[]{:S(2)}, u32[]{:S(2)}) collective-permute-start(bf16[224,768]{1,0:T(8,128)(2,1)} %get-tuple-element.114.refs_5_), channel_id=1, source_target_pairs={{0,8},{8,0},{16,24},{24,16},{1,9},{9,1},{17,25},{25,17},{2,10},{10... | collective-permute-start | bytes 1032200 | tf_op jit(solution)/shard_map/ppermute | solution.py:58
  32.8 25.8 %collective-permute-start.11 = (bf16[224,768]{1,0:T(8,128)(2,1)}, bf16[224,768]{1,0:T(8,128)(2,1)S(1)}, u32[]{:S(2)}, u32[]{:S(2)}) collective-permute-start(bf16[224,768]{1,0:T(8,128)(2,1)} %get-tuple-element.114.refs_5_), channel_id=1, source_target_pairs={{0,16},{8,24},{16,0},{24,8},{1,17},{9,25},{17,1},{25,9},{2,18},{10... | collective-permute-start | bytes 1032200 | tf_op jit(solution)/shard_map/ppermute | solution.py:58
  34.3 24.3 %collective-permute-start.12 = (bf16[224,768]{1,0:T(8,128)(2,1)}, bf16[224,768]{1,0:T(8,128)(2,1)S(1)}, u32[]{:S(2)}, u32[]{:S(2)}) collective-permute-start(bf16[224,768]{1,0:T(8,128)(2,1)} %get-tuple-element.114.refs_5_), channel_id=1, source_target_pairs={{0,24},{8,16},{16,8},{24,0},{1,25},{9,17},{17,9},{25,1},{2,26},{10... | collective-permute-start | bytes 1032200 | tf_op jit(solution)/shard_map/ppermute | solution.py:58
  34.8 23.7 %collective-permute-start.14 = (bf16[192,768]{1,0:T(8,128)(2,1)S(1)}, bf16[192,768]{1,0:T(8,128)(2,1)S(1)}, u32[]{:S(2)}, u32[]{:S(2)}) collective-permute-start(bf16[192,768]{1,0:T(8,128)(2,1)S(1)} %copy-done.8), channel_id=1, source_target_pairs={{0,4},{1,5},{2,6},{3,7},{4,0},{5,1},{6,2},{7,3},{8,12},{9,13},{10,... | collective-permute-start | bytes 884744 | tf_op jit(solution)/shard_map/ppermute | solution.py:55
  44.3 14.3 %collective-permute-start.15 = (bf16[192,768]{1,0:T(8,128)(2,1)S(1)}, bf16[192,768]{1,0:T(8,128)(2,1)S(1)}, u32[]{:S(2)}, u32[]{:S(2)}) collective-permute-start(bf16[192,768]{1,0:T(8,128)(2,1)S(1)} %copy-done.8), channel_id=1, source_target_pairs={{0,6},{1,7},{2,0},{3,1},{4,2},{5,3},{6,4},{7,5},{8,14},{9,15},{10,... | collective-permute-start | bytes 884744 | tf_op jit(solution)/shard_map/ppermute | solution.py:55
  73.1 9.4 %collective-permute-start.26 = (bf16[128,768]{1,0:T(8,128)(2,1)}, bf16[128,768]{1,0:T(8,128)(2,1)S(1)}, u32[]{:S(2)}, u32[]{:S(2)}) collective-permute-start(bf16[128,768]{1,0:T(8,128)(2,1)} %get-tuple-element.135), channel_id=1, source_target_pairs={{0,8},{8,0},{16,24},{24,16},{1,9},{9,1},{17,25},{25,17},{2,10},{10... | collective-permute-start | bytes 589832 | tf_op jit(solution)/shard_map/ppermute | solution.py:58
  74.3 11.1 %collective-permute-start.27 = (bf16[128,768]{1,0:T(8,128)(2,1)}, bf16[128,768]{1,0:T(8,128)(2,1)S(1)}, u32[]{:S(2)}, u32[]{:S(2)}) collective-permute-start(bf16[128,768]{1,0:T(8,128)(2,1)} %get-tuple-element.136), channel_id=1, source_target_pairs={{0,16},{8,24},{16,0},{24,8},{1,17},{9,25},{17,1},{25,9},{2,18},{10... | collective-permute-start | bytes 589832 | tf_op jit(solution)/shard_map/ppermute | solution.py:58
  75.2 10.2 %collective-permute-start.28 = (bf16[128,768]{1,0:T(8,128)(2,1)}, bf16[128,768]{1,0:T(8,128)(2,1)S(1)}, u32[]{:S(2)}, u32[]{:S(2)}) collective-permute-start(bf16[128,768]{1,0:T(8,128)(2,1)} %get-tuple-element.137), channel_id=1, source_target_pairs={{0,24},{8,16},{16,8},{24,0},{1,25},{9,17},{17,9},{25,1},{2,26},{10... | collective-permute-start | bytes 589832 | tf_op jit(solution)/shard_map/ppermute | solution.py:58
  86.4 9.4 %collective-permute-start.23 = (bf16[128,768]{1,0:T(8,128)(2,1)}, bf16[128,768]{1,0:T(8,128)(2,1)S(1)}, u32[]{:S(2)}, u32[]{:S(2)}) collective-permute-start(bf16[128,768]{1,0:T(8,128)(2,1)} %get-tuple-element.131), channel_id=1, source_target_pairs={{0,8},{8,0},{16,24},{24,16},{1,9},{9,1},{17,25},{25,17},{2,10},{10... | collective-permute-start | bytes 589832 | tf_op jit(solution)/shard_map/ppermute | solution.py:58
  87.4 12.8 %collective-permute-start.24 = (bf16[128,768]{1,0:T(8,128)(2,1)}, bf16[128,768]{1,0:T(8,128)(2,1)S(1)}, u32[]{:S(2)}, u32[]{:S(2)}) collective-permute-start(bf16[128,768]{1,0:T(8,128)(2,1)} %get-tuple-element.132), channel_id=1, source_target_pairs={{0,16},{8,24},{16,0},{24,8},{1,17},{9,25},{17,1},{25,9},{2,18},{10... | collective-permute-start | bytes 589832 | tf_op jit(solution)/shard_map/ppermute | solution.py:58
  88.5 11.7 %collective-permute-start.25 = (bf16[128,768]{1,0:T(8,128)(2,1)}, bf16[128,768]{1,0:T(8,128)(2,1)S(1)}, u32[]{:S(2)}, u32[]{:S(2)}) collective-permute-start(bf16[128,768]{1,0:T(8,128)(2,1)} %get-tuple-element.133), channel_id=1, source_target_pairs={{0,24},{8,16},{16,8},{24,0},{1,25},{9,17},{17,9},{25,1},{2,26},{10... | collective-permute-start | bytes 589832 | tf_op jit(solution)/shard_map/ppermute | solution.py:58
  93.0 31.3 %collective-permute-start.33 = (bf16[192,768]{1,0:T(8,128)(2,1)S(1)}, bf16[192,768]{1,0:T(8,128)(2,1)S(1)}, u32[]{:S(2)}, u32[]{:S(2)}) collective-permute-start(bf16[192,768]{1,0:T(8,128)(2,1)S(1)} %get-tuple-element.158), channel_id=1, source_target_pairs={{0,2},{1,3},{2,4},{3,5},{4,6},{5,7},{6,0},{7,1},{8,10},{9,11},{10,... | collective-permute-start | bytes 884744 | tf_op jit(solution)/shard_map/ppermute | solution.py:55
  93.3 32.5 %collective-permute-start.34 = (bf16[192,768]{1,0:T(8,128)(2,1)S(1)}, bf16[192,768]{1,0:T(8,128)(2,1)S(1)}, u32[]{:S(2)}, u32[]{:S(2)}) collective-permute-start(bf16[192,768]{1,0:T(8,128)(2,1)S(1)} %get-tuple-element.159), channel_id=1, source_target_pairs={{0,4},{1,5},{2,6},{3,7},{4,0},{5,1},{6,2},{7,3},{8,12},{9,13},{10,... | collective-permute-start | bytes 884744 | tf_op jit(solution)/shard_map/ppermute | solution.py:55
  95.8 30.0 %collective-permute-start.35 = (bf16[192,768]{1,0:T(8,128)(2,1)S(1)}, bf16[192,768]{1,0:T(8,128)(2,1)S(1)}, u32[]{:S(2)}, u32[]{:S(2)}) collective-permute-start(bf16[192,768]{1,0:T(8,128)(2,1)S(1)} %get-tuple-element.160), channel_id=1, source_target_pairs={{0,6},{1,7},{2,0},{3,1},{4,2},{5,3},{6,4},{7,5},{8,14},{9,15},{10,... | collective-permute-start | bytes 884744 | tf_op jit(solution)/shard_map/ppermute | solution.py:55
  132.8 11.3 %collective-permute-start.41 = (bf16[192,768]{1,0:T(8,128)(2,1)S(1)}, bf16[192,768]{1,0:T(8,128)(2,1)S(1)}, u32[]{:S(2)}, u32[]{:S(2)}) collective-permute-start(bf16[192,768]{1,0:T(8,128)(2,1)S(1)} %convert_add_fusion.refs_0_), channel_id=1, source_target_pairs={{0,16},{8,24},{16,0},{24,8},{1,17},{9,25},{17,1},{25,9},{2,18},{10... | collective-permute-start | bytes 884744 | tf_op jit(solution)/shard_map/ppermute | solution.py:58
  133.9 10.2 %collective-permute-start.42 = (bf16[192,768]{1,0:T(8,128)(2,1)S(1)}, bf16[192,768]{1,0:T(8,128)(2,1)S(1)}, u32[]{:S(2)}, u32[]{:S(2)}) collective-permute-start(bf16[192,768]{1,0:T(8,128)(2,1)S(1)} %convert_add_fusion.refs_0_), channel_id=1, source_target_pairs={{0,24},{8,16},{16,8},{24,0},{1,25},{9,17},{17,9},{25,1},{2,26},{10... | collective-permute-start | bytes 884744 | tf_op jit(solution)/shard_map/ppermute | solution.py:58
  135.5 13.1 %collective-permute-start.37 = (bf16[112,768]{1,0:T(8,128)(2,1)S(1)}, bf16[112,768]{1,0:T(8,128)(2,1)S(1)}, u32[]{:S(2)}, u32[]{:S(2)}) collective-permute-start(bf16[112,768]{1,0:T(8,128)(2,1)S(1)} %get-tuple-element.162), channel_id=1, source_target_pairs={{0,2},{1,3},{2,4},{3,5},{4,6},{5,7},{6,0},{7,1},{8,10},{9,11},{10,... | collective-permute-start | bytes 516104 | tf_op jit(solution)/shard_map/ppermute | solution.py:55
  135.6 13.0 %collective-permute-start.38 = (bf16[112,768]{1,0:T(8,128)(2,1)S(1)}, bf16[112,768]{1,0:T(8,128)(2,1)S(1)}, u32[]{:S(2)}, u32[]{:S(2)}) collective-permute-start(bf16[112,768]{1,0:T(8,128)(2,1)S(1)} %get-tuple-element.163), channel_id=1, source_target_pairs={{0,4},{1,5},{2,6},{3,7},{4,0},{5,1},{6,2},{7,3},{8,12},{9,13},{10,... | collective-permute-start | bytes 516104 | tf_op jit(solution)/shard_map/ppermute | solution.py:55
  (61 other events, 350.9 us)

commit v4 on v3

--- a/solution.py
+++ b/solution.py
@@ -86,8 +86,9 @@
     return [block] + [links.along(block, hop) for hop in range(1, end or links.line)]
 
 
-def with_partners(links, mine):
-    return mine + [links.core(v) for v in mine]
+def with_partners(links, mine, own_theirs=None):
+    theirs = [links.core(v) for v in mine[1:]]
+    return mine + [links.core(mine[0]) if own_theirs is None else own_theirs] + theirs
 
 
 def assemble(scalar_ref, refs, out, start, rows):
@@ -637,7 +638,8 @@
 
     proj_mine, proj_other = proj_lanes(links, attn_blocks, out_grad, rows, part)
     proj = links.rep_gather(proj_mine)
-    attn_blocks = tie(attn_blocks, proj_mine)
+    ff_own_theirs = links.core(ff_block)
+    attn_blocks = tie(attn_blocks, (proj_mine, ff_own_theirs))
     weights, normed_one, qkv, probs, sent, small_f = attn_forward(
         links, got, attn_blocks, slots, heads, count, rows
     )
@@ -645,7 +647,7 @@
     attended = lax.all_gather(sent, "rep", axis=0)
     proj, ff_mine = tie((proj, ff_mine), attended)
     proj = proj + [proj_other] + [links.core(v) for v in proj[1:]]
-    ff_blocks = with_partners(links, ff_mine)
+    ff_blocks = with_partners(links, ff_mine, ff_own_theirs)
     (
         attended,
         middle,

time: 163 us -> 163 us (level)
  transfers between devices with their start and end apart: 43 -> 43, of which waited for: 15 -> 13; matrix products, arithmetic and copies ran while one was open for 3% -> 3% of each run, Pallas kernels for 22% -> 22%
where the time goes in v4:
time: 163 us; the launch traced here: 162 us
  Pallas kernels  49.7 us (30%)
  starting transfers between devices  45.1 us (28%)
  blocking collectives  36.4 us (22%)
  waiting for transfers between devices  20.5 us (13%)
  other arithmetic  4.79 us (3%)
  local copies, waits for them, and re-layouts  4.43 us (3%)
    pallas_call x11, Pallas kernels, run(): pl.pallas_call(kernel, out_shape=[jax.ShapeDtypeStruct(shape, dtype) for...  49.7 us
    ppermute x12, starting transfers between devices, along(): return lax.ppermute(v, 'shard', [(i, (i + 2 * hop) % n) for i in range(n)])  21.3 us
    ppermute x18, starting transfers between devices, rep(): return lax.ppermute(v, 'rep', [(i, i ^ k) for i in range(4)])  21.2 us
    all_gather x1, blocking collectives, local(): attended = lax.all_gather(sent, 'rep', axis=0)  14.1 us
    ppermute x18, waiting for transfers between devices, rep(): return lax.ppermute(v, 'rep', [(i, i ^ k) for i in range(4)])  12.2 us
    all_gather x1, blocking collectives, local(): grad_branch = lax.all_gather(grad_branch, 'rep', axis=0)  11.5 us
    all_gather x1, blocking collectives, local(): lax.all_gather(attn_sum.astype(LOW), 'rep', axis=0)  10.9 us
    ppermute x12, waiting for transfers between devices, along(): return lax.ppermute(v, 'shard', [(i, (i + 2 * hop) % n) for i in range(n)])  4.29 us
  transfers between devices with their start and end apart: 43, of which 13 were waited for; matrix products, arithmetic and copies ran while one was open for 3% of the time, Pallas kernels for 22%

profile of v4, /device:TPU:0, one launch (start us, length us, event | category | flops | bytes accessed | tf_op | source)
XLA Modules:
  0.0 162.1 jit_solution(710920066679243291)
XLA Ops:
  1.2 2.1 %shard_map.169.refs_0_.refs_4_ = bf16[112,768]{1,0:T(8,128)(2,1)} custom-call(s32[4]{0:T(128)} %pad_add_fusion.scalar_ref, bf16[2,96]{1,0:T(2,128)(2,1)} %gain.1, bf16[6,96]{1,0:T(8,128)(2,1)} %shift.1, bf16[384]{0:T(512)(128)(2,1)} %bias_ref.1, bf16[96,2304]{1,0:T(8,128)(2,1)} %qkv_ref.1, bf16[96,768]{1,0:T(8,128)(2,1)} %p_ref.1), custom_call_target="tpu_custom_call" | custom-call | flops 1 | bytes 1 | tf_op jit(solution)/shard_map/pallas_call | solution.py:69
  3.4 3.0 %collective-permute-start = (bf16[112,768]{1,0:T(8,128)(2,1)}, bf16[112,768]{1,0:T(8,128)(2,1)S(1)}, u32[]{:S(2)}, u32[]{:S(2)}) collective-permute-start(bf16[112,768]{1,0:T(8,128)(2,1)} %shard_map.169.refs_0_.refs_4_), channel_id=1, source_target_pairs={{0,2},{1,3},{2,4},{3,5},{4,6},{5,7},{6,0},{7,1},{8,10},{9,11},{10,... | collective-permute-start | bytes 516104 | tf_op jit(solution)/shard_map/ppermute | solution.py:55
  11.5 2.6 %collective-permute-start.1 = (bf16[112,768]{1,0:T(8,128)(2,1)}, bf16[112,768]{1,0:T(8,128)(2,1)S(1)}, u32[]{:S(2)}, u32[]{:S(2)}) collective-permute-start(bf16[112,768]{1,0:T(8,128)(2,1)} %shard_map.169.refs_0_.refs_4_), channel_id=1, source_target_pairs={{0,4},{1,5},{2,6},{3,7},{4,0},{5,1},{6,2},{7,3},{8,12},{9,13},{10,... | collective-permute-start | bytes 516104 | tf_op jit(solution)/shard_map/ppermute | solution.py:55
  15.5 2.8 %shard_map.171.refs_13_ = bf16[192,768]{1,0:T(8,128)(2,1)} custom-call(s32[4]{0:T(128)} %pad_add_fusion.scalar_ref, bf16[96,3072]{1,0:T(8,128)(2,1)} %fc_ref, bf16[384,768]{1,0:T(8,128)(2,1)} %fc2_ref), custom_call_target="tpu_custom_call" | custom-call | flops 1 | bytes 1 | tf_op jit(solution)/shard_map/pallas_call | solution.py:69
  18.2 4.3 %collective-permute-done.1.refs_2_.refs_6_ = bf16[112,768]{1,0:T(8,128)(2,1)S(1)} collective-permute-done((bf16[112,768]{1,0:T(8,128)(2,1)}, bf16[112,768]{1,0:T(8,128)(2,1)S(1)}, u32[]{:S(2)}, u32[]{:S(2)}) %collective-permute-start.1) | collective-permute-done | bytes 172064 | tf_op jit(solution)/shard_map/ppermute | solution.py:55
  23.2 3.1 %collective-permute-start.14 = (bf16[192,768]{1,0:T(8,128)(2,1)}, bf16[192,768]{1,0:T(8,128)(2,1)S(1)}, u32[]{:S(2)}, u32[]{:S(2)}) collective-permute-start(bf16[192,768]{1,0:T(8,128)(2,1)} %shard_map.171.refs_13_), channel_id=1, source_target_pairs={{0,2},{1,3},{2,4},{3,5},{4,6},{5,7},{6,0},{7,1},{8,10},{9,11},{10,... | collective-permute-start | bytes 884744 | tf_op jit(solution)/shard_map/ppermute | solution.py:55
  29.2 2.4 %shard_map.172 = (bf16[224,768]{1,0:T(8,128)(2,1)}, bf16[96,768]{1,0:T(8,128)(2,1)}) custom-call(s32[4]{0:T(128)} %pad_add_fusion.scalar_ref, bf16[112,768]{1,0:T(8,128)(2,1)} %shard_map.169.refs_0_.refs_4_, bf16[112,768]{1,0:T(8,128)(2,1)} %copy-done.10, bf16[112,768]{1,0:T(8,128)(2,1)} %copy-done.11, bf16[112,768]{1,0:T(8,128)(2,1)} %copy-done.12, ...), custom_call_target="tpu_custom_call" | custom-call | flops 1 | bytes 1 | tf_op jit(solution)/shard_map/pallas_call | solution.py:69
  35.1 2.4 %collective-permute-start.15 = (bf16[192,768]{1,0:T(8,128)(2,1)S(1)}, bf16[192,768]{1,0:T(8,128)(2,1)S(1)}, u32[]{:S(2)}, u32[]{:S(2)}) collective-permute-start(bf16[192,768]{1,0:T(8,128)(2,1)S(1)} %copy-done.8), channel_id=1, source_target_pairs={{0,4},{1,5},{2,6},{3,7},{4,0},{5,1},{6,2},{7,3},{8,12},{9,13},{10,... | collective-permute-start | bytes 884744 | tf_op jit(solution)/shard_map/ppermute | solution.py:55
  37.6 7.1 %shard_map.173 = (bf16[768,768]{1,0:T(8,128)(2,1)}, bf16[512,768]{1,0:T(8,128)(2,1)}, bf16[512,576]{1,0:T(8,128)(2,1)}, f32[4,3,128,128]{3,2,1,0:T(8,128)}, bf16[128,768]{1,0:T(8,128)(2,1)}, /*index=5*/f32[16,768]{1,0:T(8,128)}) custom-call(s32[4]{0:T(128)} %pad_add_fusion.scalar_ref, bf16[144,768]{1,0:T(8,128)(2,1)} %shard_map.170.refs_0_.got_ref.refs_1_, ...), custom_call_target="tpu_custom_call" | custom-call | flops 1 | bytes 1 | tf_op jit(solution)/shard_map/pallas_call | solution.py:69
  44.9 14.1 %all-gather = bf16[512,768]{1,0:T(8,128)(2,1)} all-gather(bf16[128,768]{1,0:T(8,128)(2,1)} %get-tuple-element.112), channel_id=2, replica_groups=mesh['rep'=4,'shard'=8] {'rep'}, dimensions={0}, use_global_device_ids=true | all-gather | bytes 983040 | tf_op jit(solution)/shard_map/all_gather | solution.py:647
  64.1 8.9 %shard_map.174 = (bf16[512,768]{1,0:T(8,128)(2,1)}, f32[128,768]{1,0:T(8,128)}, bf16[512,768]{1,0:T(8,128)(2,1)}, bf16[512,768]{1,0:T(8,128)(2,1)}, bf16[512,768...) custom-call(s32[4]{0:T(128)} %pad_add_fusion.scalar_ref, ...), custom_call_target="tpu_custom_call" | custom-call | flops 1 | bytes 1 | tf_op jit(solution)/shard_map/pallas_call | solution.py:69
  76.6 5.8 %shard_map.175 = (bf16[768,768]{1,0:T(8,128)(2,1)}, bf16[768,768]{1,0:T(8,128)(2,1)}, f32[128,768]{1,0:T(8,128)}, bf16[128,768]{1,0:T(8,128)(2,1)}, bf16[128,768]{1,0:T(8,128)(2,1)}, /*index=5*/bf16[128,768]{1,0:T(8,128)(2,1)}) custom-call(s32[4]{0:T(128)} %pad_add_fusion.scalar_ref, bf16[512,768]{1,0:T(8,128)(2,1)} %get-tuple-element.125.refs_0_, ...), custom_call_target="tpu_custom_call" | custom-call | flops 1 | bytes 1 | tf_op jit(solution)/shard_map/pallas_call | solution.py:69
  82.4 2.7 %collective-permute-done.27.r2 = bf16[128,768]{1,0:T(8,128)(2,1)S(1)} collective-permute-done((bf16[128,768]{1,0:T(8,128)(2,1)}, bf16[128,768]{1,0:T(8,128)(2,1)S(1)}, u32[]{:S(2)}, u32[]{:S(2)}) %collective-permute-start.27) | collective-permute-done | bytes 196640 | tf_op jit(solution)/shard_map/ppermute | solution.py:58
  89.8 2.8 %shard_map.176 = (f32[128,768]{1,0:T(8,128)}, bf16[128,768]{1,0:T(8,128)(2,1)}, f32[4,768]{1,0:T(4,128)}) custom-call(s32[4]{0:T(128)} %pad_add_fusion.scalar_ref, f32[128,768]{1,0:T(8,128)} %get-tuple-element.134.own_ref, bf16[128,768]{1,0:T(8,128)(2,1)} %copy-done.36, bf16[128,768]{1,0:T(8,128)(2,1)} %copy-done.37, bf16[128,768]{1,0:T(8,128)(2,1)} %copy-done.38, ...), custom_call_target="tpu_custom_call" | custom-call | flops 1 | bytes 1 | tf_op jit(solution)/shard_map/pallas_call | solution.py:69
  93.2 2.5 %collective-permute-start.34 = (bf16[192,768]{1,0:T(8,128)(2,1)S(1)}, bf16[192,768]{1,0:T(8,128)(2,1)S(1)}, u32[]{:S(2)}, u32[]{:S(2)}) collective-permute-start(bf16[192,768]{1,0:T(8,128)(2,1)S(1)} %get-tuple-element.159), channel_id=1, source_target_pairs={{0,4},{1,5},{2,6},{3,7},{4,0},{5,1},{6,2},{7,3},{8,12},{9,13},{10,... | collective-permute-start | bytes 884744 | tf_op jit(solution)/shard_map/ppermute | solution.py:55
  95.7 2.8 %collective-permute-start.35 = (bf16[192,768]{1,0:T(8,128)(2,1)S(1)}, bf16[192,768]{1,0:T(8,128)(2,1)S(1)}, u32[]{:S(2)}, u32[]{:S(2)}) collective-permute-start(bf16[192,768]{1,0:T(8,128)(2,1)S(1)} %get-tuple-element.160), channel_id=1, source_target_pairs={{0,6},{1,7},{2,0},{3,1},{4,2},{5,3},{6,4},{7,5},{8,14},{9,15},{10,... | collective-permute-start | bytes 884744 | tf_op jit(solution)/shard_map/ppermute | solution.py:55
  100.1 11.5 %all-gather.1 = bf16[512,768]{1,0:T(8,128)(2,1)} all-gather(bf16[128,768]{1,0:T(8,128)(2,1)S(1)} %copy-done.39), channel_id=3, replica_groups=mesh['rep'=4,'shard'=8] {'rep'}, dimensions={0}, use_global_device_ids=true | all-gather | bytes 983040 | tf_op jit(solution)/shard_map/all_gather | solution.py:680
  111.6 10.4 %shard_map.177 = (bf16[448,768]{1,0:T(8,128)(2,1)}, bf16[448,768]{1,0:T(8,128)(2,1)}, f32[128,768]{1,0:T(8,128)}, bf16[128,768]{1,0:T(8,128)(2,1)}, bf16[128,768]{1,0:T(8,128)(2,1)}, /*index=5*/bf16[128,768]{1,0:T(8,128)(2,1)}) custom-call(s32[4]{0:T(128)} %pad_add_fusion.scalar_ref, bf16[4,128,768]{2,1,0:T(8,128)(2,1)} %bitcast.7, ...), custom_call_target="tpu_custom_call" | custom-call | flops 1 | bytes 1 | tf_op jit(solution)/shard_map/pallas_call | solution.py:69
  128.4 2.6 %collective-permute-done.30 = bf16[128,768]{1,0:T(8,128)(2,1)S(1)} collective-permute-done((bf16[128,768]{1,0:T(8,128)(2,1)}, bf16[128,768]{1,0:T(8,128)(2,1)S(1)}, u32[]{:S(2)}, u32[]{:S(2)}) %collective-permute-start.30) | collective-permute-done | bytes 196640 | tf_op jit(solution)/shard_map/ppermute | solution.py:58
  137.4 2.7 %collective-permute-done.40.refs_1_ = bf16[192,768]{1,0:T(8,128)(2,1)S(1)} collective-permute-done((bf16[192,768]{1,0:T(8,128)(2,1)S(1)}, bf16[192,768]{1,0:T(8,128)(2,1)S(1)}, u32[]{:S(2)}, u32[]{:S(2)}) %collective-permute-start.40) | collective-permute-done | bytes 294944 | tf_op jit(solution)/shard_map/ppermute | solution.py:58
  141.9 2.0 %collective-permute-done.41.refs_2_ = bf16[192,768]{1,0:T(8,128)(2,1)S(1)} collective-permute-done((bf16[192,768]{1,0:T(8,128)(2,1)S(1)}, bf16[192,768]{1,0:T(8,128)(2,1)S(1)}, u32[]{:S(2)}, u32[]{:S(2)}) %collective-permute-start.41) | collective-permute-done | bytes 294944 | tf_op jit(solution)/shard_map/ppermute | solution.py:58
  145.4 3.0 %shard_map.179 = (f32[96,3072]{1,0:T(8,128)}, f32[384,768]{1,0:T(8,128)}) custom-call(s32[4]{0:T(128)} %pad_add_fusion.scalar_ref, bf16[192,768]{1,0:T(8,128)(2,1)} %copy-done.6, bf16[192,768]{1,0:T(8,128)(2,1)} %copy-done.26, bf16[192,768]{1,0:T(8,128)(2,1)} %copy-done.27, bf16[192,768]{1,0:T(8,128)(2,1)} %copy-done.28), custom_call_target="tpu_custom_call" | custom-call | flops 1 | bytes 1 | tf_op jit(solution)/shard_map/pallas_call | solution.py:69
  148.6 10.9 %all-gather.2 = bf16[448,768]{1,0:T(8,128)(2,1)} all-gather(bf16[112,768]{1,0:T(8,128)(2,1)S(1)} %add_convert_fusion.3), channel_id=4, replica_groups=mesh['rep'=4,'shard'=8] {'rep'}, dimensions={0}, use_global_device_ids=true | all-gather | bytes 860160 | tf_op jit(solution)/shard_map/all_gather | solution.py:717
  159.4 2.6 %shard_map.178 = (f32[96,2304]{1,0:T(8,128)}, f32[96,768]{1,0:T(8,128)}, f32[2,96]{1,0:T(2,128)}, f32[6,96]{1,0:T(8,128)}, f32[384]{0:T(512)}) custom-call(s32[4]{0:T(128)} %pad_add_fusion.scalar_ref, bf16[4,112,768]{2,1,0:T(8,128)(2,1)} %bitcast.9), custom_call_target="tpu_custom_call" | custom-call | flops 1 | bytes 1 | tf_op jit(solution)/shard_map/pallas_call | solution.py:69
  (176 shorter events, 45.6 us)
Async XLA Ops:
  3.4 10.8 %collective-permute-start = (bf16[112,768]{1,0:T(8,128)(2,1)}, bf16[112,768]{1,0:T(8,128)(2,1)S(1)}, u32[]{:S(2)}, u32[]{:S(2)}) collective-permute-start(bf16[112,768]{1,0:T(8,128)(2,1)} %shard_map.169.refs_0_.refs_4_), channel_id=1, source_target_pairs={{0,2},{1,3},{2,4},{3,5},{4,6},{5,7},{6,0},{7,1},{8,10},{9,11},{10,... | collective-permute-start | bytes 516104 | tf_op jit(solution)/shard_map/ppermute | solution.py:55
  8.1 14.5 %collective-permute-start.3 = (bf16[144,768]{1,0:T(8,128)(2,1)}, bf16[144,768]{1,0:T(8,128)(2,1)S(1)}, u32[]{:S(2)}, u32[]{:S(2)}) collective-permute-start(bf16[144,768]{1,0:T(8,128)(2,1)} %shard_map.170.refs_0_.got_ref.refs_1_), channel_id=1, source_target_pairs={{0,8},{8,0},{16,24},{24,16},{1,9},{9,1},{17,25},{25,17},{2,10},{10... | collective-permute-start | bytes 663560 | tf_op jit(solution)/shard_map/ppermute | solution.py:58
  9.5 13.0 %collective-permute-start.4 = (bf16[144,768]{1,0:T(8,128)(2,1)}, bf16[144,768]{1,0:T(8,128)(2,1)S(1)}, u32[]{:S(2)}, u32[]{:S(2)}) collective-permute-start(bf16[144,768]{1,0:T(8,128)(2,1)} %shard_map.170.refs_0_.got_ref.refs_1_), channel_id=1, source_target_pairs={{0,16},{8,24},{16,0},{24,8},{1,17},{9,25},{17,1},{25,9},{2,18},{10... | collective-permute-start | bytes 663560 | tf_op jit(solution)/shard_map/ppermute | solution.py:58
  11.1 11.5 %collective-permute-start.5 = (bf16[144,768]{1,0:T(8,128)(2,1)}, bf16[144,768]{1,0:T(8,128)(2,1)S(1)}, u32[]{:S(2)}, u32[]{:S(2)}) collective-permute-start(bf16[144,768]{1,0:T(8,128)(2,1)} %shard_map.170.refs_0_.got_ref.refs_1_), channel_id=1, source_target_pairs={{0,24},{8,16},{16,8},{24,0},{1,25},{9,17},{17,9},{25,1},{2,26},{10... | collective-permute-start | bytes 663560 | tf_op jit(solution)/shard_map/ppermute | solution.py:58
  11.5 11.0 %collective-permute-start.1 = (bf16[112,768]{1,0:T(8,128)(2,1)}, bf16[112,768]{1,0:T(8,128)(2,1)S(1)}, u32[]{:S(2)}, u32[]{:S(2)}) collective-permute-start(bf16[112,768]{1,0:T(8,128)(2,1)} %shard_map.169.refs_0_.refs_4_), channel_id=1, source_target_pairs={{0,4},{1,5},{2,6},{3,7},{4,0},{5,1},{6,2},{7,3},{8,12},{9,13},{10,... | collective-permute-start | bytes 516104 | tf_op jit(solution)/shard_map/ppermute | solution.py:55
  22.7 12.5 %collective-permute-start.10 = (bf16[192,768]{1,0:T(8,128)(2,1)}, bf16[192,768]{1,0:T(8,128)(2,1)S(1)}, u32[]{:S(2)}, u32[]{:S(2)}) collective-permute-start(bf16[192,768]{1,0:T(8,128)(2,1)} %shard_map.171.refs_13_), channel_id=1, source_target_pairs={{0,1},{1,0},{2,3},{3,2},{4,5},{5,4},{6,7},{7,6},{8,9},{9,8},{10,11... | collective-permute-start | bytes 884744 | tf_op jit(solution)/shard_map/ppermute | solution.py:51
  23.2 21.5 %collective-permute-start.14 = (bf16[192,768]{1,0:T(8,128)(2,1)}, bf16[192,768]{1,0:T(8,128)(2,1)S(1)}, u32[]{:S(2)}, u32[]{:S(2)}) collective-permute-start(bf16[192,768]{1,0:T(8,128)(2,1)} %shard_map.171.refs_13_), channel_id=1, source_target_pairs={{0,2},{1,3},{2,4},{3,5},{4,6},{5,7},{6,0},{7,1},{8,10},{9,11},{10,... | collective-permute-start | bytes 884744 | tf_op jit(solution)/shard_map/ppermute | solution.py:55
  31.6 27.3 %collective-permute-start.11 = (bf16[224,768]{1,0:T(8,128)(2,1)}, bf16[224,768]{1,0:T(8,128)(2,1)S(1)}, u32[]{:S(2)}, u32[]{:S(2)}) collective-permute-start(bf16[224,768]{1,0:T(8,128)(2,1)} %get-tuple-element.114.refs_5_), channel_id=1, source_target_pairs={{0,8},{8,0},{16,24},{24,16},{1,9},{9,1},{17,25},{25,17},{2,10},{10... | collective-permute-start | bytes 1032200 | tf_op jit(solution)/shard_map/ppermute | solution.py:58
  33.1 25.8 %collective-permute-start.12 = (bf16[224,768]{1,0:T(8,128)(2,1)}, bf16[224,768]{1,0:T(8,128)(2,1)S(1)}, u32[]{:S(2)}, u32[]{:S(2)}) collective-permute-start(bf16[224,768]{1,0:T(8,128)(2,1)} %get-tuple-element.114.refs_5_), channel_id=1, source_target_pairs={{0,16},{8,24},{16,0},{24,8},{1,17},{9,25},{17,1},{25,9},{2,18},{10... | collective-permute-start | bytes 1032200 | tf_op jit(solution)/shard_map/ppermute | solution.py:58
  34.6 24.3 %collective-permute-start.13 = (bf16[224,768]{1,0:T(8,128)(2,1)}, bf16[224,768]{1,0:T(8,128)(2,1)S(1)}, u32[]{:S(2)}, u32[]{:S(2)}) collective-permute-start(bf16[224,768]{1,0:T(8,128)(2,1)} %get-tuple-element.114.refs_5_), channel_id=1, source_target_pairs={{0,24},{8,16},{16,8},{24,0},{1,25},{9,17},{17,9},{25,1},{2,26},{10... | collective-permute-start | bytes 1032200 | tf_op jit(solution)/shard_map/ppermute | solution.py:58
  35.1 23.8 %collective-permute-start.15 = (bf16[192,768]{1,0:T(8,128)(2,1)S(1)}, bf16[192,768]{1,0:T(8,128)(2,1)S(1)}, u32[]{:S(2)}, u32[]{:S(2)}) collective-permute-start(bf16[192,768]{1,0:T(8,128)(2,1)S(1)} %copy-done.8), channel_id=1, source_target_pairs={{0,4},{1,5},{2,6},{3,7},{4,0},{5,1},{6,2},{7,3},{8,12},{9,13},{10,... | collective-permute-start | bytes 884744 | tf_op jit(solution)/shard_map/ppermute | solution.py:55
  44.7 14.3 %collective-permute-start.16 = (bf16[192,768]{1,0:T(8,128)(2,1)S(1)}, bf16[192,768]{1,0:T(8,128)(2,1)S(1)}, u32[]{:S(2)}, u32[]{:S(2)}) collective-permute-start(bf16[192,768]{1,0:T(8,128)(2,1)S(1)} %copy-done.8), channel_id=1, source_target_pairs={{0,6},{1,7},{2,0},{3,1},{4,2},{5,3},{6,4},{7,5},{8,14},{9,15},{10,... | collective-permute-start | bytes 884744 | tf_op jit(solution)/shard_map/ppermute | solution.py:55
  74.1 11.1 %collective-permute-start.27 = (bf16[128,768]{1,0:T(8,128)(2,1)}, bf16[128,768]{1,0:T(8,128)(2,1)S(1)}, u32[]{:S(2)}, u32[]{:S(2)}) collective-permute-start(bf16[128,768]{1,0:T(8,128)(2,1)} %get-tuple-element.136), channel_id=1, source_target_pairs={{0,16},{8,24},{16,0},{24,8},{1,17},{9,25},{17,1},{25,9},{2,18},{10... | collective-permute-start | bytes 589832 | tf_op jit(solution)/shard_map/ppermute | solution.py:58
  75.1 10.0 %collective-permute-start.28 = (bf16[128,768]{1,0:T(8,128)(2,1)}, bf16[128,768]{1,0:T(8,128)(2,1)S(1)}, u32[]{:S(2)}, u32[]{:S(2)}) collective-permute-start(bf16[128,768]{1,0:T(8,128)(2,1)} %get-tuple-element.137), channel_id=1, source_target_pairs={{0,24},{8,16},{16,8},{24,0},{1,25},{9,17},{17,9},{25,1},{2,26},{10... | collective-permute-start | bytes 589832 | tf_op jit(solution)/shard_map/ppermute | solution.py:58
  86.2 9.5 %collective-permute-start.23 = (bf16[128,768]{1,0:T(8,128)(2,1)}, bf16[128,768]{1,0:T(8,128)(2,1)S(1)}, u32[]{:S(2)}, u32[]{:S(2)}) collective-permute-start(bf16[128,768]{1,0:T(8,128)(2,1)} %get-tuple-element.131), channel_id=1, source_target_pairs={{0,8},{8,0},{16,24},{24,16},{1,9},{9,1},{17,25},{25,17},{2,10},{10... | collective-permute-start | bytes 589832 | tf_op jit(solution)/shard_map/ppermute | solution.py:58
  87.3 12.7 %collective-permute-start.24 = (bf16[128,768]{1,0:T(8,128)(2,1)}, bf16[128,768]{1,0:T(8,128)(2,1)S(1)}, u32[]{:S(2)}, u32[]{:S(2)}) collective-permute-start(bf16[128,768]{1,0:T(8,128)(2,1)} %get-tuple-element.132), channel_id=1, source_target_pairs={{0,16},{8,24},{16,0},{24,8},{1,17},{9,25},{17,1},{25,9},{2,18},{10... | collective-permute-start | bytes 589832 | tf_op jit(solution)/shard_map/ppermute | solution.py:58
  88.3 11.8 %collective-permute-start.25 = (bf16[128,768]{1,0:T(8,128)(2,1)}, bf16[128,768]{1,0:T(8,128)(2,1)S(1)}, u32[]{:S(2)}, u32[]{:S(2)}) collective-permute-start(bf16[128,768]{1,0:T(8,128)(2,1)} %get-tuple-element.133), channel_id=1, source_target_pairs={{0,24},{8,16},{16,8},{24,0},{1,25},{9,17},{17,9},{25,1},{2,26},{10... | collective-permute-start | bytes 589832 | tf_op jit(solution)/shard_map/ppermute | solution.py:58
  92.8 31.3 %collective-permute-start.33 = (bf16[192,768]{1,0:T(8,128)(2,1)S(1)}, bf16[192,768]{1,0:T(8,128)(2,1)S(1)}, u32[]{:S(2)}, u32[]{:S(2)}) collective-permute-start(bf16[192,768]{1,0:T(8,128)(2,1)S(1)} %get-tuple-element.158), channel_id=1, source_target_pairs={{0,2},{1,3},{2,4},{3,5},{4,6},{5,7},{6,0},{7,1},{8,10},{9,11},{10,... | collective-permute-start | bytes 884744 | tf_op jit(solution)/shard_map/ppermute | solution.py:55
  93.2 32.4 %collective-permute-start.34 = (bf16[192,768]{1,0:T(8,128)(2,1)S(1)}, bf16[192,768]{1,0:T(8,128)(2,1)S(1)}, u32[]{:S(2)}, u32[]{:S(2)}) collective-permute-start(bf16[192,768]{1,0:T(8,128)(2,1)S(1)} %get-tuple-element.159), channel_id=1, source_target_pairs={{0,4},{1,5},{2,6},{3,7},{4,0},{5,1},{6,2},{7,3},{8,12},{9,13},{10,... | collective-permute-start | bytes 884744 | tf_op jit(solution)/shard_map/ppermute | solution.py:55
  95.7 29.9 %collective-permute-start.35 = (bf16[192,768]{1,0:T(8,128)(2,1)S(1)}, bf16[192,768]{1,0:T(8,128)(2,1)S(1)}, u32[]{:S(2)}, u32[]{:S(2)}) collective-permute-start(bf16[192,768]{1,0:T(8,128)(2,1)S(1)} %get-tuple-element.160), channel_id=1, source_target_pairs={{0,6},{1,7},{2,0},{3,1},{4,2},{5,3},{6,4},{7,5},{8,14},{9,15},{10,... | collective-permute-start | bytes 884744 | tf_op jit(solution)/shard_map/ppermute | solution.py:55
  132.7 11.2 %collective-permute-start.41 = (bf16[192,768]{1,0:T(8,128)(2,1)S(1)}, bf16[192,768]{1,0:T(8,128)(2,1)S(1)}, u32[]{:S(2)}, u32[]{:S(2)}) collective-permute-start(bf16[192,768]{1,0:T(8,128)(2,1)S(1)} %convert_add_fusion.refs_0_), channel_id=1, source_target_pairs={{0,16},{8,24},{16,0},{24,8},{1,17},{9,25},{17,1},{25,9},{2,18},{10... | collective-permute-start | bytes 884744 | tf_op jit(solution)/shard_map/ppermute | solution.py:58
  133.7 10.2 %collective-permute-start.42 = (bf16[192,768]{1,0:T(8,128)(2,1)S(1)}, bf16[192,768]{1,0:T(8,128)(2,1)S(1)}, u32[]{:S(2)}, u32[]{:S(2)}) collective-permute-start(bf16[192,768]{1,0:T(8,128)(2,1)S(1)} %convert_add_fusion.refs_0_), channel_id=1, source_target_pairs={{0,24},{8,16},{16,8},{24,0},{1,25},{9,17},{17,9},{25,1},{2,26},{10... | collective-permute-start | bytes 884744 | tf_op jit(solution)/shard_map/ppermute | solution.py:58
  135.3 13.1 %collective-permute-start.37 = (bf16[112,768]{1,0:T(8,128)(2,1)S(1)}, bf16[112,768]{1,0:T(8,128)(2,1)S(1)}, u32[]{:S(2)}, u32[]{:S(2)}) collective-permute-start(bf16[112,768]{1,0:T(8,128)(2,1)S(1)} %get-tuple-element.162), channel_id=1, source_target_pairs={{0,2},{1,3},{2,4},{3,5},{4,6},{5,7},{6,0},{7,1},{8,10},{9,11},{10,... | collective-permute-start | bytes 516104 | tf_op jit(solution)/shard_map/ppermute | solution.py:55
  135.4 13.0 %collective-permute-start.38 = (bf16[112,768]{1,0:T(8,128)(2,1)S(1)}, bf16[112,768]{1,0:T(8,128)(2,1)S(1)}, u32[]{:S(2)}, u32[]{:S(2)}) collective-permute-start(bf16[112,768]{1,0:T(8,128)(2,1)S(1)} %get-tuple-element.163), channel_id=1, source_target_pairs={{0,4},{1,5},{2,6},{3,7},{4,0},{5,1},{6,2},{7,3},{8,12},{9,13},{10,... | collective-permute-start | bytes 516104 | tf_op jit(solution)/shard_map/ppermute | solution.py:55
  (61 other events, 378.6 us)
